TPU v7x, 32 devices: a whole 2x2x4 slice. The times are simulated.
32 devices in a mesh: dp: 16 (over z, y, x), tensor: 2 (over core).
Axes of the slice: x: 2, y: 2, z: 4, core: 2. Of those that a mesh axis runs over, the one named last changes fastest.
Arguments:
- embedded: float32 [32768, 512], P(('dp', 'tensor')), may hold values from -6 to 6
- piece_lengths: int32 [32, 8], P('dp'), may hold values from 1 to 512, 1024 in all within a row
- pair_tags: int32 [32], P('dp'), may hold values from 0 to 3
- pair_embedding: bfloat16 [4, 512], P(None, 'dp'), may hold values from -3 to 3
- w_query: bfloat16 [512, 512], P('dp', 'tensor'), may hold values from -0.25 to 0.25
- w_key: bfloat16 [512, 512], P('dp', 'tensor'), may hold values from -0.25 to 0.25
- w_value: bfloat16 [512, 512], P('dp', 'tensor'), may hold values from -0.25 to 0.25
- w_output: bfloat16 [512, 512], P('tensor', 'dp'), may hold values from -1 to 1
- w_hidden: bfloat16 [512, 2048], P('dp', 'tensor'), may hold values from -0.25 to 0.25
- w_down: bfloat16 [2048, 512], P('tensor', 'dp'), may hold values from -0.125 to 0.125
- first_gain: bfloat16 [512], P('dp'), may hold values from 0.5 to 1.5
- first_shift: bfloat16 [512], P('dp'), may hold values from -2 to 2
- second_gain: bfloat16 [512], P('dp'), may hold values from 0.5 to 1.5
- second_shift: bfloat16 [512], P('dp'), may hold values from -2 to 2
- cotangent: float32 [32768, 512], P(('dp', 'tensor')), may hold values from -6 to 6
Outputs:
- activations: float32 [32768, 512], P(('dp', 'tensor'))
- input_grad: float32 [32768, 512], P(('dp', 'tensor'))
- embedding_grad: float32 [4, 512], P(None, 'dp')
- query_grad: float32 [512, 512], P('dp', 'tensor')
- key_grad: float32 [512, 512], P('dp', 'tensor')
- value_grad: float32 [512, 512], P('dp', 'tensor')
- output_grad: float32 [512, 512], P('tensor', 'dp')
- hidden_grad: float32 [512, 2048], P('dp', 'tensor')
- down_grad: float32 [2048, 512], P('tensor', 'dp')
- first_gain_grad: float32 [512], P('dp')
- first_shift_grad: float32 [512], P('dp')
- second_gain_grad: float32 [512], P('dp')
- second_shift_grad: float32 [512], P('dp')
Inputs may be any that keep to these rules, and one draw needn't show every extreme that they name: `piece_lengths`: the 8 piece lengths of each packed sequence sum to 1024; the last piece is padding.
All inputs are finite; a program needn't handle non-finite values.
Results may differ from a plain program's by a relative error of at most 0.02.
Values may be sent and summed in bfloat16 or wider, within the bound.
No kernel may reach another device: no remote copies, remote signals or barrier semaphores. Data moves between devices by JAX's collectives and lax.ppermute only.
A program may use at most 256 MiB of HBM per device.

v0:
```python
import jax
import jax.numpy as jnp
from jax import lax
from jax.sharding import PartitionSpec as P

HEAD_DIM = 64
LEN = 1024
PIECES = 8
PAIRS = 4


HIGH = lax.Precision.HIGHEST
NEGATIVE = -1e30


def in_blocks(value, dim, size):
    shape = value.shape
    blocks = value.reshape(*shape[:dim], size, shape[dim] // size, *shape[dim + 1 :])
    return jnp.moveaxis(blocks, dim, 0)


def summed_on_arrival(value, axis, dim):
    blocks = in_blocks(value, dim, lax.axis_size(axis))
    arrived = lax.all_to_all(blocks, axis, split_axis=0, concat_axis=0, tiled=True)
    return arrived.astype(jnp.float32).sum(axis=0)


def side_by_side(arrays, axis, dim, along):
    ends, at = ([], 0)
    for a in arrays[:-1]:
        at += a.shape[along]
        ends.append(at)
    both = jnp.concatenate(arrays, axis=along)
    return tuple(jnp.split(summed_on_arrival(both, axis, dim), ends, axis=along))


def norm_rows(values, gain, shift):
    center = values - jnp.mean(values, axis=-1, keepdims=True)
    spread_sq = jnp.mean(center * center, axis=-1, keepdims=True)
    return center * lax.rsqrt(spread_sq + 1e-05) * gain + shift


def gelu_smooth(values):
    return jax.nn.gelu(values, approximate=True)


def row_dot(left, right):
    return lax.dot_general(
        left, right, (((0,), (0,)), ((), ())), preferred_element_type=jnp.float32
    )


def back_dot(left, right):
    return lax.dot_general(
        left, right, (((1,), (1,)), ((), ())), preferred_element_type=jnp.float32
    )


def segments(pieces):
    ends = jnp.cumsum(pieces, axis=-1)
    places = jnp.arange(LEN, dtype=jnp.int32)
    return jnp.sum((places[None, :, None] >= ends[:, None, :]).astype(jnp.int32), axis=2)


def allowed_mask(row_segs, key_segs, row_places, key_places):
    valid = key_segs < PIECES - 1
    return (row_segs[:, None] == key_segs[None, :]) & (
        valid[None, :] | (row_places[:, None] == key_places[None, :])
    )


def spread(rows):
    return lax.all_gather(rows, "tensor", axis=0, tiled=True)


def collect(part):
    return lax.psum_scatter(
        part.astype(jnp.bfloat16), "tensor", scatter_dimension=0, tiled=True
    ).astype(jnp.float32)


def spread_back(rows):
    return lax.all_gather(rows, "tensor", axis=0, tiled=True)


def collect_back(part):
    return lax.psum_scatter(
        part.astype(jnp.bfloat16), "tensor", scatter_dimension=0, tiled=True
    ).astype(jnp.float32)


def block_scores(query_block, key_seq, seg_seq, offset, block_rows, scaling):
    row_segs = lax.dynamic_slice_in_dim(seg_seq, offset, block_rows, 0)
    key_places = jnp.arange(LEN, dtype=jnp.int32)
    allowed = allowed_mask(
        row_segs, seg_seq, offset + jnp.arange(block_rows, dtype=jnp.int32), key_places
    )
    scores = (
        jnp.einsum("qhd,khd->hqk", query_block, key_seq, preferred_element_type=jnp.float32)
        * scaling
    )
    return jnp.where(allowed[None], scores, NEGATIVE)


def attend(queries, keys, values, segment_ids):
    block_rows = min(512, LEN)
    block_count = LEN // block_rows
    scaling = float(HEAD_DIM) ** (-0.5)

    def one_sequence(inputs):
        query_seq, key_seq, value_seq, seg_seq = inputs

        def one_block(index_value):
            offset = index_value * block_rows
            query_block = lax.dynamic_slice_in_dim(query_seq, offset, block_rows, 0)
            scores = block_scores(query_block, key_seq, seg_seq, offset, block_rows, scaling)
            highest = jnp.max(scores, axis=-1, keepdims=True)
            expd = jnp.exp(scores - highest)
            totals = jnp.sum(expd, axis=-1, keepdims=True)
            probs = expd / totals
            mixed = jnp.einsum(
                "hqk,khd->qhd",
                probs.astype(jnp.bfloat16),
                value_seq,
                preferred_element_type=jnp.float32,
            )
            return (mixed.astype(jnp.bfloat16), (highest + jnp.log(totals))[..., 0])

        outputs, log_totals = lax.map(one_block, jnp.arange(block_count, dtype=jnp.int32))
        return (outputs.reshape(query_seq.shape), log_totals)

    return lax.map(one_sequence, (queries, keys, values, segment_ids))


def attend_back(queries, keys, values, grad_mixed, log_totals, segment_ids):
    block_rows = min(512, LEN)
    block_count = LEN // block_rows
    scaling = float(HEAD_DIM) ** (-0.5)

    def one_sequence(inputs):
        query_seq, key_seq, value_seq, grad_seq, log_seq, seg_seq = inputs

        def one_block(carry, index_value):
            offset = index_value * block_rows
            query_block = lax.dynamic_slice_in_dim(query_seq, offset, block_rows, 0)
            grad_block = lax.dynamic_slice_in_dim(grad_seq, offset, block_rows, 0)
            scores = block_scores(query_block, key_seq, seg_seq, offset, block_rows, scaling)
            probs = jnp.exp(scores - log_seq[index_value][..., None])
            grad_probs = jnp.einsum(
                "qhd,khd->hqk", grad_block, value_seq, preferred_element_type=jnp.float32
            )
            inner = jnp.sum(probs * grad_probs, axis=-1, keepdims=True)
            grad_scores = (probs * (grad_probs - inner)).astype(jnp.bfloat16)
            grad_query = (
                jnp.einsum("hqk,khd->qhd", grad_scores, key_seq, preferred_element_type=jnp.float32)
                * scaling
            )
            grad_key = (
                carry[0]
                + jnp.einsum(
                    "hqk,qhd->khd", grad_scores, query_block, preferred_element_type=jnp.float32
                )
                * scaling
            )
            grad_value = carry[1] + jnp.einsum(
                "hqk,qhd->khd",
                probs.astype(jnp.bfloat16),
                grad_block,
                preferred_element_type=jnp.float32,
            )
            return ((grad_key, grad_value), grad_query.astype(jnp.bfloat16))

        zeros = jnp.zeros(key_seq.shape, jnp.float32)
        (grad_key, grad_value), grad_query = lax.scan(
            one_block, (zeros, zeros), jnp.arange(block_count, dtype=jnp.int32)
        )
        return (
            grad_query.reshape(query_seq.shape),
            grad_key.astype(jnp.bfloat16),
            grad_value.astype(jnp.bfloat16),
        )

    return lax.map(one_sequence, (queries, keys, values, grad_mixed, log_totals, segment_ids))


def forward_visit(rows, weights, segment_ids):
    (
        w_query,
        w_key,
        w_value,
        w_output,
        w_hidden,
        w_down,
        first_gain,
        first_shift,
        second_gain,
        second_shift,
    ) = weights
    packed = jnp.concatenate((w_query, w_key, w_value), axis=1)
    width = w_query.shape[1]
    shape_heads = (segment_ids.shape[0], LEN, width // HEAD_DIM, HEAD_DIM)
    low_rows = rows.astype(jnp.bfloat16)
    gathered = spread(low_rows)
    projected = jnp.dot(gathered, packed, preferred_element_type=jnp.float32).astype(jnp.bfloat16)
    queries = projected[:, :width].reshape(shape_heads)
    keys = projected[:, width : 2 * width].reshape(shape_heads)
    values = projected[:, 2 * width :].reshape(shape_heads)
    mixed, log_totals = attend(queries, keys, values, segment_ids)
    mixed = mixed.reshape(-1, width)
    summed = rows + collect(jnp.dot(mixed, w_output, preferred_element_type=jnp.float32))
    normed = norm_rows(summed, first_gain.astype(jnp.float32), first_shift.astype(jnp.float32))
    low_normed = normed.astype(jnp.bfloat16)
    gathered_normed = spread(low_normed)
    hidden = jnp.dot(gathered_normed, w_hidden, preferred_element_type=jnp.float32)
    active = gelu_smooth(hidden).astype(jnp.bfloat16)
    total = normed + collect(jnp.dot(active, w_down, preferred_element_type=jnp.float32))
    result = norm_rows(total, second_gain.astype(jnp.float32), second_shift.astype(jnp.float32))
    saved_inputs = (gathered, gathered_normed)
    return (
        result,
        (saved_inputs, queries, keys, values, log_totals, mixed, summed, hidden, active, total),
    )


def backward_visit(grad_result, saved, weights, segment_ids):
    saved_inputs, queries, keys, values, log_totals, mixed, summed, hidden, active, total = saved
    (
        w_query,
        w_key,
        w_value,
        w_output,
        w_hidden,
        w_down,
        first_gain,
        first_shift,
        second_gain,
        second_shift,
    ) = weights
    packed = jnp.concatenate((w_query, w_key, w_value), axis=1)
    width = w_query.shape[1]
    shape_heads = queries.shape
    ignored, pull_second = jax.vjp(
        norm_rows, total, second_gain.astype(jnp.float32), second_shift.astype(jnp.float32)
    )
    grad_total, grad_second_gain, grad_second_shift = pull_second(grad_result)
    grad_branch = spread_back(grad_total.astype(jnp.bfloat16))
    down_grad = row_dot(active, grad_branch)
    grad_active = back_dot(grad_branch, w_down)
    ignored, pull_gelu = jax.vjp(gelu_smooth, hidden)
    grad_hidden = pull_gelu(grad_active)[0].astype(jnp.bfloat16)
    gathered_normed = saved_inputs[1]
    hidden_grad = row_dot(gathered_normed, grad_hidden)
    grad_normed = grad_total + collect_back(back_dot(grad_hidden, w_hidden))
    ignored, pull_first = jax.vjp(
        norm_rows, summed, first_gain.astype(jnp.float32), first_shift.astype(jnp.float32)
    )
    grad_summed, grad_first_gain, grad_first_shift = pull_first(grad_normed)
    grad_attention = spread_back(grad_summed.astype(jnp.bfloat16))
    output_grad = row_dot(mixed, grad_attention)
    grad_mixed = back_dot(grad_attention, w_output).astype(jnp.bfloat16).reshape(shape_heads)
    grad_query, grad_key, grad_value = attend_back(
        queries, keys, values, grad_mixed, log_totals, segment_ids
    )
    grad_packed = jnp.concatenate(
        (grad_query.reshape(-1, width), grad_key.reshape(-1, width), grad_value.reshape(-1, width)),
        axis=1,
    )
    gathered = saved_inputs[0]
    packed_grad = row_dot(gathered, grad_packed)
    grad_rows = grad_summed + collect_back(back_dot(grad_packed, packed))
    large = (
        packed_grad[:, :width],
        packed_grad[:, width : 2 * width],
        packed_grad[:, 2 * width :],
        output_grad,
        hidden_grad,
        down_grad,
    )
    small = (grad_first_gain, grad_first_shift, grad_second_gain, grad_second_shift)
    return (grad_rows, large, small)


def body(
    embedded,
    piece_lengths,
    pair_tags,
    pair_embedding,
    w_query,
    w_key,
    w_value,
    w_output,
    w_hidden,
    w_down,
    first_gain,
    first_shift,
    second_gain,
    second_shift,
    cotangent,
):
    local_rows = embedded.shape[0]
    offset = lax.axis_index("tensor") * local_rows
    segment_ids = segments(piece_lengths)
    flat_segments = segment_ids.reshape(-1)
    row_valid = lax.dynamic_slice_in_dim(flat_segments, offset, local_rows, 0) < PIECES - 1
    row_sequence = (offset + jnp.arange(local_rows, dtype=jnp.int32)) // LEN
    seq_count = piece_lengths.shape[0]
    owners = row_sequence[:, None] == jnp.arange(seq_count, dtype=jnp.int32)[None, :]
    row_tags = jnp.sum(jnp.where(owners, pair_tags[None, :], 0), axis=1)
    row_pairs = (row_tags[:, None] == jnp.arange(PAIRS, dtype=jnp.int32)[None, :]).astype(
        jnp.float32
    )
    fetched = (
        lax.all_gather(w_query, "dp", axis=0, tiled=True),
        lax.all_gather(w_key, "dp", axis=0, tiled=True),
        lax.all_gather(w_value, "dp", axis=0, tiled=True),
        lax.all_gather(w_output, "dp", axis=1, tiled=True),
        lax.all_gather(w_hidden, "dp", axis=0, tiled=True),
        lax.all_gather(w_down, "dp", axis=1, tiled=True),
        lax.all_gather(first_gain, "dp", axis=0, tiled=True),
        lax.all_gather(first_shift, "dp", axis=0, tiled=True),
        lax.all_gather(second_gain, "dp", axis=0, tiled=True),
        lax.all_gather(second_shift, "dp", axis=0, tiled=True),
        lax.all_gather(pair_embedding, "dp", axis=1, tiled=True),
    )
    weights = fetched[:10]
    table = fetched[10].astype(jnp.float32)
    start_rows = embedded + jnp.dot(row_pairs, table, precision=HIGH)
    first_out, first_saved = forward_visit(start_rows, weights, segment_ids)
    second_out, second_saved = forward_visit(first_out, weights, segment_ids)
    seed_rows = cotangent * row_valid[:, None].astype(jnp.float32)
    grad_first, second_large, second_small = backward_visit(
        seed_rows, second_saved, weights, segment_ids
    )
    grad_start, first_large, first_small = backward_visit(
        grad_first, first_saved, weights, segment_ids
    )
    table_grad = lax.dot_general(
        row_pairs,
        grad_start,
        (((0,), (0,)), ((), ())),
        precision=HIGH,
        preferred_element_type=jnp.float32,
    )
    large = tuple((a + b for a, b in zip(first_large, second_large)))
    small = tuple((a + b for a, b in zip(first_small, second_small))) + (table_grad,)
    small = lax.psum(small, "tensor")
    totals = (
        *side_by_side(
            (
                large[0].astype(jnp.bfloat16),
                large[1].astype(jnp.bfloat16),
                large[2].astype(jnp.bfloat16),
            ),
            "dp",
            0,
            1,
        ),
        summed_on_arrival(large[3].astype(jnp.bfloat16), "dp", 1),
        summed_on_arrival(large[4].astype(jnp.bfloat16), "dp", 0),
        summed_on_arrival(large[5].astype(jnp.bfloat16), "dp", 1),
        summed_on_arrival(small[0].astype(jnp.bfloat16), "dp", 0),
        summed_on_arrival(small[1].astype(jnp.bfloat16), "dp", 0),
        summed_on_arrival(small[2].astype(jnp.bfloat16), "dp", 0),
        summed_on_arrival(small[3].astype(jnp.bfloat16), "dp", 0),
        summed_on_arrival(small[4].astype(jnp.bfloat16), "dp", 1),
    )
    return (
        second_out,
        grad_start,
        totals[10],
        totals[0],
        totals[1],
        totals[2],
        totals[3],
        totals[4],
        totals[5],
        totals[6],
        totals[7],
        totals[8],
        totals[9],
    )


def solution(mesh):
    in_specs = (
        P(("dp", "tensor"), None),
        P("dp", None),
        P("dp"),
        P(None, "dp"),
        P("dp", "tensor"),
        P("dp", "tensor"),
        P("dp", "tensor"),
        P("tensor", "dp"),
        P("dp", "tensor"),
        P("tensor", "dp"),
        P("dp"),
        P("dp"),
        P("dp"),
        P("dp"),
        P(("dp", "tensor"), None),
    )
    out_specs = (
        P(("dp", "tensor"), None),
        P(("dp", "tensor"), None),
        P(None, "dp"),
        P("dp", "tensor"),
        P("dp", "tensor"),
        P("dp", "tensor"),
        P("tensor", "dp"),
        P("dp", "tensor"),
        P("tensor", "dp"),
        P("dp"),
        P("dp"),
        P("dp"),
        P("dp"),
    )
    return jax.shard_map(body, mesh=mesh, in_specs=in_specs, out_specs=out_specs, check_vma=False)
```

profile of v0, /device:TPU:0, one launch (start us, length us, event | category | flops | bytes accessed | tf_op | source)
XLA Modules:
  0.0 1193.3 jit_solution(4407409485672931314)
XLA Ops:
  10.1 42.4 %all-gather = bf16[16,32,4]{1,2,0:T(4,128)(2,1)S(1)} all-gather(bf16[1,32,4]{1,2,0:T(4,128)(2,1)S(1)} %bitcast.350), channel_id=1, replica_groups=mesh['dp'=16,'tensor'=2] {'dp'}, dimensions={0}, use_global_device_ids=true | all-gather | bytes 4352 | tf_op jit(solution)/shard_map/all_gather | solution.py:323
  55.3 36.9 %all_gather.59 = bf16[512,256]{1,0:T(8,128)(2,1)S(1)} all-gather(bf16[32,256]{1,0:T(8,128)(2,1)S(1)} %copy-done.73), channel_id=1, replica_groups=mesh['dp'=16,'tensor'=2] {'dp'}, dimensions={0}, use_global_device_ids=true | all-gather | bytes 278528 | tf_op jit(solution)/shard_map/all_gather | solution.py:313
  92.2 39.0 %all_gather.60 = bf16[512,256]{1,0:T(8,128)(2,1)S(1)} all-gather(bf16[32,256]{1,0:T(8,128)(2,1)S(1)} %copy-done.74), channel_id=1, replica_groups=mesh['dp'=16,'tensor'=2] {'dp'}, dimensions={0}, use_global_device_ids=true | all-gather | bytes 278528 | tf_op jit(solution)/shard_map/all_gather | solution.py:314
  131.2 37.2 %all_gather.61 = bf16[512,256]{1,0:T(8,128)(2,1)S(1)} all-gather(bf16[32,256]{1,0:T(8,128)(2,1)S(1)} %copy-done.75), channel_id=1, replica_groups=mesh['dp'=16,'tensor'=2] {'dp'}, dimensions={0}, use_global_device_ids=true | all-gather | bytes 278528 | tf_op jit(solution)/shard_map/all_gather | solution.py:315
  168.5 41.0 %all_gather.62 = bf16[256,512]{0,1:T(8,128)(2,1)} all-gather(bf16[256,32]{0,1:T(8,128)(2,1)S(1)} %copy-done.76), channel_id=1, replica_groups=mesh['dp'=16,'tensor'=2] {'dp'}, dimensions={1}, use_global_device_ids=true | all-gather | bytes 278528 | tf_op jit(solution)/shard_map/all_gather | solution.py:316
  231.2 45.7 %while.107 = (s32[]{:T(128)}, bf16[2,1024,4,64]{3,2,1,0:T(4,128)(2,1)}, f32[2,2,4,512]{3,2,1,0:T(4,128)S(1)}, bf16[2,1024,4,64]{1,3,2,0:T(8,128)(2,1)}, s32[2,10...) while((s32[]{:T(128)}, ...), condition=%wide.region_8.9_spmd, body=%wide.region_3.8_spmd.sunk | while | flops 564264448 | bytes 34730944 | solution.py:132
  233.7 18.4 %while.114 = (s32[]{:T(128)}, bf16[2,512,4,64]{1,3,2,0:T(8,128)(2,1)S(1)}, f32[2,4,512]{2,1,0:T(4,128)S(1)}, s32[2]{0:T(128)S(1)}, s32[1024]{0:T(1024)S(1)}, /*i...) while((s32[]{:T(128)}, ...), condition=%wide.region_7.7_spmd, body=%wide.region_4.6_spmd.sunk | while | flops 564264448 | bytes 28922052 | solution.py:129
  256.5 18.3 %while.114 = (s32[]{:T(128)}, bf16[2,512,4,64]{1,3,2,0:T(8,128)(2,1)S(1)}, f32[2,4,512]{2,1,0:T(4,128)S(1)}, s32[2]{0:T(128)S(1)}, s32[1024]{0:T(1024)S(1)}, /*i...) while((s32[]{:T(128)}, ...), condition=%wide.region_7.7_spmd, body=%wide.region_4.6_spmd.sunk | while | flops 564264448 | bytes 28922052 | solution.py:129
  285.8 36.7 %all-reduce.5 = (bf16[512]{0:T(512)(128)(2,1)S(1)}, bf16[512]{0:T(512)(128)(2,1)S(1)}, bf16[512]{0:T(512)(128)(2,1)S(1)}, bf16[512]{0:T(512)(128)(2,1)S(1)}) all-reduce(bf16[512]{0:T(512)(128)(2,1)S(1)} %dynamic-update-slice.1, bf16[512]{0:T(512)(128)(2,1)S(1)} %dynamic-update-slice, ...), channel_id=1, replica_groups=mesh['dp'=16,'tensor'=2] {'dp'}, use_global_device_ids=true, to_apply=%add.1 | all-reduce | flops 2048 | bytes 8192
  337.2 11.4 all-gather.14.cloned.1.call-done
  348.6 10.5 multiply_convert_fusion.3
  359.2 49.1 %all-gather.18.cloned.1.call-done = bf16[1024,512]{0,1:T(8,128)(2,1)} async-done(((bf16[1024,32]{0,1:T(8,128)(2,1)}), bf16[1024,512]{0,1:T(8,128)(2,1)}) %all-gather.18.cloned.1.call-update) | async-done | bytes 1048592 | tf_op jit(solution)/shard_map/all_gather | solution.py:318
  428.1 11.9 all-gather.20.cloned.1.call-done
  460.7 47.7 %while.109 = (s32[]{:T(128)}, bf16[2,1024,4,64]{3,2,1,0:T(4,128)(2,1)}, f32[2,2,4,512]{3,2,1,0:T(4,128)S(1)}, bf16[2,1024,4,64]{1,3,2,0:T(8,128)(2,1)S(1)}, s32[...) while((s32[]{:T(128)}, ...), condition=%wide.region_20.21_spmd, body=%wide.region_15.20_spmd.sunk | while | flops 564264448 | bytes 34731452 | solution.py:132
  462.1 19.5 %while.115 = (s32[]{:T(128)}, bf16[2,512,4,64]{1,3,2,0:T(8,128)(2,1)}, f32[2,4,512]{2,1,0:T(4,128)S(1)}, s32[2]{0:T(128)S(1)}, s32[1024]{0:T(1024)S(1)}, /*index...) while((s32[]{:T(128)}, ...), condition=%wide.region_19.19_spmd, body=%wide.region_16.18_spmd.sunk | while | flops 564264448 | bytes 28922560 | solution.py:129
  485.9 19.5 %while.115 = (s32[]{:T(128)}, bf16[2,512,4,64]{1,3,2,0:T(8,128)(2,1)}, f32[2,4,512]{2,1,0:T(4,128)S(1)}, s32[2]{0:T(128)S(1)}, s32[1024]{0:T(1024)S(1)}, /*index...) while((s32[]{:T(128)}, ...), condition=%wide.region_19.19_spmd, body=%wide.region_16.18_spmd.sunk | while | flops 564264448 | bytes 28922560 | solution.py:129
  516.5 10.7 reduce-scatter.13.cloned.1.call-done
  531.7 11.7 all-gather.22.cloned.1.call-done
  576.3 11.6 all-gather.24.cloned.1.call-done
  603.8 10.9 reduce-scatter.17.cloned.1.call-done
  622.2 11.3 all-gather.26.cloned.1.call-done
  646.6 142.5 %while.111 = (s32[]{:T(128)}, bf16[2,1024,4,64]{3,2,1,0:T(4,128)(2,1)}, bf16[2,1024,4,64]{1,3,2,0:T(8,128)(2,1)}, bf16[2,1024,4,64]{1,3,2,0:T(8,128)(2,1)}, bf16...) while((s32[]{:T(128)}, ...), condition=%wide.region_36.37_spmd, body=%wide.region_32.36_spmd.sunk | while | flops 1377828352 | bytes 151378192 | solution.py:183
  651.7 60.6 %while.116 = (s32[]{:T(128)}, f32[1024,4,64]{0,2,1:T(8,128)S(1)}, f32[1024,4,64]{0,2,1:T(8,128)}, bf16[2,512,4,64]{1,3,2,0:T(8,128)(2,1)}, s32[2]{0:T(128)S(1)},...) while((s32[]{:T(128)}, f32[1024,4,64]{0,2,1:T(8,128)S(1)}, ...), condition=%wide.region_35.35_spmd.clone, body=%wide.region_33.34_spmd.clone.sunk | while | flops 1377304064 | bytes 132985736 | solution.py:174
  722.9 60.6 %while.116 = (s32[]{:T(128)}, f32[1024,4,64]{0,2,1:T(8,128)S(1)}, f32[1024,4,64]{0,2,1:T(8,128)}, bf16[2,512,4,64]{1,3,2,0:T(8,128)(2,1)}, s32[2]{0:T(128)S(1)},...) while((s32[]{:T(128)}, f32[1024,4,64]{0,2,1:T(8,128)S(1)}, ...), condition=%wide.region_35.35_spmd.clone, body=%wide.region_33.34_spmd.clone.sunk | while | flops 1377304064 | bytes 132985736 | solution.py:174
  803.1 10.8 reduce-scatter.19.cloned.1.call-done
  820.9 11.9 all-gather.28.cloned.1.call-done
  832.8 10.2 fusion.90
  901.1 142.3 %while.113 = (s32[]{:T(128)}, bf16[2,1024,4,64]{3,2,1,0:T(4,128)(2,1)}, bf16[2,1024,4,64]{1,3,2,0:T(8,128)(2,1)}, bf16[2,1024,4,64]{1,3,2,0:T(8,128)(2,1)}, bf16...) while((s32[]{:T(128)}, ...), condition=%wide.region_47.48_spmd, body=%wide.region_43.47_spmd.sunk | while | flops 1377828352 | bytes 142989520 | solution.py:183
  906.4 60.6 %while.117 = (s32[]{:T(128)}, f32[1024,4,64]{0,2,1:T(8,128)S(1)}, f32[1024,4,64]{0,2,1:T(8,128)}, bf16[2,512,4,64]{1,3,2,0:T(8,128)(2,1)}, s32[2]{0:T(128)S(1)},...) while((s32[]{:T(128)}, f32[1024,4,64]{0,2,1:T(8,128)S(1)}, ...), condition=%wide.region_46.46_spmd.clone, body=%wide.region_44.45_spmd.clone.sunk | while | flops 1377304064 | bytes 132985736 | solution.py:174
  977.5 60.6 %while.117 = (s32[]{:T(128)}, f32[1024,4,64]{0,2,1:T(8,128)S(1)}, f32[1024,4,64]{0,2,1:T(8,128)}, bf16[2,512,4,64]{1,3,2,0:T(8,128)(2,1)}, s32[2]{0:T(128)S(1)},...) while((s32[]{:T(128)}, f32[1024,4,64]{0,2,1:T(8,128)S(1)}, ...), condition=%wide.region_46.46_spmd.clone, body=%wide.region_44.45_spmd.clone.sunk | while | flops 1377304064 | bytes 132985736 | solution.py:174
  1072.2 11.6 all-to-all-done.3
  1108.0 12.4 %all-to-all-done.1 = bf16[16,32,768]{2,1,0:T(8,128)(2,1)} async-done(((bf16[16,32,768]{2,1,0:T(8,128)(2,1)}), bf16[16,32,768]{2,1,0:T(8,128)(2,1)}, u32[]{:S(2)}, u32[]{:S(2)}) %all-to-all-start.1) | async-done | bytes 786464 | tf_op jit(solution)/shard_map/all_to_all | solution.py:24
  (756 shorter events, 718.3 us)
Async XLA Ops:
  8.0 201.5 %all-gather.12.cloned.1.call-start = ((), (), s32[]{:S(2)}) async-start(), calls=%async_computation.17 | async-start | bytes 3145728 | tf_op jit(solution)/shard_map/all_gather | solution.py:73
  54.9 113.6 %copy-start.76 = (bf16[256,32]{0,1:T(8,128)(2,1)S(1)}, bf16[256,32]{0,1:T(8,128)(2,1)}, u32[]{:S(2)}) copy-start(bf16[256,32]{0,1:T(8,128)(2,1)} %param.38) | copy-start | bytes 49156
  54.9 267.7 %reduce-scatter.9.cloned.1.call-start = ((), (), s32[]{:S(2)}) async-start(), calls=%async_computation.18 | async-start | bytes 3145728 | tf_op jit(solution)/shard_map/reduce_scatter | solution.py:77
  282.7 54.6 %all-gather.16.cloned.1.call-start = ((), (), s32[]{:S(2)}) async-start(), calls=%async_computation.20 | async-start | bytes 1114112 | tf_op jit(solution)/shard_map/all_gather | solution.py:317
  283.3 65.4 %all-gather.14.cloned.1.call-start = ((), (), s32[]{:S(2)}) async-start(), calls=%async_computation.19 | async-start | bytes 3145728 | tf_op jit(solution)/shard_map/all_gather | solution.py:73
  322.6 100.4 %copy-start.41 = (f32[512]{0:T(512)}, f32[512]{0:T(512)S(1)}, u32[]{:S(2)}) copy-start(f32[512]{0:T(512)S(1)} %convert_element_type.248) | copy-start | bytes 6148
  322.6 100.4 %copy-start.61 = (f32[512]{0:T(512)}, f32[512]{0:T(512)S(1)}, u32[]{:S(2)}) copy-start(f32[512]{0:T(512)S(1)} %convert_element_type.249) | copy-start | bytes 6148
  325.0 98.0 %copy-start.4 = (f32[1024,512]{0,1:T(8,128)}, f32[1024,512]{0,1:T(8,128)S(1)}, u32[]{:S(2)}) copy-start(f32[1024,512]{0,1:T(8,128)S(1)} %get-tuple-element.851) | copy-start | bytes 6291460
  325.0 98.0 %copy-start.44 = (f32[1024]{0:T(1024)}, f32[1024]{0:T(1024)S(1)}, u32[]{:S(2)}) copy-start(f32[1024]{0:T(1024)S(1)} %broadcast_multiply_fusion.3) | copy-start | bytes 12292
  326.7 81.6 %all-gather.18.cloned.1.call-start = ((), (), s32[]{:S(2)}) async-start(), calls=%async_computation.21 | async-start | bytes 1114112 | tf_op jit(solution)/shard_map/all_gather | solution.py:318
  327.3 95.7 %reduce-scatter.11.cloned.1.call-start = ((), (), s32[]{:S(2)}) async-start(), calls=%async_computation.22 | async-start | bytes 3145728 | tf_op jit(solution)/shard_map/reduce_scatter | solution.py:77
  414.5 25.5 %all-gather.20.cloned.1.call-start = ((), (), s32[]{:S(2)}) async-start(), calls=%async_computation.23 | async-start | bytes 3145728 | tf_op jit(solution)/shard_map/all_gather | solution.py:73
  428.1 99.1 %reduce-scatter.13.cloned.1.call-start = ((), (), s32[]{:S(2)}) async-start(), calls=%async_computation.24 | async-start | bytes 3145728 | tf_op jit(solution)/shard_map/reduce_scatter | solution.py:77
  516.2 27.2 %all-gather.22.cloned.1.call-start = ((), (), s32[]{:S(2)}) async-start(), calls=%async_computation.25 | async-start | bytes 3145728 | tf_op jit(solution)/shard_map/all_gather | solution.py:73
  531.7 34.7 %reduce-scatter.15.cloned.1.call-start = ((), (), s32[]{:S(2)}) async-start(), calls=%async_computation.26 | async-start | bytes 3145728 | tf_op jit(solution)/shard_map/reduce_scatter | solution.py:77
  555.5 32.4 %all-gather.24.cloned.1.call-start = ((), (), s32[]{:S(2)}) async-start(), calls=%async_computation.27 | async-start | bytes 3145728 | tf_op jit(solution)/shard_map/all_gather | solution.py:83
  576.0 38.7 %reduce-scatter.17.cloned.1.call-start = ((), (), s32[]{:S(2)}) async-start(), calls=%async_computation.28 | async-start | bytes 3145728 | tf_op jit(solution)/shard_map/reduce_scatter | solution.py:87
  603.8 29.7 %all-gather.26.cloned.1.call-start = ((), (), s32[]{:S(2)}) async-start(), calls=%async_computation.29 | async-start | bytes 3145728 | tf_op jit(solution)/shard_map/all_gather | solution.py:83
  621.7 192.2 %reduce-scatter.19.cloned.1.call-start = ((), (), s32[]{:S(2)}) async-start(), calls=%async_computation.30 | async-start | bytes 3145728 | tf_op jit(solution)/shard_map/reduce_scatter | solution.py:87
  803.1 29.8 %all-gather.28.cloned.1.call-start = ((), (), s32[]{:S(2)}) async-start(), calls=%async_computation.31 | async-start | bytes 3145728 | tf_op jit(solution)/shard_map/all_gather | solution.py:83
  820.9 38.8 %reduce-scatter.21.cloned.1.call-start = ((), (), s32[]{:S(2)}) async-start(), calls=%async_computation.32 | async-start | bytes 3145728 | tf_op jit(solution)/shard_map/reduce_scatter | solution.py:87
  848.8 42.6 %all-gather.30.cloned.1.call-start = ((), (), s32[]{:S(2)}) async-start(), calls=%async_computation.33 | async-start | bytes 3145728 | tf_op jit(solution)/shard_map/all_gather | solution.py:83
  875.8 176.6 %all-to-all-start.4 = ((bf16[16,1024,32]{1,2,0:T(8,128)(2,1)}), bf16[16,1024,32]{1,2,0:T(8,128)(2,1)}, u32[]{:S(2)}, u32[]{:S(2)}) async-start(bf16[16,1024,32]{1,2,0:T(8,128)(2,1)} %bitcast.47), calls=%async_computation.12 | async-start | bytes 2097152 | tf_op jit(solution)/shard_map/all_to_all | solution.py:24
  1052.4 31.3 %all-to-all-start.3 = ((bf16[16,32,1024]{2,1,0:T(8,128)(2,1)}), bf16[16,32,1024]{2,1,0:T(8,128)(2,1)S(1)}, u32[]{:S(2)}, u32[]{:S(2)}) async-start(bf16[16,32,1024]{2,1,0:T(8,128)(2,1)} %bitcast.45), calls=%async_computation.11 | async-start | bytes 2097152 | tf_op jit(solution)/shard_map/all_to_all | solution.py:24
  1059.5 62.2 %reduce-scatter.23.cloned.1.call-start = ((), (), s32[]{:S(2)}) async-start(), calls=%async_computation.34 | async-start | bytes 3145728 | tf_op jit(solution)/shard_map/reduce_scatter | solution.py:87
  1083.8 14.3 %all-to-all-start.2 = ((bf16[16,256,32]{1,2,0:T(8,128)(2,1)}), bf16[16,256,32]{1,2,0:T(8,128)(2,1)S(1)}, u32[]{:S(2)}, u32[]{:S(2)}) async-start(bf16[16,256,32]{1,2,0:T(8,128)(2,1)} %bitcast.44), calls=%async_computation.10 | async-start | bytes 524288 | tf_op jit(solution)/shard_map/all_to_all | solution.py:24
  1098.1 22.3 %all-to-all-start.1 = ((bf16[16,32,768]{2,1,0:T(8,128)(2,1)}), bf16[16,32,768]{2,1,0:T(8,128)(2,1)}, u32[]{:S(2)}, u32[]{:S(2)}) async-start(bf16[16,32,768]{2,1,0:T(8,128)(2,1)} %bitcast.339), calls=%async_computation.9 | async-start | bytes 1572864 | tf_op jit(solution)/shard_map/all_to_all | solution.py:24
  1129.1 11.6 all-to-all-start.8
  1140.7 12.1 %all-to-all-start.7 = ((bf16[16,1,32]{2,1,0:T(2,128)(2,1)}), bf16[16,1,32]{2,1,0:T(2,128)(2,1)S(1)}, u32[]{:S(2)}, u32[]{:S(2)}) async-start(bf16[16,1,32]{2,1,0:T(2,128)(2,1)} %all_to_all.54), calls=%async_computation.15 | async-start | bytes 16384 | tf_op jit(solution)/shard_map/all_to_all | solution.py:24
  1152.8 10.7 all-to-all-start.6
  1163.5 10.7 all-to-all-start.5
  1174.2 10.8 all-to-all-start
  (132 other events, 1040.1 us)
Sparse Core Ops, SparseCore 0:
  55.1 6.4 all-gather.11
  282.8 5.5 reduce-scatter.8
  428.2 11.7 all-gather.19
  516.4 10.7 reduce-scatter.12
  576.1 11.7 all-gather.23
  603.9 10.7 reduce-scatter.16
  821.0 11.7 all-gather.27
  848.9 10.7 reduce-scatter.20
Sparse Core Ops, SparseCore 1:
  285.9 51.3 all-gather.15
  339.3 9.3 all-gather.13
  351.7 56.5 all-gather.17
  414.5 8.4 reduce-scatter.10
  531.8 11.6 all-gather.21
  555.6 10.7 reduce-scatter.14
  621.8 11.6 all-gather.25
  803.1 10.7 reduce-scatter.18
  866.8 11.6 all-gather.29
  1064.3 10.8 reduce-scatter.22
where the time goes:
time: 1200 us; the launch traced here: 1190 us
  matrix products  337 us (28%)
  waiting for transfers between devices  239 us (20%)
  blocking collectives  237 us (20%)
  local copies, waits for them, and re-layouts  175 us (15%)
  other arithmetic  115 us (10%)
  starting transfers between devices  46 us (4%)
  loops' own time  27.7 us (2%)
  between operations  18 us (2%)
    all_to_all x9, waiting for transfers between devices, summed_on_arrival(): lax.all_to_all(blocks, axis, split_axis=0, concat_axis=0, tiled=True)  55.9 us
    dot_general x16, matrix products, block_scores(): jnp.einsum('qhd,khd->hqk', query_block, key_seq, preferred_element_type=j...  50.5 us
    all_gather x1, waiting for transfers between devices, body(): lax.all_gather(w_down, 'dp', axis=1, tiled=True)  49.1 us
    dot_general x8, matrix products, one_block(): jnp.einsum('qhd,khd->hqk', grad_block, value_seq, preferred_element_type=...  46 us
    all_to_all x9, starting transfers between devices, summed_on_arrival(): lax.all_to_all(blocks, axis, split_axis=0, concat_axis=0, tiled=True)  44.2 us
    dot_general x8, matrix products, back_dot(): lax.dot_general(left, right, (((1,), (1,)), ((), ())), preferred_element_...  42.7 us
    all_gather x1, blocking collectives, body(): lax.all_gather(pair_embedding, 'dp', axis=1, tiled=True)  42.4 us
    all_gather x1, blocking collectives, body(): lax.all_gather(w_output, 'dp', axis=1, tiled=True)  41 us
  transfers between devices with their start and end apart: 27, of which 22 were waited for; matrix products, arithmetic and copies ran while one was open for 18% of the time, Pallas kernels for 0%

commit v1 on v0

v1 whole, which is shorter than its diff:
```python
import functools
import math

import jax
import jax.numpy as jnp
from jax import lax
from jax.sharding import PartitionSpec as P
from jax.experimental import pallas as pl
from jax.experimental.pallas import tpu as pltpu

HEAD_DIM = 64
LEN = 1024
PIECES = 8
PAIRS = 4
D = 512
FF = 2048
HALF = 256
QB = 128
NQ = LEN // QB
BIG = 1e30
LOG2E = math.log2(math.e)
QSCALE = LOG2E / math.sqrt(HEAD_DIM)
KSCALE = math.log(2.0)
WIDTHS = (1, 2, 3, 4, 5, 6, 8)
EPS = 1e-5
C1 = math.sqrt(2.0 / math.pi)
C2 = C1 * 0.044715
F32 = jnp.float32
BF = jnp.bfloat16
VMEM_LIMIT = 60 * 1024 * 1024


def nn(a, b):
    return jnp.dot(a, b, preferred_element_type=F32)


def nt(a, b):
    return lax.dot_general(a, b, (((1,), (1,)), ((), ())), preferred_element_type=F32)


def tn(a, b):
    return lax.dot_general(a, b, (((0,), (0,)), ((), ())), preferred_element_type=F32)


def piece_ends(pieces_ref):
    ends, at = [], 0
    for j in range(PIECES):
        at = at + pieces_ref[j]
        ends.append(at)
    return ends


def window(block, ends):
    first = block * QB
    last = first + QB - 1
    low, high = jnp.int32(0), jnp.int32(LEN)
    for end in ends[:-1]:
        low = jnp.maximum(low, jnp.where(end <= first, end, 0))
        high = jnp.minimum(high, jnp.where(end > last, end, LEN))
    low = jnp.where(first >= ends[-2], first, low)
    high = jnp.where(last >= ends[-2], last + 1, high)
    return low // QB, (high + QB - 1) // QB


def over_widths(block, ends, run):
    low, high = window(block, ends)
    count = high - low
    previous = 0
    for wide in WIDTHS:
        begin = jnp.minimum(low, NQ - wide)

        @pl.when((count > previous) & (count <= wide))
        def _(wide=wide, begin=begin):
            run(wide, pl.multiple_of(begin * QB, QB))

        previous = wide


def segment_codes(ends, segq_ref, segk_ref):
    rows = lax.broadcasted_iota(jnp.int32, (LEN, 128), 0)
    lanes = lax.broadcasted_iota(jnp.int32, (LEN, 128), 1)
    ids = jnp.zeros((LEN, 128), jnp.int32)
    for end in ends[:-1]:
        ids = ids + jnp.where(rows >= end, 1, 0)
    same = lanes == ids
    segk_ref[...] = jnp.where(same, 1.0, 0.0).astype(BF)
    free = (lanes >= PIECES) | (same & (lanes < PIECES - 1))
    segq_ref[...] = jnp.where(free, 0.0, -BIG).astype(BF)


def lane_half(shape):
    return lax.broadcasted_iota(jnp.int32, shape, 1) < HEAD_DIM


def two_heads(block):
    left = lane_half(block.shape)
    zero = jnp.zeros_like(block)
    return jnp.where(left, block, zero), jnp.where(left, zero, block)


def attend_kernel(pieces_ref, x_ref, w_ref, q_ref, k_ref, v_ref, mixed_ref, exact_ref, inv_ref, p_ref,
                  segq_ref, segk_ref, vt_ref):
    step = pl.program_id(0)
    ends = piece_ends(pieces_ref)

    @pl.when(step == 0)
    def _():
        low = x_ref[...].astype(BF)
        q_ref[...] = (nn(low, w_ref[:, :HALF]) * QSCALE).astype(BF)
        k_ref[...] = nn(low, w_ref[:, HALF:2 * HALF]).astype(BF)
        values = nn(low, w_ref[:, 2 * HALF:])
        v_ref[...] = values.astype(BF)
        for pair in range(2):
            vt_ref[pair, :128, :] = values[:, pair * 128:(pair + 1) * 128].T.astype(BF)
            vt_ref[pair, 128:, :] = jnp.ones((16, LEN), BF)
        segment_codes(ends, segq_ref, segk_ref)

    rows = pl.ds(pl.multiple_of(step * QB, QB), QB)

    def run(wide, begin):
        keys = pl.ds(begin, wide * QB)
        segq = segq_ref[rows, :]
        segk = segk_ref[keys, :]
        pad = lax.broadcasted_iota(jnp.int32, (QB, 128), 0) + step * QB >= ends[-2]
        for pair in range(2):
            cols = slice(pair * 128, (pair + 1) * 128)
            even, odd = two_heads(q_ref[rows, cols])
            query = jnp.concatenate(
                [jnp.concatenate([even, segq], axis=1), jnp.concatenate([odd, segq], axis=1)], axis=0)
            key = jnp.concatenate([k_ref[keys, cols], segk], axis=1)
            scores = nt(key, query)
            top = jnp.max(scores, axis=0, keepdims=True)
            probs = jnp.exp2(scores - top).astype(BF)
            p_ref[0, pair, :wide * QB, :] = probs
            out = nn(vt_ref[pair, :, keys], probs)
            inv = 1.0 / out[128:129, :]
            inv_both = jnp.concatenate(
                [jnp.broadcast_to(inv[:, :128], (64, 128)), jnp.broadcast_to(inv[:, 128:], (64, 128))], axis=0)
            out_both = jnp.concatenate([out[:64, :128], out[64:128, 128:]], axis=0) * inv_both
            exact = out_both.T
            exact_ref[:, cols] = exact
            mixed_ref[:, cols] = jnp.where(pad, v_ref[rows, cols].astype(F32), exact).astype(BF)
            inv_ref[:, cols] = inv_both.T

    over_widths(step, ends, run)


def attend(pieces, x, w):
    whole = lambda i: (0, 0)
    block = lambda i: (i, 0)
    return pl.pallas_call(
        attend_kernel,
        grid=(NQ,),
        in_specs=[
            pl.BlockSpec(memory_space=pltpu.SMEM),
            pl.BlockSpec((LEN, D), whole),
            pl.BlockSpec((D, 3 * HALF), whole),
        ],
        out_specs=[
            pl.BlockSpec((LEN, HALF), whole),
            pl.BlockSpec((LEN, HALF), whole),
            pl.BlockSpec((LEN, HALF), whole),
            pl.BlockSpec((QB, HALF), block),
            pl.BlockSpec((QB, HALF), block),
            pl.BlockSpec((QB, HALF), block),
            pl.BlockSpec((1, 2, LEN, 256), lambda i: (i, 0, 0, 0)),
        ],
        out_shape=[
            jax.ShapeDtypeStruct((LEN, HALF), BF),
            jax.ShapeDtypeStruct((LEN, HALF), BF),
            jax.ShapeDtypeStruct((LEN, HALF), BF),
            jax.ShapeDtypeStruct((LEN, HALF), BF),
            jax.ShapeDtypeStruct((LEN, HALF), F32),
            jax.ShapeDtypeStruct((LEN, HALF), F32),
            jax.ShapeDtypeStruct((NQ, 2, LEN, 256), BF),
        ],
        scratch_shapes=[
            pltpu.VMEM((LEN, 128), BF),
            pltpu.VMEM((LEN, 128), BF),
            pltpu.VMEM((2, 144, LEN), BF),
        ],
        compiler_params=pltpu.CompilerParams(vmem_limit_bytes=VMEM_LIMIT),
    )(pieces, x, w)


def attend_back_kernel(pieces_ref, base_ref, x_ref, w_ref, q_ref, k_ref, v_ref, mixed_ref, grad_ref, p_ref,
                       old_ref, dx_ref, dw_ref, dk_ref, dv_ref, grads_ref, kt_ref):
    step = pl.program_id(0)
    ends = piece_ends(pieces_ref)

    @pl.when(step == 0)
    def _():
        dk_ref[...] = jnp.zeros_like(dk_ref)
        dv_ref[...] = jnp.zeros_like(dv_ref)
        for pair in range(2):
            kt_ref[pair] = k_ref[:, pair * 128:(pair + 1) * 128].astype(F32).T.astype(BF)

    rows = pl.ds(pl.multiple_of(step * QB, QB), QB)

    def run(wide, begin):
        keys = pl.ds(begin, wide * QB)
        for pair in range(2):
            cols = slice(pair * 128, (pair + 1) * 128)
            grad = grad_ref[rows, cols]
            inner = grad.astype(F32) * mixed_ref[rows, cols]
            high = inner.astype(BF)
            rest = pltpu.roll(inner - high.astype(F32), HEAD_DIM, 1).astype(BF)
            left = lane_half(inner.shape)
            inner = jnp.concatenate([jnp.where(left, high, rest), jnp.where(left, rest, high)], axis=0)
            outer = jnp.concatenate(two_heads(grad), axis=0)
            both = jnp.concatenate([outer, inner], axis=1)
            value = jnp.concatenate([v_ref[keys, cols], jnp.full((wide * QB, 128), -1.0, BF)], axis=1)
            probs = p_ref[0, pair, :wide * QB, :]
            slope = nt(value, both)
            scores = (probs.astype(F32) * slope).astype(BF)
            query = jnp.concatenate(two_heads(q_ref[rows, cols]), axis=0)
            dv_ref[pair, keys, :] += nn(probs, outer)
            dk_ref[pair, keys, :] += nn(scores, query)
            out = nn(kt_ref[pair, :, keys], scores)
            out = jnp.concatenate([out[:64, :128], out[64:, 128:]], axis=0)
            grads_ref[rows, cols] = (out.T * (HEAD_DIM ** -0.5)).astype(BF)

    over_widths(step, ends, run)

    @pl.when(step == NQ - 1)
    def _():
        for pair in range(2):
            cols = slice(HALF + pair * 128, HALF + (pair + 1) * 128)
            grads_ref[:, cols] = (dk_ref[pair] * KSCALE).astype(BF)
            cols = slice(2 * HALF + pair * 128, 2 * HALF + (pair + 1) * 128)
            grads_ref[:, cols] = dv_ref[pair].astype(BF)
        low = x_ref[...].astype(BF)
        dw_ref[...] = (tn(low, grads_ref[...]) + old_ref[...].astype(F32)).astype(BF)
        dx_ref[...] = base_ref[...] + nt(grads_ref[...], w_ref[...])


def attend_back(pieces, base, x, w, q, k, v, mixed, grad, p, old):
    whole = lambda i: (0, 0)
    return pl.pallas_call(
        attend_back_kernel,
        grid=(NQ,),
        in_specs=[
            pl.BlockSpec(memory_space=pltpu.SMEM),
            pl.BlockSpec((LEN, D), whole),
            pl.BlockSpec((LEN, D), whole),
            pl.BlockSpec((D, 3 * HALF), whole),
            pl.BlockSpec((LEN, HALF), whole),
            pl.BlockSpec((LEN, HALF), whole),
            pl.BlockSpec((LEN, HALF), whole),
            pl.BlockSpec((LEN, HALF), whole),
            pl.BlockSpec((LEN, HALF), whole),
            pl.BlockSpec((1, 2, LEN, 256), lambda i: (i, 0, 0, 0)),
            pl.BlockSpec((D, 3 * HALF), whole),
        ],
        out_specs=[pl.BlockSpec((LEN, D), whole), pl.BlockSpec((D, 3 * HALF), whole)],
        out_shape=[jax.ShapeDtypeStruct((LEN, D), F32), jax.ShapeDtypeStruct((D, 3 * HALF), BF)],
        scratch_shapes=[
            pltpu.VMEM((2, LEN, 128), F32),
            pltpu.VMEM((2, LEN, 128), F32),
            pltpu.VMEM((LEN, 3 * HALF), BF),
            pltpu.VMEM((2, 128, LEN), BF),
        ],
        compiler_params=pltpu.CompilerParams(vmem_limit_bytes=VMEM_LIMIT),
    )(pieces, base, x, w, q, k, v, mixed, grad, p, old)


TM = 256


def unit_rows(values):
    center = values - jnp.mean(values, axis=-1, keepdims=True)
    spread = jnp.mean(center * center, axis=-1, keepdims=True)
    inv = lax.rsqrt(spread + EPS)
    return center * inv, inv


def feed_kernel(x_ref, ma_ref, mb_ref, wo_ref, wh_ref, wd_ref, par_ref, out_ref, unit1_ref, inv1_ref,
                norm_ref, act_ref, slope_ref, unit2_ref, inv2_ref):
    summed = x_ref[...] + nt(ma_ref[...], wo_ref[:, :HALF]) + nt(mb_ref[...], wo_ref[:, HALF:])
    unit, inv = unit_rows(summed)
    unit1_ref[...] = unit.astype(BF)
    inv1_ref[...] = inv
    normed = unit * par_ref[0:1, :] + par_ref[1:2, :]
    low = normed.astype(BF)
    norm_ref[...] = low
    for at in range(0, FF, 512):
        cols = slice(at, at + 512)
        hidden = nn(low, wh_ref[:, cols])
        square = hidden * hidden
        gate = 0.5 + 0.5 * jnp.tanh(hidden * (C1 + C2 * square))
        act_ref[:, cols] = (hidden * gate).astype(BF)
        slope_ref[:, cols] = (gate + gate * (1.0 - gate) * hidden * (2 * C1 + 6 * C2 * square)).astype(BF)
    total = normed + nt(act_ref[...], wd_ref[...])
    unit, inv = unit_rows(total)
    unit2_ref[...] = unit.astype(BF)
    inv2_ref[...] = inv
    out_ref[...] = unit * par_ref[2:3, :] + par_ref[3:4, :]


def feed(x, ma, mb, wo, wh, wd, par):
    whole = lambda i: (0, 0)
    block = lambda i: (i, 0)
    wide = [(D, F32), (D, BF), (1, F32), (D, BF), (FF, BF), (FF, BF), (D, BF), (1, F32)]
    return pl.pallas_call(
        feed_kernel,
        grid=(LEN // TM,),
        in_specs=[
            pl.BlockSpec((TM, D), block),
            pl.BlockSpec((TM, HALF), block),
            pl.BlockSpec((TM, HALF), block),
            pl.BlockSpec((D, D), whole),
            pl.BlockSpec((D, FF), whole),
            pl.BlockSpec((D, FF), whole),
            pl.BlockSpec((8, D), whole),
        ],
        out_specs=[pl.BlockSpec((TM, w), block) for w, _ in wide],
        out_shape=[jax.ShapeDtypeStruct((LEN, w), t) for w, t in wide],
        compiler_params=pltpu.CompilerParams(vmem_limit_bytes=VMEM_LIMIT),
    )(x, ma, mb, wo, wh, wd, par)


def unit_back(grad, unit, inv, gain):
    scaled = grad * gain
    first = jnp.mean(scaled, axis=-1, keepdims=True)
    second = jnp.mean(scaled * unit, axis=-1, keepdims=True)
    return inv * (scaled - first - unit * second)


def fold_rows(values):
    return jnp.sum(values.reshape(-1, 8, values.shape[-1]), axis=0)


def feed_back_kernel(grad_ref, unit1_ref, inv1_ref, norm_ref, act_ref, slope_ref, unit2_ref, inv2_ref,
                     ma_ref, mb_ref, ia_ref, ib_ref, wo_ref, wh_ref, wd_ref, par_ref,
                     old_d_ref, old_h_ref, old_o_ref,
                     base_ref, ga_ref, gb_ref, dd_ref, dh_ref, do_ref, small_ref,
                     acc_d_ref, acc_h_ref, acc_o_ref):
    step = pl.program_id(0)

    @pl.when(step == 0)
    def _():
        acc_d_ref[...] = old_d_ref[...].astype(F32)
        acc_h_ref[...] = old_h_ref[...].astype(F32)
        acc_o_ref[...] = old_o_ref[...].astype(F32)
        small_ref[...] = jnp.zeros_like(small_ref)

    grad = grad_ref[...]
    unit2 = unit2_ref[...].astype(F32)
    small_ref[16:24, :] += fold_rows(grad * unit2)
    small_ref[24:32, :] += fold_rows(grad)
    total = unit_back(grad, unit2, inv2_ref[...], par_ref[2:3, :])
    low = total.astype(BF)
    normed = total
    for at in range(0, FF, 512):
        cols = slice(at, at + 512)
        acc_d_ref[:, cols] += tn(low, act_ref[:, cols])
        hidden = (nn(low, wd_ref[:, cols]) * slope_ref[:, cols].astype(F32)).astype(BF)
        acc_h_ref[:, cols] += tn(norm_ref[...], hidden)
        normed = normed + nt(hidden, wh_ref[:, cols])
    unit1 = unit1_ref[...].astype(F32)
    small_ref[0:8, :] += fold_rows(normed * unit1)
    small_ref[8:16, :] += fold_rows(normed)
    summed = unit_back(normed, unit1, inv1_ref[...], par_ref[0:1, :])
    base_ref[...] = summed
    low = summed.astype(BF)
    acc_o_ref[:, :HALF] += tn(low, ma_ref[...])
    acc_o_ref[:, HALF:] += tn(low, mb_ref[...])
    ga_ref[...] = (nn(low, wo_ref[:, :HALF]) * ia_ref[...]).astype(BF)
    gb_ref[...] = (nn(low, wo_ref[:, HALF:]) * ib_ref[...]).astype(BF)

    @pl.when(step == LEN // TM - 1)
    def _():
        dd_ref[...] = acc_d_ref[...].astype(BF)
        dh_ref[...] = acc_h_ref[...].astype(BF)
        do_ref[...] = acc_o_ref[...].astype(BF)


def feed_back(grad, saved, ma, mb, ia, ib, wo, wh, wd, par, old):
    whole = lambda i: (0, 0)
    block = lambda i: (i, 0)
    ins = [(D, F32), (D, BF), (1, F32), (D, BF), (FF, BF), (FF, BF), (D, BF), (1, F32),
           (HALF, BF), (HALF, BF), (HALF, F32), (HALF, F32)]
    big = [pl.BlockSpec((D, FF), whole), pl.BlockSpec((D, FF), whole), pl.BlockSpec((D, D), whole)]
    return pl.pallas_call(
        feed_back_kernel,
        grid=(LEN // TM,),
        in_specs=[pl.BlockSpec((TM, w), block) for w, _ in ins]
        + [pl.BlockSpec((D, D), whole), pl.BlockSpec((D, FF), whole), pl.BlockSpec((D, FF), whole),
           pl.BlockSpec((8, D), whole)] + big,
        out_specs=[pl.BlockSpec((TM, D), block), pl.BlockSpec((TM, HALF), block), pl.BlockSpec((TM, HALF), block)]
        + big + [pl.BlockSpec((32, D), whole)],
        out_shape=[
            jax.ShapeDtypeStruct((LEN, D), F32),
            jax.ShapeDtypeStruct((LEN, HALF), BF),
            jax.ShapeDtypeStruct((LEN, HALF), BF),
            jax.ShapeDtypeStruct((D, FF), BF),
            jax.ShapeDtypeStruct((D, FF), BF),
            jax.ShapeDtypeStruct((D, D), BF),
            jax.ShapeDtypeStruct((32, D), F32),
        ],
        scratch_shapes=[pltpu.VMEM((D, FF), F32), pltpu.VMEM((D, FF), F32), pltpu.VMEM((D, D), F32)],
        compiler_params=pltpu.CompilerParams(vmem_limit_bytes=VMEM_LIMIT),
    )(grad, *saved, ma, mb, ia, ib, wo, wh, wd, par, *old)


GROUP = ("dp", "tensor")
FIRST = 3 * HALF + 128
REST = HALF + FF


def plan(dp):
    if dp == 16:
        return (8, 4, 1, 2), (8, 4, 2, 1)
    bits = [1 << i for i in range(dp.bit_length() - 1)]
    side = len(bits) // 3
    x, y, z = bits[:side], bits[side:2 * side], bits[2 * side:]
    return tuple(z[::-1] + x[::-1] + y[::-1]), tuple(z[::-1] + y[::-1] + x[::-1])


def flip(value, dp, masks):
    pairs = [(d * 2 + t, (d ^ masks[t]) * 2 + t) for d in range(dp) for t in range(2)]
    return lax.ppermute(value, GROUP, pairs)


def swap(value):
    return lax.ppermute(value, "tensor", [(0, 1), (1, 0)])


def gather(own, dp):
    held = own[None]
    for masks in zip(*plan(dp)):
        held = jnp.concatenate([held, flip(held, dp, masks)], axis=0)
    return held


def places(dp, mine, tensor, last_first):
    rel = jnp.arange(dp, dtype=jnp.int32) ^ mine
    found = []
    for order in plan(dp):
        at = jnp.zeros((dp,), jnp.int32)
        for i, mask in enumerate(order):
            bit = (rel & mask) // mask
            at = at + bit * (1 << (i if not last_first else i))
        found.append(at)
    return jnp.where(tensor == 0, found[0], found[1])


def order_kernel(dp, spans, at_ref, own_ref, other_ref, *refs):
    outs, sem = refs[:-1], refs[-1]
    copies = []
    rows = D // dp
    for b in range(dp):
        for half, ref in enumerate((own_ref, other_ref)):
            for out, (out_half, begin, width, to) in zip([outs[s[0]] for s in spans], [s[1:] for s in spans]):
                if out_half != half:
                    continue
                copies.append(pltpu.make_async_copy(
                    ref.at[at_ref[half, b], :, pl.ds(begin, width)],
                    out.at[pl.ds(b * rows, rows), pl.ds(to, width)], sem.at[len(copies)]))
    for c in copies:
        c.start()
    for c in copies:
        c.wait()


def order(at, own, other, spans, widths):
    dp = own.shape[0]
    return pl.pallas_call(
        functools.partial(order_kernel, dp, spans),
        in_specs=[pl.BlockSpec(memory_space=pltpu.SMEM), pl.BlockSpec(memory_space=pl.ANY),
                  pl.BlockSpec(memory_space=pl.ANY)],
        out_specs=[pl.BlockSpec(memory_space=pl.ANY)] * len(widths),
        out_shape=[jax.ShapeDtypeStruct((D, w), BF) for w in widths],
        scratch_shapes=[pltpu.SemaphoreType.DMA((dp * len(spans),))],
    )(at, own, other)


def reduce(keep, send, dp):
    held = add(keep, swap(send))
    phases = list(zip(*plan(dp)))[::-1]
    for i, masks in enumerate(phases):
        half = held.shape[0] // 2
        arrived = flip(held[half:], dp, masks)
        held = add(held[:half], arrived, F32 if i == len(phases) - 1 else BF)
    return held[0]


def add(a, b, kind=BF):
    return (a.astype(F32) + b.astype(F32)).astype(kind)


def body(embedded, piece_lengths, pair_tags, pair_embedding, w_query, w_key, w_value, w_output, w_hidden,
         w_down, first_gain, first_shift, second_gain, second_shift, cotangent):
    dp = lax.axis_size("dp")
    mine, tensor = lax.axis_index("dp"), lax.axis_index("tensor")
    rows = D // dp
    pieces = lax.dynamic_index_in_dim(piece_lengths, tensor, 0, keepdims=False)
    tag = lax.dynamic_index_in_dim(pair_tags, tensor, 0, keepdims=False)
    small = jnp.stack([first_gain, first_shift, second_gain, second_shift], axis=1)
    small = jnp.concatenate([small, pair_embedding.T, jnp.zeros((rows, 120), BF)], axis=1)
    first = gather(jnp.concatenate([w_query, w_key, w_value, small], axis=1), dp)
    rest = gather(jnp.concatenate([w_output.T, w_hidden, w_down.T], axis=1), dp)
    at = jnp.stack([places(dp, mine, tensor, False), places(dp, mine, 1 - tensor, False)])
    wa, wb, small = order(at, first, swap(first),
                          ((0, 0, 0, 3 * HALF, 0), (1, 1, 0, 3 * HALF, 0), (2, 0, 3 * HALF, 128, 0)),
                          (3 * HALF, 3 * HALF, 128))
    wo, wh, wd = order(at, rest, swap(rest),
                       ((0, 0, 0, HALF, 0), (0, 1, 0, HALF, HALF),
                        (1, 0, HALF, FF // 2, 0), (1, 1, HALF, FF // 2, FF // 2),
                        (2, 0, HALF + FF // 2, FF // 2, 0), (2, 1, HALF + FF // 2, FF // 2, FF // 2)),
                       (D, FF, FF))
    par = small[:, :8].T.astype(F32)
    tags = jnp.arange(PAIRS, dtype=jnp.int32) == tag
    start = embedded + jnp.sum(jnp.where(tags[:, None], par[4:], 0.0), axis=0)[None]

    def forward(x):
        qa, ka, va, ma, ea, ia, pa = attend(pieces, x, wa)
        qb, kb, vb, mb, eb, ib, pb = attend(pieces, x, wb)
        out, *saved = feed(x, ma, mb, wo, wh, wd, par)
        return out, (x, (qa, ka, va), (qb, kb, vb), (ma, mb), (ea, eb), (ia, ib), (pa, pb), saved)

    def backward(grad, kept, old):
        x, ha, hb, mixed, exact, inv, probs, saved = kept
        base, ga, gb, dd, dh, do, stats = feed_back(grad, saved, *mixed, *inv, wo, wh, wd, par, old[:3])
        base, da = attend_back(pieces, base, x, wa, *ha, exact[0], ga, probs[0], old[3])
        base, db = attend_back(pieces, base, x, wb, *hb, exact[1], gb, probs[1], old[4])
        return base, (dd, dh, do, da, db), stats

    hidden, kept_first = forward(start)
    result, kept_second = forward(hidden)
    valid = jnp.arange(LEN, dtype=jnp.int32)[:, None] < jnp.sum(pieces[:-1])
    zeros = lambda n: jnp.zeros((D, n), BF)
    old = (zeros(FF), zeros(FF), zeros(D), zeros(3 * HALF), zeros(3 * HALF))
    grad, old, stats_second = backward(jnp.where(valid, cotangent, 0.0), kept_second, old)
    grad, new, stats_first = backward(grad, kept_first, old)
    dd, dh, do, da, db = new
    stats = (stats_first + stats_second).reshape(4, 8, D).sum(axis=1)
    table = jnp.where(tags[:, None], jnp.sum(grad, axis=0)[None], 0.0)
    stats = jnp.concatenate([stats, table], axis=0).T.astype(BF)
    stats = jnp.concatenate([stats, jnp.zeros((D, 120), BF)], axis=1)

    def blocks(value, partner):
        to = places(dp, mine, 1 - tensor if partner else tensor, True)
        back = jnp.zeros((dp,), jnp.int32).at[to].set(jnp.arange(dp, dtype=jnp.int32))
        return value.reshape(dp, rows, -1)[back]

    half = FF // 2
    keep = jnp.concatenate([do[:, :HALF], dh[:, :half], dd[:, :half]], axis=1)
    send = jnp.concatenate([do[:, HALF:], dh[:, half:], dd[:, half:]], axis=1)
    total = reduce(blocks(keep, False), blocks(send, True), dp)
    do, dh, dd = total[:, :HALF], total[:, HALF:HALF + half], total[:, HALF + half:]
    total = reduce(blocks(jnp.concatenate([da, stats], axis=1), False),
                   blocks(jnp.concatenate([db, stats], axis=1), True), dp)
    small = total[:, 3 * HALF:3 * HALF + 8].T
    return (result, grad, small[4:], total[:, :HALF], total[:, HALF:2 * HALF], total[:, 2 * HALF:3 * HALF],
            do.T, dh, dd.T, small[0], small[1], small[2], small[3])


def solution(mesh):
    both = P(GROUP, None)
    params = (P("dp", "tensor"),) * 3 + (P("tensor", "dp"), P("dp", "tensor"), P("tensor", "dp"))
    in_specs = (both, P("dp", None), P("dp"), P(None, "dp")) + params + (P("dp"),) * 4 + (both,)
    out_specs = (both, both, P(None, "dp")) + params + (P("dp"),) * 4
    return jax.shard_map(body, mesh=mesh, in_specs=in_specs, out_specs=out_specs, check_vma=False)
```

time: 1200 us -> 571 us (0.48)
  Pallas kernels: 0 us -> 416 us
  matrix products: 337 us -> 0 us
  blocking collectives: 237 us -> 0 us
  waiting for transfers between devices: 239 us -> 58.8 us
  local copies, waits for them, and re-layouts: 175 us -> 35.9 us
  other arithmetic: 115 us -> 27.4 us
  loops' own time: 27.7 us -> 0 us
  starting transfers between devices: 46 us -> 23.4 us
  between operations: 18 us -> 1.55 us
    pallas_call x0 -> x14, Pallas kernels: none -> 416 us  [the longest x2 199 us: order(): pl.pallas_call(functools.partial(order_kernel, dp, spans), in_specs=[pl.B...]
    dot_general x82 -> x0, matrix products: 337 us -> none  [the longest x16 50.5 us: block_scores(): jnp.einsum('qhd,khd->hqk', query_block, key_seq, preferred_element_type=j...]
    all_gather x5 -> x0, blocking collectives: 197 us -> none  [the longest x1 42.4 us: body(): lax.all_gather(pair_embedding, 'dp', axis=1, tiled=True)]
    all_gather x10 -> x0, waiting for transfers between devices: 129 us -> none  [the longest x1 49.1 us: body(): lax.all_gather(w_down, 'dp', axis=1, tiled=True)]
    ppermute x0 -> x20, waiting for transfers between devices: none -> 58.8 us  [the longest x16 58.8 us: flip(): return lax.ppermute(value, GROUP, pairs)]
    all_to_all x9 -> x0, waiting for transfers between devices: 55.9 us -> none  [summed_on_arrival(): lax.all_to_all(blocks, axis, split_axis=0, concat_axis=0, tiled=True)]
    reduce_scatter x8 -> x0, waiting for transfers between devices: 52.6 us -> none  [the longest x4 26.9 us: collect(): lax.psum_scatter(part.astype(jnp.bfloat16), 'tensor', scatter_dimension=0...]
    reduce_sum x35 -> x4, other arithmetic: 52 us -> 2.66 us  [the longest x1 1.91 us: body(): table = jnp.where(tags[:, None], jnp.sum(grad, axis=0)[None], 0.0)]
  transfers between devices with their start and end apart: 27 -> 20, of which waited for: 22 -> 12; matrix products, arithmetic and copies ran while one was open for 18% -> 9% of each run, Pallas kernels for 0% -> 22%
where the time goes in v1:
time: 571 us; the launch traced here: 563 us
  Pallas kernels  416 us (73%)
  waiting for transfers between devices  58.8 us (10%)
  local copies, waits for them, and re-layouts  35.9 us (6%)
  other arithmetic  27.4 us (5%)
  starting transfers between devices  23.4 us (4%)
    pallas_call x2, Pallas kernels, order(): pl.pallas_call(functools.partial(order_kernel, dp, spans), in_specs=[pl.B...  199 us
    pallas_call x4, Pallas kernels, attend_back(): pl.pallas_call(attend_back_kernel, grid=(NQ,), in_specs=[pl.BlockSpec(mem...  67.9 us
    pallas_call x4, Pallas kernels, attend(): pl.pallas_call(attend_kernel, grid=(NQ,), in_specs=[pl.BlockSpec(memory_s...  67.7 us
    ppermute x16, waiting for transfers between devices, flip(): return lax.ppermute(value, GROUP, pairs)  58.8 us
    pallas_call x2, Pallas kernels, feed_back(): pl.pallas_call(feed_back_kernel, grid=(LEN // TM,), in_specs=[pl.BlockSpe...  50.7 us
    pallas_call x2, Pallas kernels, feed(): pl.pallas_call(feed_kernel, grid=(LEN // TM,), in_specs=[pl.BlockSpec((TM...  29.9 us
    ppermute x16, starting transfers between devices, flip(): return lax.ppermute(value, GROUP, pairs)  23.1 us
  transfers between devices with their start and end apart: 20, of which 12 were waited for; matrix products, arithmetic and copies ran while one was open for 9% of the time, Pallas kernels for 22%

profile of v1, /device:TPU:0, one launch (start us, length us, event | category | flops | bytes accessed | tf_op | source)
XLA Modules:
  0.0 562.7 jit_solution(11865116310342758602)
XLA Ops:
  1.6 4.1 collective-permute-start.5
  12.7 2.0 collective-permute-start.6
  16.2 5.5 collective-permute-done.6
  28.1 4.6 collective-permute-done.7
  36.9 7.0 %collective-permute-done.2 = bf16[4,32,896]{2,1,0:T(8,128)(2,1)S(1)} collective-permute-done((bf16[4,32,896]{2,1,0:T(8,128)(2,1)S(1)}, bf16[4,32,896]{2,1,0:T(8,128)(2,1)S(1)}, u32[]{:S(2)}, u32[]{:S(2)}) %collective-permute-start.2) | collective-permute-done | bytes 229408 | tf_op jit(solution)/shard_map/ppermute | solution.py:422
  45.5 5.4 collective-permute-done.8
  59.3 3.2 broadcast_select_fusion.grad_ref
  63.4 53.9 %shard_map.246 = (bf16[512,768]{1,0:T(8,128)(2,1)}, bf16[512,768]{1,0:T(8,128)(2,1)}, bf16[512,128]{1,0:T(8,128)(2,1)}) custom-call(s32[2,16]{1,0:T(2,128)} %pad_add_fusion.at_ref, bf16[16,32,896]{2,1,0:T(8,128)(2,1)} %constant_dynamic-update-slice_fusion.own_ref, bf16[16,32,896]{2,1,0:T(8,128)(2,1)} %copy-done.5), custom_call_target="tpu_custom_call" | custom-call | tf_op jit(solution)/shard_map/pallas_call | solution.py:468
  118.4 3.1 broadcast_add_fusion.x_ref
  121.5 16.6 %shard_map.247 = (bf16[1024,256]{1,0:T(8,128)(2,1)}, bf16[1024,256]{1,0:T(8,128)(2,1)}, bf16[1024,256]{1,0:T(8,128)(2,1)}, bf16[1024,256]{1,0:T(8,128)(2,1)}, f3...) custom-call(s32[8]{0:T(128)} %fusion.15.pieces_ref, ...), custom_call_target="tpu_custom_call" | custom-call | tf_op jit(solution)/shard_map/pallas_call | solution.py:151
  138.2 17.2 %shard_map.248 = (bf16[1024,256]{1,0:T(8,128)(2,1)}, bf16[1024,256]{1,0:T(8,128)(2,1)}, bf16[1024,256]{1,0:T(8,128)(2,1)}, bf16[1024,256]{1,0:T(8,128)(2,1)}, f3...) custom-call(s32[8]{0:T(128)} %fusion.15.pieces_ref, ...), custom_call_target="tpu_custom_call" | custom-call | tf_op jit(solution)/shard_map/pallas_call | solution.py:151
  155.4 145.6 %shard_map.249 = (bf16[512,512]{1,0:T(8,128)(2,1)}, bf16[512,2048]{1,0:T(8,128)(2,1)}, bf16[512,2048]{1,0:T(8,128)(2,1)}) custom-call(s32[2,16]{1,0:T(2,128)} %pad_add_fusion.at_ref, bf16[16,32,2304]{2,1,0:T(8,128)(2,1)} %copy-done.3, bf16[16,32,2304]{2,1,0:T(8,128)(2,1)} %collective-permute-done.9.other_ref), custom_call_target="tpu_custom_call" | custom-call | tf_op jit(solution)/shard_map/pallas_call | solution.py:468
  301.0 15.0 %shard_map.250 = (f32[1024,512]{1,0:T(8,128)}, bf16[1024,512]{1,0:T(8,128)(2,1)}, f32[1024,1]{1,0:T(8,128)}, bf16[1024,512]{1,0:T(8,128)(2,1)}, bf16[1024,2048]{...) custom-call(f32[1024,512]{1,0:T(8,128)} %broadcast_add_fusion.x_ref, ...), custom_call_target="tpu_custom_call" | custom-call | tf_op jit(solution)/shard_map/pallas_call | solution.py:304
  316.0 16.9 %shard_map.251 = (bf16[1024,256]{1,0:T(8,128)(2,1)}, bf16[1024,256]{1,0:T(8,128)(2,1)}, bf16[1024,256]{1,0:T(8,128)(2,1)}, bf16[1024,256]{1,0:T(8,128)(2,1)}, f3...) custom-call(s32[8]{0:T(128)} %fusion.15.pieces_ref, ...), custom_call_target="tpu_custom_call" | custom-call | tf_op jit(solution)/shard_map/pallas_call | solution.py:151
  332.9 16.9 %shard_map.252 = (bf16[1024,256]{1,0:T(8,128)(2,1)}, bf16[1024,256]{1,0:T(8,128)(2,1)}, bf16[1024,256]{1,0:T(8,128)(2,1)}, bf16[1024,256]{1,0:T(8,128)(2,1)}, f3...) custom-call(s32[8]{0:T(128)} %fusion.15.pieces_ref, ...), custom_call_target="tpu_custom_call" | custom-call | tf_op jit(solution)/shard_map/pallas_call | solution.py:151
  349.8 14.9 %shard_map.253 = (f32[1024,512]{1,0:T(8,128)}, bf16[1024,512]{1,0:T(8,128)(2,1)}, f32[1024,1]{1,0:T(8,128)}, bf16[1024,512]{1,0:T(8,128)(2,1)}, bf16[1024,2048]{...) custom-call(f32[1024,512]{1,0:T(8,128)} %get-tuple-element.93.x_ref, ...), custom_call_target="tpu_custom_call" | custom-call | tf_op jit(solution)/shard_map/pallas_call | solution.py:304
  367.1 25.9 %shard_map.254 = (f32[1024,512]{1,0:T(8,128)}, bf16[1024,256]{1,0:T(8,128)(2,1)}, bf16[1024,256]{1,0:T(8,128)(2,1)}, bf16[512,2048]{1,0:T(8,128)(2,1)}, bf16[512...) custom-call(f32[1024,512]{1,0:T(8,128)} %broadcast_select_fusion.grad_ref, ...), custom_call_target="tpu_custom_call" | custom-call | tf_op jit(solution)/shard_map/pallas_call | solution.py:384
  394.0 16.8 %shard_map.255 = (f32[1024,512]{1,0:T(8,128)}, bf16[512,768]{1,0:T(8,128)(2,1)}) custom-call(s32[8]{0:T(128)} %fusion.15.pieces_ref, f32[1024,512]{1,0:T(8,128)} %get-tuple-element.106.base_ref, f32[1024,512]{1,0:T(8,128)} %get-tuple-element.93.x_ref, bf16[512,768]{1,0:T(8,128)(2,1)} %get-tuple-element.86.w_ref, bf16[1024,256]{1,0:T(8,128)(2,1)} %get-tuple-element.107.q_ref, ...), custom_call_target="tpu_custom_call" | custom-call | tf_op jit(solution)/shard_map/pallas_call | solution.py:239
  410.8 17.1 %shard_map.256 = (f32[1024,512]{1,0:T(8,128)}, bf16[512,768]{1,0:T(8,128)(2,1)}) custom-call(s32[8]{0:T(128)} %fusion.15.pieces_ref, f32[1024,512]{1,0:T(8,128)} %get-tuple-element.113.base_ref, f32[1024,512]{1,0:T(8,128)} %get-tuple-element.93.x_ref, bf16[512,768]{1,0:T(8,128)(2,1)} %get-tuple-element.88.w_ref, bf16[1024,256]{1,0:T(8,128)(2,1)} %get-tuple-element.114.q_ref, ...), custom_call_target="tpu_custom_call" | custom-call | tf_op jit(solution)/shard_map/pallas_call | solution.py:239
  427.9 24.8 %shard_map.257 = (f32[1024,512]{1,0:T(8,128)}, bf16[1024,256]{1,0:T(8,128)(2,1)}, bf16[1024,256]{1,0:T(8,128)(2,1)}, bf16[512,2048]{1,0:T(8,128)(2,1)}, bf16[512...) custom-call(f32[1024,512]{1,0:T(8,128)} %get-tuple-element.120.grad_ref, ...), custom_call_target="tpu_custom_call" | custom-call | tf_op jit(solution)/shard_map/pallas_call | solution.py:384
  457.0 2.1 gather_fusion.3
  459.8 16.9 %shard_map.258 = (f32[1024,512]{1,0:T(8,128)}, bf16[512,768]{1,0:T(8,128)(2,1)}) custom-call(s32[8]{0:T(128)} %fusion.15.pieces_ref, f32[1024,512]{1,0:T(8,128)} %get-tuple-element.133.base_ref, f32[1024,512]{1,0:T(8,128)} %broadcast_add_fusion.x_ref, bf16[512,768]{1,0:T(8,128)(2,1)} %get-tuple-element.86.w_ref, bf16[1024,256]{1,0:T(8,128)(2,1)} %get-tuple-element.134.q_ref, ...), custom_call_target="tpu_custom_call" | custom-call | tf_op jit(solution)/shard_map/pallas_call | solution.py:239
  476.7 17.1 %shard_map.259 = (f32[1024,512]{1,0:T(8,128)}, bf16[512,768]{1,0:T(8,128)(2,1)}) custom-call(s32[8]{0:T(128)} %fusion.15.pieces_ref, f32[1024,512]{1,0:T(8,128)} %get-tuple-element.141.base_ref, f32[1024,512]{1,0:T(8,128)} %broadcast_add_fusion.x_ref, bf16[512,768]{1,0:T(8,128)(2,1)} %get-tuple-element.88.w_ref, bf16[1024,256]{1,0:T(8,128)(2,1)} %get-tuple-element.142.q_ref, ...), custom_call_target="tpu_custom_call" | custom-call | tf_op jit(solution)/shard_map/pallas_call | solution.py:239
  496.7 2.2 fusion
  502.1 2.1 gather_fusion.2
  504.3 3.0 add_convert_fusion
  513.8 15.9 %collective-permute-done.11 = bf16[8,32,896]{2,1,0:T(8,128)(2,1)S(1)} collective-permute-done((bf16[8,32,896]{2,1,0:T(8,128)(2,1)S(1)}, bf16[8,32,896]{2,1,0:T(8,128)(2,1)S(1)}, u32[]{:S(2)}, u32[]{:S(2)}) %collective-permute-start.11) | collective-permute-done | bytes 458784 | tf_op jit(solution)/shard_map/ppermute | solution.py:422
  533.7 2.3 collective-permute-done.12
  536.9 3.9 collective-permute-done.13
  540.9 5.4 collective-permute-start.14
  549.2 5.1 collective-permute-done.18
  556.1 4.8 collective-permute-done.19
  (143 shorter events, 63.8 us)
Async XLA Ops:
  0.6 24.9 %copy-start = (s32[2,8]{1,0:T(2,128)S(1)}, s32[2,8]{1,0:T(2,128)}, u32[]{:S(2)}) copy-start(s32[2,8]{1,0:T(2,128)} %param.16) | copy-start | bytes 196
  1.6 11.1 %collective-permute-start.5 = (bf16[1,32,2304]{2,1,0:T(8,128)(2,1)S(1)}, bf16[1,32,2304]{2,1,0:T(8,128)(2,1)S(1)}, u32[]{:S(2)}, u32[]{:S(2)}) collective-permute-start(bf16[1,32,2304]{2,1,0:T(8,128)(2,1)S(1)} %maximum_bitcast_fusion), channel_id=1, source_target_pairs={{0,16},{1,17},{2,18},{3,19},{4,20},{5,21},{6,22},{7,23},{8,24},{9,... | collective-permute-start | bytes 442376 | tf_op jit(solution)/shard_map/ppermute | solution.py:422
  10.9 15.2 %collective-permute-start = (bf16[1,32,896]{2,1,0:T(8,128)(2,1)}, bf16[1,32,896]{2,1,0:T(8,128)(2,1)}, u32[]{:S(2)}, u32[]{:S(2)}) collective-permute-start(bf16[1,32,896]{2,1,0:T(8,128)(2,1)} %bitcast.6), channel_id=1, source_target_pairs={{0,16},{1,17},{2,18},{3,19},{4,20},{5,21},{6,22},{7,23},{8,24},{9,... | collective-permute-start | bytes 172040 | tf_op jit(solution)/shard_map/ppermute | solution.py:422
  12.7 9.1 %collective-permute-start.6 = (bf16[2,32,2304]{2,1,0:T(8,128)(2,1)S(1)}, bf16[2,32,2304]{2,1,0:T(8,128)(2,1)S(1)}, u32[]{:S(2)}, u32[]{:S(2)}) collective-permute-start(bf16[2,32,2304]{2,1,0:T(8,128)(2,1)S(1)} %pad_maximum_fusion.7), channel_id=1, source_target_pairs={{0,8},{1,9},{2,10},{3,11},{4,12},{5,13},{6,14},{7,15},{8,0},{9,1},... | collective-permute-start | bytes 884744 | tf_op jit(solution)/shard_map/ppermute | solution.py:422
  22.6 10.1 %collective-permute-start.7 = (bf16[4,32,2304]{2,1,0:T(8,128)(2,1)}, bf16[4,32,2304]{2,1,0:T(8,128)(2,1)S(1)}, u32[]{:S(2)}, u32[]{:S(2)}) collective-permute-start(bf16[4,32,2304]{2,1,0:T(8,128)(2,1)} %pad_maximum_fusion.5), channel_id=1, source_target_pairs={{0,2},{1,5},{2,0},{3,7},{4,6},{5,1},{6,4},{7,3},{8,10},{9,13},{10,... | collective-permute-start | bytes 1769480 | tf_op jit(solution)/shard_map/ppermute | solution.py:422
  26.9 7.5 %collective-permute-start.1 = (bf16[2,32,896]{2,1,0:T(8,128)(2,1)S(1)}, bf16[2,32,896]{2,1,0:T(8,128)(2,1)S(1)}, u32[]{:S(2)}, u32[]{:S(2)}) collective-permute-start(bf16[2,32,896]{2,1,0:T(8,128)(2,1)S(1)} %pad_maximum_fusion.9), channel_id=1, source_target_pairs={{0,8},{1,9},{2,10},{3,11},{4,12},{5,13},{6,14},{7,15},{8,0},{9,1},... | collective-permute-start | bytes 344072 | tf_op jit(solution)/shard_map/ppermute | solution.py:422
  32.8 18.0 %collective-permute-start.8 = (bf16[8,32,2304]{2,1,0:T(8,128)(2,1)S(1)}, bf16[8,32,2304]{2,1,0:T(8,128)(2,1)S(1)}, u32[]{:S(2)}, u32[]{:S(2)}) collective-permute-start(bf16[8,32,2304]{2,1,0:T(8,128)(2,1)S(1)} %pad_maximum_fusion.4), channel_id=1, source_target_pairs={{0,4},{1,3},{2,6},{3,1},{4,0},{5,7},{6,2},{7,5},{8,12},{9,11},{10,... | collective-permute-start | bytes 3538952 | tf_op jit(solution)/shard_map/ppermute | solution.py:422
  35.3 8.6 %collective-permute-start.2 = (bf16[4,32,896]{2,1,0:T(8,128)(2,1)S(1)}, bf16[4,32,896]{2,1,0:T(8,128)(2,1)S(1)}, u32[]{:S(2)}, u32[]{:S(2)}) collective-permute-start(bf16[4,32,896]{2,1,0:T(8,128)(2,1)S(1)} %pad_maximum_fusion.8), channel_id=1, source_target_pairs={{0,2},{1,5},{2,0},{3,7},{4,6},{5,1},{6,4},{7,3},{8,10},{9,13},{10,... | collective-permute-start | bytes 688136 | tf_op jit(solution)/shard_map/ppermute | solution.py:422
  36.9 14.2 %copy-start.14 = (s32[2]{0:T(128)S(1)}, s32[2]{0:T(128)}, u32[]{:S(2)}) copy-start(s32[2]{0:T(128)} %param.17) | copy-start | bytes 28
  44.8 11.0 %collective-permute-start.3 = (bf16[8,32,896]{2,1,0:T(8,128)(2,1)S(1)}, bf16[8,32,896]{2,1,0:T(8,128)(2,1)S(1)}, u32[]{:S(2)}, u32[]{:S(2)}) collective-permute-start(bf16[8,32,896]{2,1,0:T(8,128)(2,1)S(1)} %pad_maximum_fusion.6), channel_id=1, source_target_pairs={{0,4},{1,3},{2,6},{3,1},{4,0},{5,7},{6,2},{7,5},{8,12},{9,11},{10,... | collective-permute-start | bytes 1376264 | tf_op jit(solution)/shard_map/ppermute | solution.py:422
  51.0 11.5 %copy-start.3 = (bf16[16,32,2304]{2,1,0:T(8,128)(2,1)}, bf16[16,32,2304]{2,1,0:T(8,128)(2,1)S(1)}, u32[]{:S(2)}) copy-start(bf16[16,32,2304]{2,1,0:T(8,128)(2,1)S(1)} %constant_dynamic-update-slice_fusion.5.own_ref) | copy-start | bytes 7077892
  51.0 104.4 %collective-permute-start.9 = (bf16[16,32,2304]{2,1,0:T(8,128)(2,1)S(1)}, bf16[16,32,2304]{2,1,0:T(8,128)(2,1)}, u32[]{:S(2)}, u32[]{:S(2)}) collective-permute-start(bf16[16,32,2304]{2,1,0:T(8,128)(2,1)S(1)} %constant_dynamic-update-slice_fusion.5.own_ref), channel_id=1, source_target_pairs={{0,1},{1,0},{2,3},{3,2},{4,5},{5,4},{6,7},{7,6},{8,9},{9,8},{10,11... | collective-permute-start | bytes 7077896 | tf_op jit(solution)/shard_map/ppermute | solution.py:426
  56.6 5.9 %collective-permute-start.4 = (bf16[16,32,896]{2,1,0:T(8,128)(2,1)}, bf16[16,32,896]{2,1,0:T(8,128)(2,1)S(1)}, u32[]{:S(2)}, u32[]{:S(2)}) collective-permute-start(bf16[16,32,896]{2,1,0:T(8,128)(2,1)} %constant_dynamic-update-slice_fusion.own_ref), channel_id=1, source_target_pairs={{0,1},{1,0},{2,3},{3,2},{4,5},{5,4},{6,7},{7,6},{8,9},{9,8},{10,11... | collective-permute-start | bytes 2752520 | tf_op jit(solution)/shard_map/ppermute | solution.py:426
  57.3 61.0 %copy-start.12 = (pred[4]{0:T(512)(128)(4,1)}, pred[4]{0:T(512)(128)(4,1)S(1)}, u32[]{:S(2)}) copy-start(pred[4]{0:T(512)(128)(4,1)S(1)} %iota_compare_fusion.1) | copy-start | bytes 16
  118.3 19.8 %copy-start.9 = (f32[8,512]{1,0:T(8,128)}, f32[8,512]{1,0:T(8,128)S(1)}, u32[]{:S(2)}) copy-start(f32[8,512]{1,0:T(8,128)S(1)} %convert_bitcast_fusion.par_ref) | copy-start | bytes 49156
  452.7 2.2 copy-start.4
  459.1 45.2 %collective-permute-start.15 = (bf16[16,32,2304]{2,1,0:T(8,128)(2,1)}, bf16[16,32,2304]{2,1,0:T(8,128)(2,1)}, u32[]{:S(2)}, u32[]{:S(2)}) collective-permute-start(bf16[16,32,2304]{2,1,0:T(8,128)(2,1)} %gather_fusion.3), channel_id=1, source_target_pairs={{0,1},{1,0},{2,3},{3,2},{4,5},{5,4},{6,7},{7,6},{8,9},{9,8},{10,11... | collective-permute-start | bytes 7077896 | tf_op jit(solution)/shard_map/ppermute | solution.py:426
  476.7 19.1 %copy-start.10 = (f32[32,512]{1,0:T(8,128)S(1)}, f32[32,512]{1,0:T(8,128)}, u32[]{:S(2)}) copy-start(f32[32,512]{1,0:T(8,128)} %get-tuple-element.152) | copy-start | bytes 196612
  476.7 19.1 %copy-start.11 = (f32[32,512]{1,0:T(8,128)S(1)}, f32[32,512]{1,0:T(8,128)}, u32[]{:S(2)}) copy-start(f32[32,512]{1,0:T(8,128)} %get-tuple-element.151) | copy-start | bytes 196612
  476.7 19.1 %copy-start.13 = (pred[4]{0:T(512)(128)(4,1)S(1)}, pred[4]{0:T(512)(128)(4,1)}, u32[]{:S(2)}) copy-start(pred[4]{0:T(512)(128)(4,1)} %copy-done.12) | copy-start | bytes 16
  493.9 2.9 copy-start.6
  493.9 2.9 copy-start.7
  500.5 9.9 %collective-permute-start.10 = (bf16[16,32,896]{2,1,0:T(8,128)(2,1)}, bf16[16,32,896]{2,1,0:T(8,128)(2,1)}, u32[]{:S(2)}, u32[]{:S(2)}) collective-permute-start(bf16[16,32,896]{2,1,0:T(8,128)(2,1)} %gather_fusion.1), channel_id=1, source_target_pairs={{0,1},{1,0},{2,3},{3,2},{4,5},{5,4},{6,7},{7,6},{8,9},{9,8},{10,11... | collective-permute-start | bytes 2752520 | tf_op jit(solution)/shard_map/ppermute | solution.py:426
  508.4 22.5 %collective-permute-start.16 = (bf16[8,32,2304]{2,1,0:T(8,128)(2,1)}, bf16[8,32,2304]{2,1,0:T(8,128)(2,1)}, u32[]{:S(2)}, u32[]{:S(2)}) collective-permute-start(bf16[8,32,2304]{2,1,0:T(8,128)(2,1)} %slice.173), channel_id=1, source_target_pairs={{0,4},{1,3},{2,6},{3,1},{4,0},{5,7},{6,2},{7,5},{8,12},{9,11},{10,... | collective-permute-start | bytes 3538952 | tf_op jit(solution)/shard_map/ppermute | solution.py:422
  512.2 17.5 %collective-permute-start.11 = (bf16[8,32,896]{2,1,0:T(8,128)(2,1)S(1)}, bf16[8,32,896]{2,1,0:T(8,128)(2,1)S(1)}, u32[]{:S(2)}, u32[]{:S(2)}) collective-permute-start(bf16[8,32,896]{2,1,0:T(8,128)(2,1)S(1)} %slice.160), channel_id=1, source_target_pairs={{0,4},{1,3},{2,6},{3,1},{4,0},{5,7},{6,2},{7,5},{8,12},{9,11},{10,... | collective-permute-start | bytes 1376264 | tf_op jit(solution)/shard_map/ppermute | solution.py:422
  529.8 6.1 %collective-permute-start.12 = (bf16[4,32,896]{2,1,0:T(8,128)(2,1)S(1)}, bf16[4,32,896]{2,1,0:T(8,128)(2,1)S(1)}, u32[]{:S(2)}, u32[]{:S(2)}) collective-permute-start(bf16[4,32,896]{2,1,0:T(8,128)(2,1)S(1)} %slice.162), channel_id=1, source_target_pairs={{0,2},{1,5},{2,0},{3,7},{4,6},{5,1},{6,4},{7,3},{8,10},{9,13},{10,... | collective-permute-start | bytes 688136 | tf_op jit(solution)/shard_map/ppermute | solution.py:422
  532.5 13.8 %collective-permute-start.17 = (bf16[4,32,2304]{2,1,0:T(8,128)(2,1)S(1)}, bf16[4,32,2304]{2,1,0:T(8,128)(2,1)S(1)}, u32[]{:S(2)}, u32[]{:S(2)}) collective-permute-start(bf16[4,32,2304]{2,1,0:T(8,128)(2,1)S(1)} %slice.175), channel_id=1, source_target_pairs={{0,2},{1,5},{2,0},{3,7},{4,6},{5,1},{6,4},{7,3},{8,10},{9,13},{10,... | collective-permute-start | bytes 1769480 | tf_op jit(solution)/shard_map/ppermute | solution.py:422
  536.0 4.9 collective-permute-start.13
  540.9 21.3 %copy-start.1 = (s32[2,8]{1,0:T(2,128)S(1)}, s32[2,8]{1,0:T(2,128)}, u32[]{:S(2)}) copy-start(s32[2,8]{1,0:T(2,128)} %param.16) | copy-start | bytes 196
  540.9 7.7 %collective-permute-start.14 = (bf16[1,32,896]{2,1,0:T(8,128)(2,1)S(1)}, bf16[1,32,896]{2,1,0:T(8,128)(2,1)S(1)}, u32[]{:S(2)}, u32[]{:S(2)}) collective-permute-start(bf16[1,32,896]{2,1,0:T(8,128)(2,1)S(1)} %slice.166), channel_id=1, source_target_pairs={{0,16},{1,17},{2,18},{3,19},{4,20},{5,21},{6,22},{7,23},{8,24},{9,... | collective-permute-start | bytes 172040 | tf_op jit(solution)/shard_map/ppermute | solution.py:422
  546.5 7.8 %collective-permute-start.18 = (bf16[2,32,2304]{2,1,0:T(8,128)(2,1)S(1)}, bf16[2,32,2304]{2,1,0:T(8,128)(2,1)S(1)}, u32[]{:S(2)}, u32[]{:S(2)}) collective-permute-start(bf16[2,32,2304]{2,1,0:T(8,128)(2,1)S(1)} %slice.177), channel_id=1, source_target_pairs={{0,8},{1,9},{2,10},{3,11},{4,12},{5,13},{6,14},{7,15},{8,0},{9,1},... | collective-permute-start | bytes 884744 | tf_op jit(solution)/shard_map/ppermute | solution.py:422
  554.4 6.5 %collective-permute-start.19 = (bf16[1,32,2304]{2,1,0:T(8,128)(2,1)S(1)}, bf16[1,32,2304]{2,1,0:T(8,128)(2,1)S(1)}, u32[]{:S(2)}, u32[]{:S(2)}) collective-permute-start(bf16[1,32,2304]{2,1,0:T(8,128)(2,1)S(1)} %slice.179), channel_id=1, source_target_pairs={{0,16},{1,17},{2,18},{3,19},{4,20},{5,21},{6,22},{7,23},{8,24},{9,... | collective-permute-start | bytes 442376 | tf_op jit(solution)/shard_map/ppermute | solution.py:422
  (3 other events, 4.0 us)

commit v2 on v1

v2 whole, which is shorter than its diff:
```python
import functools
import math

import jax
import jax.numpy as jnp
from jax import lax
from jax.sharding import PartitionSpec as P
from jax.experimental import pallas as pl
from jax.experimental.pallas import tpu as pltpu

HEAD_DIM = 64
LEN = 1024
PIECES = 8
PAIRS = 4
D = 512
FF = 2048
HALF = 256
HEADS2 = 4
QB = 256
KB = 128
NQ = LEN // QB
NK = LEN // KB
BIG = 1e30
LOG2E = math.log2(math.e)
QSCALE = LOG2E / math.sqrt(HEAD_DIM)
KSCALE = math.log(2.0)
WIDTHS = (2, 3, 4, 5, 6, 7, 8)
EPS = 1e-5
C1 = math.sqrt(2.0 / math.pi)
C2 = C1 * 0.044715
F32 = jnp.float32
BF = jnp.bfloat16
VMEM_LIMIT = 60 * 1024 * 1024
TM = 256


def nn(a, b):
    return jnp.dot(a, b, preferred_element_type=F32)


def nt(a, b):
    return lax.dot_general(a, b, (((1,), (1,)), ((), ())), preferred_element_type=F32)


def tn(a, b):
    return lax.dot_general(a, b, (((0,), (0,)), ((), ())), preferred_element_type=F32)


def piece_ends(pieces_ref):
    ends, at = [], 0
    for j in range(PIECES):
        at = at + pieces_ref[j]
        ends.append(at)
    return ends


def window(block, ends):
    first = block * QB
    last = first + QB - 1
    low, high = jnp.int32(0), jnp.int32(LEN)
    for end in ends[:-1]:
        low = jnp.maximum(low, jnp.where(end <= first, end, 0))
        high = jnp.minimum(high, jnp.where(end > last, end, LEN))
    low = jnp.where(first >= ends[-2], first, low)
    high = jnp.where(last >= ends[-2], last + 1, high)
    return low // KB, (high + KB - 1) // KB


def over_widths(block, ends, run):
    low, high = window(block, ends)
    count = high - low
    previous = 0
    for wide in WIDTHS:
        begin = jnp.minimum(low, NK - wide)

        @pl.when((count > previous) & (count <= wide))
        def _(wide=wide, begin=begin):
            run(wide, pl.multiple_of(begin * KB, KB))

        previous = wide


def segment_codes(ends, segq_ref, segk_ref):
    rows = lax.broadcasted_iota(jnp.int32, (LEN, 128), 0)
    lanes = lax.broadcasted_iota(jnp.int32, (LEN, 128), 1)
    ids = jnp.zeros((LEN, 128), jnp.int32)
    for end in ends[:-1]:
        ids = ids + jnp.where(rows >= end, 1, 0)
    same = lanes == ids
    segk_ref[...] = jnp.where(same, 1.0, 0.0).astype(BF)
    free = (lanes >= PIECES) | (same & (lanes < PIECES - 1))
    segq_ref[...] = jnp.where(free, 0.0, -BIG).astype(BF)


def lane_half(shape):
    return lax.broadcasted_iota(jnp.int32, shape, 1) < HEAD_DIM


def two_heads(block):
    left = lane_half(block.shape)
    zero = jnp.zeros_like(block)
    return jnp.where(left, block, zero), jnp.where(left, zero, block)


def block_rows(index, size):
    return pl.ds(pl.multiple_of(index * size, size), size)


def head_norms(values, half):
    heads = lax.broadcasted_iota(jnp.int32, (HALF, 128), 0) // HEAD_DIM + half * (HALF // HEAD_DIM)
    pick = jnp.where(heads == lax.broadcasted_iota(jnp.int32, (HALF, 128), 1), 1.0, 0.0).astype(BF)
    return jnp.max(nn((values * values).astype(BF), pick), axis=0, keepdims=True)


def project_stage(x_ref, w_refs, q_ref, k_ref, v_ref, vt_ref):
    def chunk(i, carry):
        rows = block_rows(i, TM)
        low = x_ref[rows, :]
        q_top, k_top = carry
        for half in range(2):
            cols = slice(half * HALF, (half + 1) * HALF)
            queries = nn(low, w_refs[half][:, :HALF]) * QSCALE
            keys = nn(low, w_refs[half][:, HALF:2 * HALF])
            q_ref[rows, cols] = queries.astype(BF)
            k_ref[rows, cols] = keys.astype(BF)
            q_top = jnp.maximum(q_top, head_norms(queries, half))
            k_top = jnp.maximum(k_top, head_norms(keys, half))
            values = nn(low, w_refs[half][:, 2 * HALF:])
            v_ref[rows, cols] = values.astype(BF)
            for pair in range(2):
                vt_ref[half * 2 + pair, :128, rows] = values[:, pair * 128:(pair + 1) * 128].T.astype(BF)
        return q_top, k_top

    zero = jnp.zeros((1, 128), F32)
    q_top, k_top = lax.fori_loop(0, LEN // TM, chunk, (zero, zero))
    for pair in range(HEADS2):
        vt_ref[pair, 128:, :] = jnp.ones((16, LEN), BF)
    return jnp.max(q_top * k_top)


def probs_copy(p_slots, p_ref, sem, i, wide):
    slot = i % 2
    return pltpu.make_async_copy(p_slots.at[slot, :, pl.ds(0, wide * KB), :],
                                 p_ref.at[i, :, pl.ds(0, wide * KB), :], sem.at[slot])


def attend_stage(ends, shifted, q_ref, k_ref, v_ref, vt_ref, segq_ref, segk_ref, mixed_ref, exact_ref, inv_ref,
                 p_slots, p_out, p_sem):
    def block(i, carry):
        rows = block_rows(i, QB)
        p_ref = p_slots.at[i % 2]

        @pl.when(i >= 2)
        def _():
            over_widths(i - 2, ends, lambda wide, begin: probs_copy(p_slots, p_out, p_sem, i - 2, wide).wait())

        def run(wide, begin):
            keys = pl.ds(begin, wide * KB)
            segq = segq_ref[rows, :]
            segk = segk_ref[keys, :]
            pad = lax.broadcasted_iota(jnp.int32, (QB, 128), 0) + i * QB >= ends[-2]
            span = [slice(pair * 128, (pair + 1) * 128) for pair in range(HEADS2)]

            def score(pair):
                even, odd = two_heads(q_ref[rows, span[pair]])
                query = jnp.concatenate(
                    [jnp.concatenate([even, segq], axis=1), jnp.concatenate([odd, segq], axis=1)], axis=0)
                key = jnp.concatenate([k_ref[keys, span[pair]], segk], axis=1)
                return nt(key, query)

            def soften(pair, scores):
                if shifted:
                    scores = scores - jnp.max(scores, axis=0, keepdims=True)
                probs = jnp.exp2(scores).astype(BF)
                p_ref[pair, :wide * KB, :] = probs
                return probs

            def mix(pair, probs):
                return nn(vt_ref[pair, :, keys], probs)

            def finish(pair, out):
                cols = span[pair]
                inv = 1.0 / jnp.maximum(out[128:129, :], 1e-30)
                inv_both = jnp.concatenate(
                    [jnp.broadcast_to(inv[:, :QB], (64, QB)), jnp.broadcast_to(inv[:, QB:], (64, QB))], axis=0)
                out_both = jnp.concatenate([out[:64, :QB], out[64:128, QB:]], axis=0) * inv_both
                exact = out_both.T
                exact_ref[rows, cols] = exact
                mixed_ref[rows, cols] = jnp.where(pad, v_ref[rows, cols].astype(F32), exact).astype(BF)
                inv_ref[rows, cols] = inv_both.T

            s = {0: score(0), 1: score(1)}
            p, o = {}, {}
            for pair in range(HEADS2):
                p[pair] = soften(pair, s[pair])
                if pair + 2 < HEADS2:
                    s[pair + 2] = score(pair + 2)
                if pair:
                    o[pair - 1] = mix(pair - 1, p[pair - 1])
                if pair > 1:
                    finish(pair - 2, o[pair - 2])
            probs_copy(p_slots, p_out, p_sem, i, wide).start()
            o[HEADS2 - 1] = mix(HEADS2 - 1, p[HEADS2 - 1])
            finish(HEADS2 - 2, o[HEADS2 - 2])
            finish(HEADS2 - 1, o[HEADS2 - 1])

        over_widths(i, ends, run)
        return carry

    lax.fori_loop(0, NQ, block, 0)
    for i in range(NQ - 2, NQ):
        over_widths(i, ends, lambda wide, begin, i=i: probs_copy(p_slots, p_out, p_sem, i, wide).wait())


def probs_fetch(p_in, p_slots, sem, i, wide):
    return pltpu.make_async_copy(p_in.at[i, :, pl.ds(0, wide * KB), :],
                                 p_slots.at[i, :, pl.ds(0, wide * KB), :], sem.at[i])


def probs_start(ends, p_in, p_slots, sem):
    for i in range(NQ):
        over_widths(i, ends, lambda wide, begin, i=i: probs_fetch(p_in, p_slots, sem, i, wide).start())


def attend_back_stage(ends, q_ref, k_ref, v_ref, kt_ref, exact_ref, grad_ref, p_in, p_slots, p_sem,
                      dk_ref, dv_ref, grads_ref):
    dk_ref[...] = jnp.zeros_like(dk_ref)
    dv_ref[...] = jnp.zeros_like(dv_ref)
    for pair in range(HEADS2):
        kt_ref[pair] = k_ref[:, pair * 128:(pair + 1) * 128].astype(F32).T.astype(BF)
    span = [slice(pair * 128, (pair + 1) * 128) for pair in range(HEADS2)]

    def block(i, carry):
        rows = block_rows(i, QB)
        p_ref = p_slots.at[i]

        def run(wide, begin):
            keys = pl.ds(begin, wide * KB)
            probs_fetch(p_in, p_slots, p_sem, i, wide).wait()

            def outer(pair):
                return jnp.concatenate(two_heads(grad_ref[rows, span[pair]]), axis=0)

            def slope(pair):
                grad = grad_ref[rows, span[pair]]
                inner = grad.astype(F32) * exact_ref[rows, span[pair]]
                high = inner.astype(BF)
                rest = pltpu.roll(inner - high.astype(F32), HEAD_DIM, 1).astype(BF)
                left = lane_half(inner.shape)
                inner = jnp.concatenate([jnp.where(left, high, rest), jnp.where(left, rest, high)], axis=0)
                both = jnp.concatenate([outer(pair), inner], axis=1)
                value = jnp.concatenate([v_ref[keys, span[pair]], jnp.full((wide * KB, 128), -1.0, BF)], axis=1)
                return nt(value, both)

            def bend(pair, slope):
                return (p_ref[pair, :wide * KB, :].astype(F32) * slope).astype(BF)

            def values(pair):
                dv_ref[pair, keys, :] += nn(p_ref[pair, :wide * KB, :], outer(pair))

            def rest(pair, scores):
                query = jnp.concatenate(two_heads(q_ref[rows, span[pair]]), axis=0)
                dk_ref[pair, keys, :] += nn(scores, query)
                out = nn(kt_ref[pair, :, keys], scores)
                out = jnp.concatenate([out[:64, :QB], out[64:, QB:]], axis=0)
                grads_ref[rows, span[pair]] = (out.T * (HEAD_DIM ** -0.5)).astype(BF)

            s = {0: slope(0), 1: slope(1)}
            d = {}
            for pair in range(HEADS2):
                d[pair] = bend(pair, s[pair])
                values(pair)
                if pair + 2 < HEADS2:
                    s[pair + 2] = slope(pair + 2)
                if pair:
                    rest(pair - 1, d[pair - 1])
            rest(HEADS2 - 1, d[HEADS2 - 1])

        over_widths(i, ends, run)
        return carry

    lax.fori_loop(0, NQ, block, 0)
    for pair in range(HEADS2):
        grads_ref[:, D + pair * 128:D + (pair + 1) * 128] = (dk_ref[pair] * KSCALE).astype(BF)
        grads_ref[:, 2 * D + pair * 128:2 * D + (pair + 1) * 128] = dv_ref[pair].astype(BF)


def unit_rows(values):
    center = values - jnp.mean(values, axis=-1, keepdims=True)
    spread = jnp.mean(center * center, axis=-1, keepdims=True)
    inv = lax.rsqrt(spread + EPS)
    return center * inv, inv


def feed_stage(x_ref, mixed_ref, wo_ref, wh_ref, wd_ref, par_ref, out_ref, unit1_ref, inv1_ref,
               norm_ref, act_ref, slope_ref, unit2_ref, inv2_ref, tm=512):
    def chunk(i, carry):
        rows = block_rows(i, tm)
        summed = x_ref[rows, :] + nt(mixed_ref[rows, :], wo_ref[...])
        unit, inv = unit_rows(summed)
        unit1_ref[rows, :] = unit.astype(BF)
        inv1_ref[rows, :] = inv
        normed = unit * par_ref[0:1, :] + par_ref[1:2, :]
        low = normed.astype(BF)
        norm_ref[rows, :] = low
        total = normed
        for at in range(0, FF, 512):
            cols = slice(at, at + 512)
            hidden = nn(low, wh_ref[:, cols])
            square = hidden * hidden
            gate = 0.5 + 0.5 * jnp.tanh(hidden * (C1 + C2 * square))
            act = (hidden * gate).astype(BF)
            act_ref[rows, cols] = act
            slope_ref[rows, cols] = (gate + gate * (1.0 - gate) * hidden * (2 * C1 + 6 * C2 * square)).astype(BF)
        total = normed + nt(act_ref[rows, :], wd_ref[...])
        unit, inv = unit_rows(total)
        unit2_ref[rows, :] = unit.astype(BF)
        inv2_ref[rows, :] = inv
        out_ref[rows, :] = unit * par_ref[2:3, :] + par_ref[3:4, :]
        return carry

    lax.fori_loop(0, LEN // tm, chunk, 0)


def unit_back(grad, unit, inv, gain):
    scaled = grad * gain
    first = jnp.mean(scaled, axis=-1, keepdims=True)
    second = jnp.mean(scaled * unit, axis=-1, keepdims=True)
    return inv * (scaled - first - unit * second)


def fold_rows(values):
    return jnp.sum(values.reshape(-1, 8, values.shape[-1]), axis=0)


def total_stage(limit, grad_ref, unit2_ref, inv2_ref, par_ref, total_ref, low_ref, small_ref, tm=512):
    small_ref[...] = jnp.zeros_like(small_ref)

    def chunk(i, carry):
        rows = block_rows(i, tm)
        grad = grad_ref[rows, :]
        if limit is not None:
            grad = jnp.where(lax.broadcasted_iota(jnp.int32, grad.shape, 0) + i * tm < limit, grad, 0.0)
        unit2 = unit2_ref[rows, :].astype(F32)
        small_ref[16:24, :] += fold_rows(grad * unit2)
        small_ref[24:32, :] += fold_rows(grad)
        total = unit_back(grad, unit2, inv2_ref[rows, :], par_ref[2:3, :])
        total_ref[rows, :] = total
        low_ref[rows, :] = total.astype(BF)
        return carry

    lax.fori_loop(0, LEN // tm, chunk, 0)


def feed_back_stage(total_ref, low_ref, unit1_ref, inv1_ref, slope_ref, inv_ref, wo_ref, wh_ref, wd_ref, par_ref,
                    base_ref, gm_ref, small_ref, hid_ref, att_ref, tm=512):
    def chunk(i, carry):
        rows = block_rows(i, tm)
        low = low_ref[rows, :]
        for at in range(0, FF, 512):
            cols = slice(at, at + 512)
            hid_ref[rows, cols] = (nn(low, wd_ref[:, cols]) * slope_ref[rows, cols].astype(F32)).astype(BF)
        normed = total_ref[rows, :] + nt(hid_ref[rows, :], wh_ref[...])
        unit1 = unit1_ref[rows, :].astype(F32)
        small_ref[0:8, :] += fold_rows(normed * unit1)
        small_ref[8:16, :] += fold_rows(normed)
        summed = unit_back(normed, unit1, inv1_ref[rows, :], par_ref[0:1, :])
        base_ref[rows, :] = summed
        low = summed.astype(BF)
        att_ref[rows, :] = low
        gm_ref[rows, :] = (nn(low, wo_ref[...]) * inv_ref[rows, :]).astype(BF)
        return carry

    lax.fori_loop(0, LEN // tm, chunk, 0)


def weight_stage(left_ref, right_ref, old_ref, out_ref, width=512):
    def chunk(i, carry):
        cols = block_rows(i, width)
        value = tn(left_ref[...], right_ref[:, cols])
        if old_ref is not None:
            value = value + old_ref[:, cols].astype(F32)
        out_ref[:, cols] = value.astype(BF)
        return carry

    lax.fori_loop(0, out_ref.shape[1] // width, chunk, 0)


def input_stage(base_ref, grads_ref, w_refs, out_ref):
    def chunk(i, carry):
        rows = block_rows(i, TM)
        value = base_ref[rows, :]
        for half in range(2):
            for part in range(3):
                value = value + nt(grads_ref[rows, part * D + half * HALF:part * D + (half + 1) * HALF],
                                   w_refs[half][:, part * HALF:(part + 1) * HALF])
        out_ref[rows, :] = value
        return carry

    lax.fori_loop(0, LEN // TM, chunk, 0)


LIMIT = 64.0 ** 2
P_SHAPE = (NQ, HEADS2, LEN, 2 * QB)
VMEM = pltpu.VMEM


class Moves:
    def __init__(self, sem):
        self.sem, self.count, self.open = sem, 0, []

    def fetch(self, source, target):
        copy = pltpu.make_async_copy(source, target, self.sem.at[self.count])
        self.count += 1
        copy.start()
        return copy

    def send(self, source, target):
        self.open.append(self.fetch(source, target))

    def finish(self):
        for copy in self.open:
            copy.wait()


def wait(*copies):
    for copy in copies:
        copy.wait()


def rows_in(moves, at_ref, half, source, target, begin, width, to):
    if len(source.shape) == 2:
        return [moves.fetch(source.at[:, pl.ds(begin, width)], target.at[:, pl.ds(to, width)])]
    dp, rows, _ = source.shape
    return [moves.fetch(source.at[at_ref[half, b], :, pl.ds(begin, width)],
                        target.at[pl.ds(b * rows, rows), pl.ds(to, width)]) for b in range(dp)]


def rows_out(moves, to_ref, half, source, begin, width, target, to):
    if len(target.shape) == 2:
        moves.send(source.at[:, pl.ds(begin, width)], target.at[:, pl.ds(to, width)])
        return
    dp, rows, _ = target.shape
    for b in range(dp):
        moves.send(source.at[pl.ds(b * rows, rows), pl.ds(begin, width)],
                   target.at[to_ref[half, b], :, pl.ds(to, width)])


ANY = pl.BlockSpec(memory_space=pl.ANY)
SMEM = pl.BlockSpec(memory_space=pltpu.SMEM)


def shaped(*shapes):
    return [jax.ShapeDtypeStruct(s, t) for s, t in shapes]


def like(shapes):
    return [VMEM(s, t) for s, t in shapes]


def full(width, kind=BF):
    return ((LEN, width), kind)


ATTEND_OUT = (full(D), full(D), full(D), full(D), full(D, F32), full(D, F32))
ATTEND_WORK = [VMEM((HEADS2, 144, LEN), BF), VMEM((LEN, 128), BF), VMEM((LEN, 128), BF),
               VMEM((2,) + P_SHAPE[1:], BF), pltpu.SemaphoreType.DMA((2,))]


def attend_whole(ends, moves, low_s, weights, outs, scratch, p_out, work):
    q, k, v, mixed, exact, inv = scratch
    vt, segq, segk, p_slots, p_sem = work
    bound = project_stage(low_s, weights, q, k, v, vt)
    for i in range(3):
        moves.send(scratch[i], outs[i])
    for shifted in (False, True):
        @pl.when((bound > LIMIT) if shifted else (bound <= LIMIT))
        def _(shifted=shifted):
            attend_stage(ends, shifted, q, k, v, vt, segq, segk, mixed, exact, inv, p_slots, p_out, p_sem)
    for i in range(3, 6):
        moves.send(scratch[i], outs[i])


def call(kernel, ins, outs, scratch, sems, flops, *args):
    smem = sum(a.dtype == jnp.int32 for a in args)
    return pl.pallas_call(
        kernel,
        in_specs=[SMEM] * smem + [ANY] * (len(args) - smem),
        out_specs=[ANY] * len(outs),
        out_shape=shaped(*outs),
        scratch_shapes=scratch + [pltpu.SemaphoreType.DMA((sems,))],
        compiler_params=pltpu.CompilerParams(vmem_limit_bytes=VMEM_LIMIT),
        cost_estimate=pl.CostEstimate(flops=flops, bytes_accessed=8 << 20, transcendentals=0),
    )(*args)


def open_kernel(pieces_ref, tag_ref, at_ref, emb_ref, own_ref, other_ref, *refs):
    outs, refs = refs[:12], refs[12:]
    x_o, low_o, par_o, wa_o, wb_o, p_o = outs[:6]
    x_s, low_s, par_s, wa_s, wb_s, small_s = refs[:6]
    scratch, work, sem = refs[6:12], refs[12:17], refs[17]
    moves = Moves(sem)
    ends = piece_ends(pieces_ref)
    first = moves.fetch(emb_ref, x_s)
    small = rows_in(moves, at_ref, 0, own_ref, small_s, 3 * HALF, 128, 0)
    weights = rows_in(moves, at_ref, 0, own_ref, wa_s, 0, 3 * HALF, 0)
    weights += rows_in(moves, at_ref, 1, other_ref, wb_s, 0, 3 * HALF, 0)
    segment_codes(ends, work[1], work[2])
    wait(*small)
    par_s[...] = small_s[...].astype(F32).T[:8, :]
    moves.send(par_s, par_o)
    wait(first)
    row = par_s[pl.ds(4 + tag_ref[0], 1), :]

    def chunk(i, carry):
        rows = block_rows(i, TM)
        value = x_s[rows, :] + row
        x_s[rows, :] = value
        low_s[rows, :] = value.astype(BF)
        return carry

    lax.fori_loop(0, LEN // TM, chunk, 0)
    moves.send(x_s, x_o)
    moves.send(low_s, low_o)
    wait(*weights)
    moves.send(wa_s, wa_o)
    moves.send(wb_s, wb_o)
    attend_whole(ends, moves, low_s, (wa_s, wb_s), outs[6:], scratch, p_o, work)
    moves.finish()


def open_visit(pieces, tag, at, embedded, own, other):
    own_outs = (full(D, F32), full(D), ((8, D), F32), ((D, 3 * HALF), BF), ((D, 3 * HALF), BF))
    outs = own_outs + ((P_SHAPE, BF),) + ATTEND_OUT
    scratch = like(own_outs) + [VMEM((D, 128), BF)] + like(ATTEND_OUT) + ATTEND_WORK
    x, low, par, wa, wb, p, *rest = call(open_kernel, None, outs, scratch, 3 * 64 + 16, 7_000_000_000,
                                         pieces, tag, at, embedded, own, other)
    return x, low, par, wa, wb, (*rest, p)


SAVED = (full(D), full(1, F32), full(D), full(FF), full(FF), full(D), full(1, F32))


def second_kernel(pieces_ref, at_ref, x_ref, mixed_ref, own_ref, other_ref, par_ref, wa_ref, wb_ref, *refs):
    weight_o, saved_o, x_o, low_o, p_o, outs = refs[:3], refs[3:10], refs[10], refs[11], refs[12], refs[13:19]
    refs = refs[19:]
    x_s, mix_s, par_s, wa_s, wb_s = refs[:5]
    weight_s, saved_s, low_s = refs[5:8], refs[8:15], refs[15]
    scratch, work, sem = refs[16:22], refs[22:27], refs[27]
    moves = Moves(sem)
    ends = piece_ends(pieces_ref)
    wo_s, wh_s, wd_s = weight_s
    first = [moves.fetch(x_ref, x_s), moves.fetch(mixed_ref, mix_s), moves.fetch(par_ref, par_s)]
    for half, ref in enumerate((own_ref, other_ref)):
        first += rows_in(moves, at_ref, half, ref, wo_s, 0, HALF, half * HALF)
        first += rows_in(moves, at_ref, half, ref, wh_s, HALF, FF // 2, half * (FF // 2))
        first += rows_in(moves, at_ref, half, ref, wd_s, HALF + FF // 2, FF // 2, half * (FF // 2))
    later = [moves.fetch(wa_ref, wa_s), moves.fetch(wb_ref, wb_s)]
    segment_codes(ends, work[1], work[2])
    wait(*first)
    feed_stage(x_s, mix_s, wo_s, wh_s, wd_s, par_s, x_s, *saved_s)
    for a, b in zip(weight_s + saved_s + (x_s,), weight_o + saved_o + (x_o,)):
        moves.send(a, b)

    def chunk(i, carry):
        rows = block_rows(i, TM)
        low_s[rows, :] = x_s[rows, :].astype(BF)
        return carry

    lax.fori_loop(0, LEN // TM, chunk, 0)
    moves.send(low_s, low_o)
    wait(*later)
    attend_whole(ends, moves, low_s, (wa_s, wb_s), outs, scratch, p_o, work)
    moves.finish()


def second_visit(pieces, at, x, mixed, own, other, par, wa, wb):
    weights = (((D, D), BF), ((D, FF), BF), ((D, FF), BF))
    outs = weights + SAVED + (full(D, F32), full(D), (P_SHAPE, BF)) + ATTEND_OUT
    scratch = (like((full(D, F32), full(D), ((8, D), F32), ((D, 3 * HALF), BF), ((D, 3 * HALF), BF)) + weights + SAVED
                    + (full(D),) + ATTEND_OUT) + ATTEND_WORK)
    got = call(second_kernel, None, outs, scratch, 6 * 64 + 32, 12_000_000_000,
               pieces, at, x, mixed, own, other, par, wa, wb)
    return got[:3], got[3:10], got[10], got[11], (*got[13:], got[12])


def middle_kernel(pieces_ref, x_ref, mixed_ref, inv_ref, cot_ref, wo_ref, wh_ref, wd_ref, par_ref, *refs):
    outs, refs = refs[:7], refs[7:]
    ins, refs = refs[:8], refs[8:]
    saved, refs = refs[:7], refs[7:]
    result, total, low, hid, att = refs[:5]
    base, gm, dd, dh, do, small = refs[5:11]
    x, mixed, inv, cot, wo, wh, wd, par = ins
    unit1, inv1, norm, act, slope, unit2, inv2 = saved
    moves = Moves(refs[11])
    ends = piece_ends(pieces_ref)
    order = ((x_ref, x), (mixed_ref, mixed), (wo_ref, wo), (par_ref, par), (wh_ref, wh), (wd_ref, wd))
    first = [moves.fetch(a, b) for a, b in order]
    later = [moves.fetch(cot_ref, cot), moves.fetch(inv_ref, inv)]
    wait(*first)
    feed_stage(x, mixed, wo, wh, wd, par, result, *saved)
    moves.send(result, outs[0])
    wait(*later)
    total_stage(ends[-2], cot, unit2, inv2, par, total, low, small)
    feed_back_stage(total, low, unit1, inv1, slope, inv, wo, wh, wd, par, base, gm, small, hid, att)
    moves.send(base, outs[1])
    moves.send(gm, outs[2])
    moves.send(small, outs[6])
    weight_stage(low, act, None, dd)
    moves.send(dd, outs[3])
    weight_stage(norm, hid, None, dh)
    moves.send(dh, outs[4])
    weight_stage(att, mixed, None, do)
    moves.send(do, outs[5])
    moves.finish()


def middle(pieces, x, mixed, inv, cot, wo, wh, wd, par):
    outs = (full(D, F32), full(D, F32), full(D), ((D, FF), BF), ((D, FF), BF), ((D, D), BF), ((32, D), F32))
    ins = (full(D, F32), full(D), full(D, F32), full(D, F32), ((D, D), BF), ((D, FF), BF), ((D, FF), BF), ((8, D), F32))
    scratch = like(ins + SAVED + (full(D, F32), full(D, F32), full(D), full(FF), full(D)) + outs[1:])
    return call(middle_kernel, None, outs, scratch, 32, 20_000_000_000,
                pieces, x, mixed, inv, cot, wo, wh, wd, par)


BACK_WORK = [VMEM(P_SHAPE, BF), VMEM((HEADS2, 128, LEN), BF), VMEM((HEADS2, LEN, 128), F32),
             VMEM((HEADS2, LEN, 128), F32), VMEM((LEN, 3 * D), BF), pltpu.SemaphoreType.DMA((NQ,))]
BACK_IN = (full(D), full(D), full(D), full(D, F32), full(D), full(D))


def pack_grads(low, grads, olds, outs):
    for half in range(2):
        for part in range(3):
            cols = slice(part * HALF, (part + 1) * HALF)
            value = tn(low[...], grads[:, part * D + half * HALF:part * D + (half + 1) * HALF])
            if olds is not None:
                value = value + olds[half][:, cols].astype(F32)
            outs[half][:, cols] = value.astype(BF)


def back_kernel(pieces_ref, q_ref, k_ref, v_ref, exact_ref, gm_ref, low_ref, p_ref, base_ref, wa_ref, wb_ref, *refs):
    dx_o, da_o, db_o = refs[:3]
    ins, refs = refs[3:9], refs[9:]
    base, wa, wb, dx, da, db = refs[:6]
    p_slots, kt, dk, dv, grads, p_sem, sem = refs[6:]
    moves = Moves(sem)
    ends = piece_ends(pieces_ref)
    first = [moves.fetch(a, b) for a, b in zip((q_ref, k_ref, v_ref, exact_ref, gm_ref), ins)]
    probs_start(ends, p_ref, p_slots, p_sem)
    later = [moves.fetch(a, b) for a, b in ((low_ref, ins[5]), (base_ref, base), (wa_ref, wa), (wb_ref, wb))]
    wait(*first)
    q, k, v, exact, gm, low = ins
    attend_back_stage(ends, q, k, v, kt, exact, gm, p_ref, p_slots, p_sem, dk, dv, grads)
    wait(*later)
    input_stage(base, grads, (wa, wb), dx)
    moves.send(dx, dx_o)
    pack_grads(low, grads, None, (da, db))
    moves.send(da, da_o)
    moves.send(db, db_o)
    moves.finish()


def back(pieces, heads, low, gm, base, wa, wb):
    q, k, v, mixed, exact, inv, p = heads
    pair = (((D, 3 * HALF), BF),) * 2
    outs = (full(D, F32),) + pair
    scratch = like(BACK_IN + (full(D, F32),) + pair + outs) + BACK_WORK
    return call(back_kernel, None, outs, scratch, 16, 14_000_000_000,
                pieces, q, k, v, exact, gm, low, p, base, wa, wb)


def down_kernel(to_ref, grad_ref, unit2_ref, inv2_ref, par_ref, act_ref, old_ref, *refs):
    total_o, low_o, small_o, keep_o, send_o = refs[:5]
    grad, unit2, inv2, par, act, old, total, low, small, dd, sem = refs[5:]
    moves = Moves(sem)
    first = [moves.fetch(a, b) for a, b in ((grad_ref, grad), (unit2_ref, unit2), (inv2_ref, inv2), (par_ref, par))]
    later = [moves.fetch(act_ref, act), moves.fetch(old_ref, old)]
    wait(*first)
    total_stage(None, grad, unit2, inv2, par, total, low, small)
    moves.send(total, total_o)
    moves.send(low, low_o)
    moves.send(small, small_o)
    wait(*later)
    weight_stage(low, act, old, dd)
    for half, target in enumerate((keep_o, send_o)):
        rows_out(moves, to_ref, half, dd, half * (FF // 2), FF // 2, target, 0)
    moves.finish()


def down(to, part, grad, unit2, inv2, par, act, old):
    outs = (full(D, F32), full(D), ((32, D), F32), (part(FF // 2), BF), (part(FF // 2), BF))
    scratch = like((full(D, F32), full(D), full(1, F32), ((8, D), F32), full(FF), ((D, FF), BF))
                   + outs[:3] + (((D, FF), BF),))
    return call(down_kernel, None, outs, scratch, 160, 3_000_000_000, to, grad, unit2, inv2, par, act, old)


def hidden_kernel(to_ref, total_ref, low_ref, small_ref, unit1_ref, inv1_ref, norm_ref, slope_ref, inv_ref, mixed_ref,
                  wo_ref, wh_ref, wd_ref, par_ref, old_h_ref, old_o_ref, *refs):
    base_o, gm_o, small_o, keep_o, send_o = refs[:5]
    ins, refs = refs[5:20], refs[20:]
    base, gm, hid, att, dh, do, sem = refs
    total, low, small, unit1, inv1, norm, slope, inv, mixed, wo, wh, wd, par, old_h, old_o = ins
    moves = Moves(sem)
    first = [moves.fetch(a, b) for a, b in (
        (low_ref, low), (wd_ref, wd), (slope_ref, slope), (wh_ref, wh), (total_ref, total), (small_ref, small),
        (unit1_ref, unit1), (inv1_ref, inv1), (par_ref, par), (wo_ref, wo), (inv_ref, inv))]
    later = [moves.fetch(a, b) for a, b in (
        (norm_ref, norm), (old_h_ref, old_h), (mixed_ref, mixed), (old_o_ref, old_o))]
    wait(*first)
    feed_back_stage(total, low, unit1, inv1, slope, inv, wo, wh, wd, par, base, gm, small, hid, att)
    moves.send(base, base_o)
    moves.send(gm, gm_o)
    moves.send(small, small_o)
    wait(*later)
    weight_stage(norm, hid, old_h, dh)
    for half, target in enumerate((keep_o, send_o)):
        rows_out(moves, to_ref, half, dh, half * (FF // 2), FF // 2, target, HALF)
    weight_stage(att, mixed, old_o, do)
    for half, target in enumerate((keep_o, send_o)):
        rows_out(moves, to_ref, half, do, half * HALF, HALF, target, 0)
    moves.finish()


def hidden_back(to, part, total, low, small, unit1, inv1, norm, slope, inv, mixed, wo, wh, wd, par, old_h, old_o):
    outs = (full(D, F32), full(D), ((32, D), F32), (part(REST_H), BF), (part(REST_H), BF))
    args = (total, low, small, unit1, inv1, norm, slope, inv, mixed, wo, wh, wd, par, old_h, old_o)
    scratch = like(tuple((a.shape, a.dtype) for a in args) + outs[:2]
                   + (full(FF), full(D), ((D, FF), BF), ((D, D), BF)))
    return call(hidden_kernel, None, outs, scratch, 320, 12_000_000_000, to, *args)


REST_H = HALF + FF // 2
FIRST = 3 * HALF + 128


def last_kernel(pieces_ref, tag_ref, to_ref, q_ref, k_ref, v_ref, exact_ref, gm_ref, low_ref, p_ref, base_ref, wa_ref,
                wb_ref, old_a_ref, old_b_ref, small_a_ref, small_b_ref, *refs):
    grads_o, keep_o, send_o = refs[:3]
    ins, refs = refs[3:9], refs[9:]
    base, wa, wb, old_a, old_b, small_a, small_b, da, db, stats = refs[:10]
    p_slots, kt, dk, dv, grads, p_sem, sem = refs[10:]
    moves = Moves(sem)
    ends = piece_ends(pieces_ref)
    first = [moves.fetch(a, b) for a, b in zip((q_ref, k_ref, v_ref, exact_ref, gm_ref), ins)]
    probs_start(ends, p_ref, p_slots, p_sem)
    later = [moves.fetch(a, b) for a, b in (
        (low_ref, ins[5]), (base_ref, base), (wa_ref, wa), (wb_ref, wb), (old_a_ref, old_a), (old_b_ref, old_b),
        (small_a_ref, small_a), (small_b_ref, small_b))]
    wait(*first)
    q, k, v, exact, gm, low = ins
    attend_back_stage(ends, q, k, v, kt, exact, gm, p_ref, p_slots, p_sem, dk, dv, grads)
    moves.send(grads, grads_o)
    wait(*later)
    pack_grads(low, grads, (old_a, old_b), (da, db))
    rows_out(moves, to_ref, 0, da, 0, 3 * HALF, keep_o, 0)
    rows_out(moves, to_ref, 1, db, 0, 3 * HALF, send_o, 0)
    sums = nn(jnp.ones((8, LEN), BF), grads[...])
    high = sums.astype(BF)
    rest = (sums - high.astype(F32)).astype(BF)
    column = jnp.sum(base[...], axis=0, keepdims=True)
    for half, w in enumerate((wa, wb)):
        for part in range(3):
            at = part * D + half * HALF
            for piece in (high, rest):
                column = column + nt(piece[:, at:at + HALF], w[:, part * HALF:(part + 1) * HALF])[:1]
    norms = jnp.sum((small_a[...] + small_b[...]).reshape(4, 8, D), axis=1)
    tags = lax.broadcasted_iota(jnp.int32, (PAIRS, D), 0) == tag_ref[0]
    table = jnp.where(tags, jnp.broadcast_to(column, (PAIRS, D)), 0.0)
    rows = jnp.concatenate([norms, table, jnp.zeros((120, D), F32)], axis=0)
    stats[...] = rows.T.astype(BF)
    rows_out(moves, to_ref, 0, stats, 0, 128, keep_o, 3 * HALF)
    rows_out(moves, to_ref, 1, stats, 0, 128, send_o, 3 * HALF)
    moves.finish()


def last_back(pieces, tag, to, part, heads, low, gm, base, wa, wb, old_a, old_b, small_a, small_b):
    q, k, v, mixed, exact, inv, p = heads
    pair = (((D, 3 * HALF), BF),) * 2
    outs = (full(3 * D), (part(FIRST), BF), (part(FIRST), BF))
    stats = ((32, D), F32)
    scratch = like(BACK_IN + (full(D, F32),) + pair + pair + (stats, stats) + pair + (((D, 128), BF),)) + BACK_WORK
    return call(last_kernel, None, outs, scratch, 4 * 64 + 32, 12_000_000_000,
                pieces, tag, to, q, k, v, exact, gm, low, p, base, wa, wb, old_a, old_b, small_a, small_b)


def input_kernel(base_ref, grads_ref, wa_ref, wb_ref, out_ref):
    input_stage(base_ref, grads_ref, (wa_ref, wb_ref), out_ref)


def input_back(base, grads, wa, wb):
    return pl.pallas_call(
        input_kernel,
        out_shape=jax.ShapeDtypeStruct((LEN, D), F32),
        compiler_params=pltpu.CompilerParams(vmem_limit_bytes=VMEM_LIMIT),
        cost_estimate=pl.CostEstimate(flops=1_600_000_000, bytes_accessed=9 << 20, transcendentals=0),
    )(base, grads, wa, wb)


GROUP = ("dp", "tensor")


def plan(dp):
    if dp == 16:
        return (8, 4, 1, 2), (8, 4, 2, 1)
    bits = [1 << i for i in range(dp.bit_length() - 1)]
    side = len(bits) // 3
    x, y, z = bits[:side], bits[side:2 * side], bits[2 * side:]
    return tuple(z[::-1] + x[::-1] + y[::-1]), tuple(z[::-1] + y[::-1] + x[::-1])


def flip(value, dp, masks):
    pairs = [(d * 2 + t, (d ^ masks[t]) * 2 + t) for d in range(dp) for t in range(2)]
    return lax.ppermute(value, GROUP, pairs)


def swap(value):
    return lax.ppermute(value, "tensor", [(0, 1), (1, 0)])


def gather(own, dp):
    held = own[None]
    for masks in zip(*plan(dp)):
        held = jnp.concatenate([held, flip(held, dp, masks)], axis=0)
    return held


def places(dp, mine, tensor):
    rel = jnp.arange(dp, dtype=jnp.int32) ^ mine
    found = []
    for order in plan(dp):
        found.append(sum(((rel & mask) // mask) << i for i, mask in enumerate(order)))
    return jnp.stack([jnp.where(tensor == t, found[0], found[1]) for t in (0, 1)])


def reduce(keep, send, dp):
    held = add(keep, swap(send))
    phases = list(zip(*plan(dp)))[::-1]
    for i, masks in enumerate(phases):
        half = held.shape[0] // 2
        arrived = flip(held[half:], dp, masks)
        held = add(held[:half], arrived, F32 if i == len(phases) - 1 else BF)
    return held[0]


def add(a, b, kind=BF):
    return (a.astype(F32) + b.astype(F32)).astype(kind)


def body(embedded, piece_lengths, pair_tags, pair_embedding, w_query, w_key, w_value, w_output, w_hidden,
         w_down, first_gain, first_shift, second_gain, second_shift, cotangent):
    dp = lax.axis_size("dp")
    mine, tensor = lax.axis_index("dp"), lax.axis_index("tensor")
    rows = D // dp
    blocked = rows % 16 == 0
    pieces = lax.dynamic_index_in_dim(piece_lengths, tensor, 0, keepdims=False)
    tag = lax.dynamic_index_in_dim(pair_tags, tensor, 0, keepdims=True)
    small = jnp.stack([first_gain, first_shift, second_gain, second_shift], axis=1)
    small = jnp.concatenate([small, pair_embedding.T, jnp.zeros((rows, 120), BF)], axis=1)
    first = gather(jnp.concatenate([w_query, w_key, w_value, small], axis=1), dp)
    rest = gather(jnp.concatenate([w_output.T, w_hidden, w_down.T], axis=1), dp)
    at = places(dp, mine, tensor)

    def arranged(held):
        both = held, swap(held)
        if blocked:
            return both
        return tuple(h[at[i]].reshape(D, -1) for i, h in enumerate(both))

    def part(width):
        return (dp, rows, width) if blocked else (D, width)

    def summed(keep, send):
        if not blocked:
            keep, send = (v.reshape(dp, rows, -1)[jnp.zeros((dp,), jnp.int32).at[at[i]].set(jnp.arange(dp))]
                          for i, v in enumerate((keep, send)))
        return reduce(keep, send, dp)

    x, low, par, wa, wb, heads = open_visit(pieces, tag, at, embedded, *arranged(first))
    (wo, wh, wd), saved, x_second, low_second, heads_second = second_visit(
        pieces, at, x, heads[3], *arranged(rest), par, wa, wb)
    result, base, gm, dd, dh, do, small_second = middle(
        pieces, x_second, heads_second[3], heads_second[5], cotangent, wo, wh, wd, par)
    grad, da, db = back(pieces, heads_second, low_second, gm, base, wa, wb)
    unit1, inv1, norm, act, slope, unit2, inv2 = saved
    total, low_total, small, *dd = down(at, part, grad, unit2, inv2, par, act, dd)
    dd = summed(*dd)
    base, gm, small, *dh = hidden_back(at, part, total, low_total, small, unit1, inv1, norm, slope, heads[5], heads[3],
                                       wo, wh, wd, par, dh, do)
    dh = summed(*dh)
    grads, *da = last_back(pieces, tag, at, part, heads, low, gm, base, wa, wb, da, db, small_second, small)
    grad = input_back(base, grads, wa, wb)
    da = summed(*da)
    small = da[:, 3 * HALF:3 * HALF + 8].T
    return (result, grad, small[4:], da[:, :HALF], da[:, HALF:2 * HALF], da[:, 2 * HALF:3 * HALF],
            dh[:, :HALF].T, dh[:, HALF:], dd.T, small[0], small[1], small[2], small[3])


def solution(mesh):
    both = P(GROUP, None)
    params = (P("dp", "tensor"),) * 3 + (P("tensor", "dp"), P("dp", "tensor"), P("tensor", "dp"))
    in_specs = (both, P("dp", None), P("dp"), P(None, "dp")) + params + (P("dp"),) * 4 + (both,)
    out_specs = (both, both, P(None, "dp")) + params + (P("dp"),) * 4
    return jax.shard_map(body, mesh=mesh, in_specs=in_specs, out_specs=out_specs, check_vma=False)
```

time: 571 us -> 293 us (0.51)
  Pallas kernels: 416 us -> 155 us
  starting transfers between devices: 23.4 us -> 55.5 us
  local copies, waits for them, and re-layouts: 35.9 us -> 12.6 us
  other arithmetic: 27.4 us -> 7.51 us
    pallas_call x14 -> x8, Pallas kernels: 416 us -> 155 us  [the longest x7 148 us: call(): pl.pallas_call(kernel, in_specs=[SMEM] * smem + [ANY] * (len(args) - smem...]
    ppermute x16 -> x20, starting transfers between devices: 23.1 us -> 54.7 us  [flip(): return lax.ppermute(value, GROUP, pairs)]
    gather x4 -> x0, local copies, waits for them, and re-layouts: 7.41 us -> none  [blocks(): return value.reshape(dp, rows, -1)[back]]
    ppermute x16 -> x20, waiting for transfers between devices: 58.8 us -> 54.1 us  [flip(): return lax.ppermute(value, GROUP, pairs)]
  transfers between devices with their start and end apart: 20 -> 25, of which waited for: 12 -> 16; matrix products, arithmetic and copies ran while one was open for 9% -> 6% of each run, Pallas kernels for 22% -> 9%
where the time goes in v2:
time: 293 us; the launch traced here: 289 us
  Pallas kernels  155 us (53%)
  waiting for transfers between devices  57.4 us (20%)
  starting transfers between devices  55.5 us (19%)
  local copies, waits for them, and re-layouts  12.6 us (4%)
  other arithmetic  7.51 us (3%)
    pallas_call x7, Pallas kernels, call(): pl.pallas_call(kernel, in_specs=[SMEM] * smem + [ANY] * (len(args) - smem...  148 us
    ppermute x20, starting transfers between devices, flip(): return lax.ppermute(value, GROUP, pairs)  54.7 us
    ppermute x20, waiting for transfers between devices, flip(): return lax.ppermute(value, GROUP, pairs)  54.1 us
    pallas_call x1, Pallas kernels, input_back(): pl.pallas_call(input_kernel, out_shape=jax.ShapeDtypeStruct((LEN, D), F32...  6.66 us
  transfers between devices with their start and end apart: 25, of which 16 were waited for; matrix products, arithmetic and copies ran while one was open for 6% of the time, Pallas kernels for 9%

profile of v2, /device:TPU:0, one launch (start us, length us, event | category | flops | bytes accessed | tf_op | source)
XLA Modules:
  0.0 289.1 jit_solution(10281569992974670451)
XLA Ops:
  1.7 4.1 %collective-permute-start.5 = (bf16[1,32,2304]{2,1,0:T(8,128)(2,1)S(1)}, bf16[1,32,2304]{2,1,0:T(8,128)(2,1)S(1)}, u32[]{:S(2)}, u32[]{:S(2)}) collective-permute-start(bf16[1,32,2304]{2,1,0:T(8,128)(2,1)S(1)} %maximum_bitcast_fusion), channel_id=1, source_target_pairs={{0,16},{1,17},{2,18},{3,19},{4,20},{5,21},{6,22},{7,23},{8,24},{9,... | collective-permute-start | bytes 442376 | tf_op jit(solution)/shard_map/ppermute | solution.py:813
  5.8 7.0 %collective-permute-done.5 = bf16[1,32,2304]{2,1,0:T(8,128)(2,1)S(1)} collective-permute-done((bf16[1,32,2304]{2,1,0:T(8,128)(2,1)S(1)}, bf16[1,32,2304]{2,1,0:T(8,128)(2,1)S(1)}, u32[]{:S(2)}, u32[]{:S(2)}) %collective-permute-start.5) | collective-permute-done | bytes 147488 | tf_op jit(solution)/shard_map/ppermute | solution.py:813
  13.6 7.5 %collective-permute-done.6 = bf16[2,32,2304]{2,1,0:T(8,128)(2,1)S(1)} collective-permute-done((bf16[2,32,2304]{2,1,0:T(8,128)(2,1)S(1)}, bf16[2,32,2304]{2,1,0:T(8,128)(2,1)S(1)}, u32[]{:S(2)}, u32[]{:S(2)}) %collective-permute-start.6) | collective-permute-done | bytes 294944 | tf_op jit(solution)/shard_map/ppermute | solution.py:813
  25.1 3.4 %collective-permute-start = (bf16[1,32,896]{2,1,0:T(8,128)(2,1)S(1)}, bf16[1,32,896]{2,1,0:T(8,128)(2,1)S(1)}, u32[]{:S(2)}, u32[]{:S(2)}) collective-permute-start(bf16[1,32,896]{2,1,0:T(8,128)(2,1)S(1)} %bitcast.27), channel_id=1, source_target_pairs={{0,16},{1,17},{2,18},{3,19},{4,20},{5,21},{6,22},{7,23},{8,24},{9,... | collective-permute-start | bytes 172040 | tf_op jit(solution)/shard_map/ppermute | solution.py:813
  29.2 1.9 collective-permute-done.7
  32.6 1.8 collective-permute-start.1
  35.0 2.4 collective-permute-done.1
  40.7 9.3 %collective-permute-done.8 = bf16[8,32,2304]{2,1,0:T(8,128)(2,1)S(1)} collective-permute-done((bf16[8,32,2304]{2,1,0:T(8,128)(2,1)S(1)}, bf16[8,32,2304]{2,1,0:T(8,128)(2,1)S(1)}, u32[]{:S(2)}, u32[]{:S(2)}) %collective-permute-start.8) | collective-permute-done | bytes 1179680 | tf_op jit(solution)/shard_map/ppermute | solution.py:813
  52.5 7.1 %collective-permute-done.3 = bf16[8,32,896]{2,1,0:T(8,128)(2,1)S(1)} collective-permute-done((bf16[8,32,896]{2,1,0:T(8,128)(2,1)S(1)}, bf16[8,32,896]{2,1,0:T(8,128)(2,1)S(1)}, u32[]{:S(2)}, u32[]{:S(2)}) %collective-permute-start.3) | collective-permute-done | bytes 458784 | tf_op jit(solution)/shard_map/ppermute | solution.py:813
  63.2 17.9 %shard_map.246 = (f32[1024,512]{1,0:T(8,128)}, bf16[1024,512]{1,0:T(8,128)(2,1)}, f32[8,512]{1,0:T(8,128)}, bf16[512,768]{1,0:T(8,128)(2,1)}, bf16[512,768]{1,0:...) custom-call(s32[8]{0:T(128)} %dynamic-slice_bitcast_fusion.pieces_re, ...), custom_call_target="tpu_custom_call" | custom-call | flops 7000000000 | bytes 8388608 | tf_op jit(solution)/shard_map/pallas_call | solution.py:486
  81.2 31.2 %shard_map.247 = (bf16[512,512]{1,0:T(8,128)(2,1)}, bf16[512,2048]{1,0:T(8,128)(2,1)}, bf16[512,2048]{1,0:T(8,128)(2,1)}, bf16[1024,512]{1,0:T(8,128)(2,1)}, f32...) custom-call(s32[8]{0:T(128)} %dynamic-slice_bitcast_fusion.pieces_re, ...), custom_call_target="tpu_custom_call" | custom-call | flops 12000000000 | bytes 8388608 | tf_op jit(solution)/shard_map/pallas_call | solution.py:486
  112.4 28.7 %shard_map.248 = (f32[1024,512]{1,0:T(8,128)}, f32[1024,512]{1,0:T(8,128)}, bf16[1024,512]{1,0:T(8,128)(2,1)}, bf16[512,2048]{1,0:T(8,128)(2,1)}, bf16[512,2048]...) custom-call(s32[8]{0:T(128)} %dynamic-slice_bitcast_fusion.pieces_ref, ...), custom_call_target="tpu_custom_call" | custom-call | flops 20000000000 | bytes 8388608 | tf_op jit(solution)/shard_map/pallas_call | solution.py:486
  141.1 19.3 %shard_map.249 = (f32[1024,512]{1,0:T(8,128)}, bf16[512,768]{1,0:T(8,128)(2,1)}, bf16[512,768]{1,0:T(8,128)(2,1)}) custom-call(s32[8]{0:T(128)} %dynamic-slice_bitcast_fusion.pieces_ref, bf16[1024,512]{1,0:T(8,128)(2,1)} %get-tuple-element.79.q_ref, bf16[1024,512]{1,0:T(8,128)(2,1)} %get-tuple-element.80.k_ref, bf16[1024,512]{1,0:T(8,128)(2,1)} %get-tuple-element.81.v_ref, ...), custom_call_target="tpu_custom_call" | custom-call | flops 14000000000 | bytes 8388608 | tf_op jit(solution)/shard_map/pallas_call | solution.py:486
  160.4 10.3 %shard_map.250 = (f32[1024,512]{1,0:T(8,128)}, bf16[1024,512]{1,0:T(8,128)(2,1)}, f32[32,512]{1,0:T(8,128)}, bf16[16,32,1024]{2,1,0:T(8,128)(2,1)}, bf16[16,32,1024]{2,1,0:T(8,128)(2,1)}) custom-call(s32[2,16]{1,0:T(2,128)} %pad_add_fusion.at_ref.to_ref, f32[1024,512]{1,0:T(8,128)} %get-tuple-element.87.grad_ref, ...), custom_call_target="tpu_custom_call" | custom-call | flops 3000000000 | bytes 8388608 | tf_op jit(solution)/shard_map/pallas_call | solution.py:486
  170.7 19.8 %shard_map.251 = (f32[1024,512]{1,0:T(8,128)}, bf16[1024,512]{1,0:T(8,128)(2,1)}, f32[32,512]{1,0:T(8,128)}, bf16[16,32,1280]{2,1,0:T(8,128)(2,1)}, bf16[16,32,1280]{2,1,0:T(8,128)(2,1)}) custom-call(s32[2,16]{1,0:T(2,128)} %pad_add_fusion.at_ref.to_ref, f32[1024,512]{1,0:T(8,128)} %get-tuple-element.92.total_ref, ...), custom_call_target="tpu_custom_call" | custom-call | flops 12000000000 | bytes 8388608 | tf_op jit(solution)/shard_map/pallas_call | solution.py:486
  190.5 20.9 %shard_map.252 = (bf16[1024,1536]{1,0:T(8,128)(2,1)}, bf16[16,32,896]{2,1,0:T(8,128)(2,1)}, bf16[16,32,896]{2,1,0:T(8,128)(2,1)}) custom-call(s32[8]{0:T(128)} %dynamic-slice_bitcast_fusion.pieces_ref, s32[1]{0:T(128)} %dynamic_slice.9.tag_ref, s32[2,16]{1,0:T(2,128)} %pad_add_fusion.at_ref.to_ref, bf16[1024,512]{1,0:T(8,128)(2,1)} %get-tuple-element.103.q_ref, ...), custom_call_target="tpu_custom_call" | custom-call | flops 12000000000 | bytes 8388608 | tf_op jit(solution)/shard_map/pallas_call | solution.py:486
  212.2 2.6 collective-permute-done.10
  216.2 16.9 %collective-permute-start.11 = (bf16[8,32,896]{2,1,0:T(8,128)(2,1)S(1)}, bf16[8,32,896]{2,1,0:T(8,128)(2,1)S(1)}, u32[]{:S(2)}, u32[]{:S(2)}) collective-permute-start(bf16[8,32,896]{2,1,0:T(8,128)(2,1)S(1)} %slice.141), channel_id=1, source_target_pairs={{0,4},{1,3},{2,6},{3,1},{4,0},{5,7},{6,2},{7,5},{8,12},{9,11},{10,... | collective-permute-start | bytes 1376264 | tf_op jit(solution)/shard_map/ppermute | solution.py:813
  233.1 6.7 %shard_map.253 = f32[1024,512]{1,0:T(8,128)} custom-call(f32[1024,512]{1,0:T(8,128)} %get-tuple-element.102.base_ref, bf16[1024,1536]{1,0:T(8,128)(2,1)} %get-tuple-element.114.grads_ref, bf16[512,768]{1,0:T(8,128)(2,1)} %get-tuple-element.70.wa_ref, bf16[512,768]{1,0:T(8,128)(2,1)} %get-tuple-element.71.wb_ref), custom_call_target="tpu_custom_call" | custom-call | flops 1600000000 | bytes 9437184 | tf_op jit(solution)/shard_map/pallas_call | solution.py:791
  241.2 1.7 add_convert_fusion.1
  243.0 1.6 collective-permute-start.21
  244.6 2.1 collective-permute-done.12
  246.8 3.6 %collective-permute-start.13 = (bf16[2,32,896]{2,1,0:T(8,128)(2,1)S(1)}, bf16[2,32,896]{2,1,0:T(8,128)(2,1)S(1)}, u32[]{:S(2)}, u32[]{:S(2)}) collective-permute-start(bf16[2,32,896]{2,1,0:T(8,128)(2,1)S(1)} %slice.145), channel_id=1, source_target_pairs={{0,8},{1,9},{2,10},{3,11},{4,12},{5,13},{6,14},{7,15},{8,0},{9,1},... | collective-permute-start | bytes 344072 | tf_op jit(solution)/shard_map/ppermute | solution.py:813
  250.9 2.3 collective-permute-done.13
  253.2 5.1 %collective-permute-start.14 = (bf16[1,32,896]{2,1,0:T(8,128)(2,1)S(1)}, bf16[1,32,896]{2,1,0:T(8,128)(2,1)S(1)}, u32[]{:S(2)}, u32[]{:S(2)}) collective-permute-start(bf16[1,32,896]{2,1,0:T(8,128)(2,1)S(1)} %slice.147), channel_id=1, source_target_pairs={{0,16},{1,17},{2,18},{3,19},{4,20},{5,21},{6,22},{7,23},{8,24},{9,... | collective-permute-start | bytes 172040 | tf_op jit(solution)/shard_map/ppermute | solution.py:813
  261.8 3.9 %collective-permute-done.16 = bf16[8,32,1280]{2,1,0:T(8,128)(2,1)S(1)} collective-permute-done((bf16[8,32,1280]{2,1,0:T(8,128)(2,1)S(1)}, bf16[8,32,1280]{2,1,0:T(8,128)(2,1)S(1)}, u32[]{:S(2)}, u32[]{:S(2)}) %collective-permute-start.16) | collective-permute-done | bytes 655392 | tf_op jit(solution)/shard_map/ppermute | solution.py:813
  265.9 4.3 %collective-permute-start.17 = (bf16[4,32,1280]{2,1,0:T(8,128)(2,1)S(1)}, bf16[4,32,1280]{2,1,0:T(8,128)(2,1)S(1)}, u32[]{:S(2)}, u32[]{:S(2)}) collective-permute-start(bf16[4,32,1280]{2,1,0:T(8,128)(2,1)S(1)} %slice.156), channel_id=1, source_target_pairs={{0,2},{1,5},{2,0},{3,7},{4,6},{5,1},{6,4},{7,3},{8,10},{9,13},{10,... | collective-permute-start | bytes 983048 | tf_op jit(solution)/shard_map/ppermute | solution.py:813
  271.1 4.1 %collective-permute-done.17 = bf16[4,32,1280]{2,1,0:T(8,128)(2,1)S(1)} collective-permute-done((bf16[4,32,1280]{2,1,0:T(8,128)(2,1)S(1)}, bf16[4,32,1280]{2,1,0:T(8,128)(2,1)S(1)}, u32[]{:S(2)}, u32[]{:S(2)}) %collective-permute-start.17) | collective-permute-done | bytes 327712 | tf_op jit(solution)/shard_map/ppermute | solution.py:813
  276.1 3.1 %collective-permute-start.24 = (bf16[1,32,1024]{2,1,0:T(8,128)(2,1)S(1)}, bf16[1,32,1024]{2,1,0:T(8,128)(2,1)S(1)}, u32[]{:S(2)}, u32[]{:S(2)}) collective-permute-start(bf16[1,32,1024]{2,1,0:T(8,128)(2,1)S(1)} %slice.170), channel_id=1, source_target_pairs={{0,16},{1,17},{2,18},{3,19},{4,20},{5,21},{6,22},{7,23},{8,24},{9,... | collective-permute-start | bytes 196616 | tf_op jit(solution)/shard_map/ppermute | solution.py:813
  279.2 2.9 %collective-permute-done.18 = bf16[2,32,1280]{2,1,0:T(8,128)(2,1)S(1)} collective-permute-done((bf16[2,32,1280]{2,1,0:T(8,128)(2,1)S(1)}, bf16[2,32,1280]{2,1,0:T(8,128)(2,1)S(1)}, u32[]{:S(2)}, u32[]{:S(2)}) %collective-permute-start.18) | collective-permute-done | bytes 163872 | tf_op jit(solution)/shard_map/ppermute | solution.py:813
  282.2 2.3 collective-permute-start.19
  285.2 2.4 collective-permute-done.19
  (118 shorter events, 29.4 us)
Async XLA Ops:
  0.6 59.9 %copy-start = (s32[2,8]{1,0:T(2,128)S(1)}, s32[2,8]{1,0:T(2,128)}, u32[]{:S(2)}) copy-start(s32[2,8]{1,0:T(2,128)} %param.16) | copy-start | bytes 196
  0.7 27.8 %copy-start.5 = (bf16[32,1024]{1,0:T(8,128)(2,1)S(1)}, bf16[32,1024]{1,0:T(8,128)(2,1)}, u32[]{:S(2)}) copy-start(bf16[32,1024]{1,0:T(8,128)(2,1)} %param.23) | copy-start | bytes 196612
  0.7 27.8 %copy-start.4 = (bf16[1024,32]{0,1:T(8,128)(2,1)S(1)}, bf16[1024,32]{0,1:T(8,128)(2,1)}, u32[]{:S(2)}) copy-start(bf16[1024,32]{0,1:T(8,128)(2,1)} %param.24) | copy-start | bytes 196612
  0.7 27.8 %copy-start.6 = (bf16[256,32]{0,1:T(8,128)(2,1)S(1)}, bf16[256,32]{0,1:T(8,128)(2,1)}, u32[]{:S(2)}) copy-start(bf16[256,32]{0,1:T(8,128)(2,1)} %param.22) | copy-start | bytes 49156
  0.7 24.3 %copy-start.9 = (bf16[32,256]{1,0:T(8,128)(2,1)S(1)}, bf16[32,256]{1,0:T(8,128)(2,1)}, u32[]{:S(2)}) copy-start(bf16[32,256]{1,0:T(8,128)(2,1)} %param.21) | copy-start | bytes 49156
  0.7 24.3 %copy-start.8 = (bf16[32,256]{1,0:T(8,128)(2,1)S(1)}, bf16[32,256]{1,0:T(8,128)(2,1)}, u32[]{:S(2)}) copy-start(bf16[32,256]{1,0:T(8,128)(2,1)} %param.20) | copy-start | bytes 49156
  0.7 24.3 %copy-start.7 = (bf16[32,256]{1,0:T(8,128)(2,1)S(1)}, bf16[32,256]{1,0:T(8,128)(2,1)}, u32[]{:S(2)}) copy-start(bf16[32,256]{1,0:T(8,128)(2,1)} %param.19) | copy-start | bytes 49156
  1.7 11.1 %collective-permute-start.5 = (bf16[1,32,2304]{2,1,0:T(8,128)(2,1)S(1)}, bf16[1,32,2304]{2,1,0:T(8,128)(2,1)S(1)}, u32[]{:S(2)}, u32[]{:S(2)}) collective-permute-start(bf16[1,32,2304]{2,1,0:T(8,128)(2,1)S(1)} %maximum_bitcast_fusion), channel_id=1, source_target_pairs={{0,16},{1,17},{2,18},{3,19},{4,20},{5,21},{6,22},{7,23},{8,24},{9,... | collective-permute-start | bytes 442376 | tf_op jit(solution)/shard_map/ppermute | solution.py:813
  12.9 8.3 %collective-permute-start.6 = (bf16[2,32,2304]{2,1,0:T(8,128)(2,1)S(1)}, bf16[2,32,2304]{2,1,0:T(8,128)(2,1)S(1)}, u32[]{:S(2)}, u32[]{:S(2)}) collective-permute-start(bf16[2,32,2304]{2,1,0:T(8,128)(2,1)S(1)} %pad_maximum_fusion.3), channel_id=1, source_target_pairs={{0,8},{1,9},{2,10},{3,11},{4,12},{5,13},{6,14},{7,15},{8,0},{9,1},... | collective-permute-start | bytes 884744 | tf_op jit(solution)/shard_map/ppermute | solution.py:813
  21.2 9.9 %collective-permute-start.7 = (bf16[4,32,2304]{2,1,0:T(8,128)(2,1)S(1)}, bf16[4,32,2304]{2,1,0:T(8,128)(2,1)S(1)}, u32[]{:S(2)}, u32[]{:S(2)}) collective-permute-start(bf16[4,32,2304]{2,1,0:T(8,128)(2,1)S(1)} %pad_maximum_fusion.1), channel_id=1, source_target_pairs={{0,2},{1,5},{2,0},{3,7},{4,6},{5,1},{6,4},{7,3},{8,10},{9,13},{10,... | collective-permute-start | bytes 1769480 | tf_op jit(solution)/shard_map/ppermute | solution.py:813
  25.1 7.5 %collective-permute-start = (bf16[1,32,896]{2,1,0:T(8,128)(2,1)S(1)}, bf16[1,32,896]{2,1,0:T(8,128)(2,1)S(1)}, u32[]{:S(2)}, u32[]{:S(2)}) collective-permute-start(bf16[1,32,896]{2,1,0:T(8,128)(2,1)S(1)} %bitcast.27), channel_id=1, source_target_pairs={{0,16},{1,17},{2,18},{3,19},{4,20},{5,21},{6,22},{7,23},{8,24},{9,... | collective-permute-start | bytes 172040 | tf_op jit(solution)/shard_map/ppermute | solution.py:813
  31.2 18.7 %collective-permute-start.8 = (bf16[8,32,2304]{2,1,0:T(8,128)(2,1)S(1)}, bf16[8,32,2304]{2,1,0:T(8,128)(2,1)S(1)}, u32[]{:S(2)}, u32[]{:S(2)}) collective-permute-start(bf16[8,32,2304]{2,1,0:T(8,128)(2,1)S(1)} %pad_maximum_fusion), channel_id=1, source_target_pairs={{0,4},{1,3},{2,6},{3,1},{4,0},{5,7},{6,2},{7,5},{8,12},{9,11},{10,... | collective-permute-start | bytes 3538952 | tf_op jit(solution)/shard_map/ppermute | solution.py:813
  32.6 4.9 %collective-permute-start.1 = (bf16[2,32,896]{2,1,0:T(8,128)(2,1)S(1)}, bf16[2,32,896]{2,1,0:T(8,128)(2,1)S(1)}, u32[]{:S(2)}, u32[]{:S(2)}) collective-permute-start(bf16[2,32,896]{2,1,0:T(8,128)(2,1)S(1)} %pad_maximum_fusion.5), channel_id=1, source_target_pairs={{0,8},{1,9},{2,10},{3,11},{4,12},{5,13},{6,14},{7,15},{8,0},{9,1},... | collective-permute-start | bytes 344072 | tf_op jit(solution)/shard_map/ppermute | solution.py:813
  37.5 13.6 %collective-permute-start.2 = (bf16[4,32,896]{2,1,0:T(8,128)(2,1)S(1)}, bf16[4,32,896]{2,1,0:T(8,128)(2,1)S(1)}, u32[]{:S(2)}, u32[]{:S(2)}) collective-permute-start(bf16[4,32,896]{2,1,0:T(8,128)(2,1)S(1)} %pad_maximum_fusion.4), channel_id=1, source_target_pairs={{0,2},{1,5},{2,0},{3,7},{4,6},{5,1},{6,4},{7,3},{8,10},{9,13},{10,... | collective-permute-start | bytes 688136 | tf_op jit(solution)/shard_map/ppermute | solution.py:813
  51.1 30.1 %collective-permute-start.9 = (bf16[16,32,2304]{2,1,0:T(8,128)(2,1)}, bf16[16,32,2304]{2,1,0:T(8,128)(2,1)}, u32[]{:S(2)}, u32[]{:S(2)}) collective-permute-start(bf16[16,32,2304]{2,1,0:T(8,128)(2,1)} %constant_dynamic-update-slice_fusion.5.own_ref), channel_id=1, source_target_pairs={{0,1},{1,0},{2,3},{3,2},{4,5},{5,4},{6,7},{7,6},{8,9},{9,8},{10,11... | collective-permute-start | bytes 7077896 | tf_op jit(solution)/shard_map/ppermute | solution.py:817
  51.1 8.5 %collective-permute-start.3 = (bf16[8,32,896]{2,1,0:T(8,128)(2,1)S(1)}, bf16[8,32,896]{2,1,0:T(8,128)(2,1)S(1)}, u32[]{:S(2)}, u32[]{:S(2)}) collective-permute-start(bf16[8,32,896]{2,1,0:T(8,128)(2,1)S(1)} %pad_maximum_fusion.2), channel_id=1, source_target_pairs={{0,4},{1,3},{2,6},{3,1},{4,0},{5,7},{6,2},{7,5},{8,12},{9,11},{10,... | collective-permute-start | bytes 1376264 | tf_op jit(solution)/shard_map/ppermute | solution.py:813
  59.7 2.5 collective-permute-start.4
  211.5 3.3 %collective-permute-start.10 = (bf16[16,32,896]{2,1,0:T(8,128)(2,1)}, bf16[16,32,896]{2,1,0:T(8,128)(2,1)S(1)}, u32[]{:S(2)}, u32[]{:S(2)}) collective-permute-start(bf16[16,32,896]{2,1,0:T(8,128)(2,1)} %get-tuple-element.116), channel_id=1, source_target_pairs={{0,1},{1,0},{2,3},{3,2},{4,5},{5,4},{6,7},{7,6},{8,9},{9,8},{10,11... | collective-permute-start | bytes 2752520 | tf_op jit(solution)/shard_map/ppermute | solution.py:817
  211.6 29.6 %collective-permute-start.20 = (bf16[16,32,1024]{2,1,0:T(8,128)(2,1)}, bf16[16,32,1024]{2,1,0:T(8,128)(2,1)}, u32[]{:S(2)}, u32[]{:S(2)}) collective-permute-start(bf16[16,32,1024]{2,1,0:T(8,128)(2,1)} %get-tuple-element.120), channel_id=1, source_target_pairs={{0,1},{1,0},{2,3},{3,2},{4,5},{5,4},{6,7},{7,6},{8,9},{9,8},{10,11... | collective-permute-start | bytes 3145736 | tf_op jit(solution)/shard_map/ppermute | solution.py:817
  212.1 38.3 %collective-permute-start.15 = (bf16[16,32,1280]{2,1,0:T(8,128)(2,1)}, bf16[16,32,1280]{2,1,0:T(8,128)(2,1)S(1)}, u32[]{:S(2)}, u32[]{:S(2)}) collective-permute-start(bf16[16,32,1280]{2,1,0:T(8,128)(2,1)} %get-tuple-element.118), channel_id=1, source_target_pairs={{0,1},{1,0},{2,3},{3,2},{4,5},{5,4},{6,7},{7,6},{8,9},{9,8},{10,11... | collective-permute-start | bytes 3932168 | tf_op jit(solution)/shard_map/ppermute | solution.py:817
  216.2 23.6 %collective-permute-start.11 = (bf16[8,32,896]{2,1,0:T(8,128)(2,1)S(1)}, bf16[8,32,896]{2,1,0:T(8,128)(2,1)S(1)}, u32[]{:S(2)}, u32[]{:S(2)}) collective-permute-start(bf16[8,32,896]{2,1,0:T(8,128)(2,1)S(1)} %slice.141), channel_id=1, source_target_pairs={{0,4},{1,3},{2,6},{3,1},{4,0},{5,7},{6,2},{7,5},{8,12},{9,11},{10,... | collective-permute-start | bytes 1376264 | tf_op jit(solution)/shard_map/ppermute | solution.py:813
  239.9 6.8 %collective-permute-start.12 = (bf16[4,32,896]{2,1,0:T(8,128)(2,1)S(1)}, bf16[4,32,896]{2,1,0:T(8,128)(2,1)S(1)}, u32[]{:S(2)}, u32[]{:S(2)}) collective-permute-start(bf16[4,32,896]{2,1,0:T(8,128)(2,1)S(1)} %slice.143), channel_id=1, source_target_pairs={{0,2},{1,5},{2,0},{3,7},{4,6},{5,1},{6,4},{7,3},{8,10},{9,13},{10,... | collective-permute-start | bytes 688136 | tf_op jit(solution)/shard_map/ppermute | solution.py:813
  243.0 15.3 %collective-permute-start.21 = (bf16[8,32,1024]{2,1,0:T(8,128)(2,1)S(1)}, bf16[8,32,1024]{2,1,0:T(8,128)(2,1)S(1)}, u32[]{:S(2)}, u32[]{:S(2)}) collective-permute-start(bf16[8,32,1024]{2,1,0:T(8,128)(2,1)S(1)} %slice.164), channel_id=1, source_target_pairs={{0,4},{1,3},{2,6},{3,1},{4,0},{5,7},{6,2},{7,5},{8,12},{9,11},{10,... | collective-permute-start | bytes 1572872 | tf_op jit(solution)/shard_map/ppermute | solution.py:813
  246.8 6.4 %collective-permute-start.13 = (bf16[2,32,896]{2,1,0:T(8,128)(2,1)S(1)}, bf16[2,32,896]{2,1,0:T(8,128)(2,1)S(1)}, u32[]{:S(2)}, u32[]{:S(2)}) collective-permute-start(bf16[2,32,896]{2,1,0:T(8,128)(2,1)S(1)} %slice.145), channel_id=1, source_target_pairs={{0,8},{1,9},{2,10},{3,11},{4,12},{5,13},{6,14},{7,15},{8,0},{9,1},... | collective-permute-start | bytes 344072 | tf_op jit(solution)/shard_map/ppermute | solution.py:813
  250.8 14.9 %collective-permute-start.16 = (bf16[8,32,1280]{2,1,0:T(8,128)(2,1)S(1)}, bf16[8,32,1280]{2,1,0:T(8,128)(2,1)S(1)}, u32[]{:S(2)}, u32[]{:S(2)}) collective-permute-start(bf16[8,32,1280]{2,1,0:T(8,128)(2,1)S(1)} %slice.154), channel_id=1, source_target_pairs={{0,4},{1,3},{2,6},{3,1},{4,0},{5,7},{6,2},{7,5},{8,12},{9,11},{10,... | collective-permute-start | bytes 1966088 | tf_op jit(solution)/shard_map/ppermute | solution.py:813
  253.2 7.2 %collective-permute-start.14 = (bf16[1,32,896]{2,1,0:T(8,128)(2,1)S(1)}, bf16[1,32,896]{2,1,0:T(8,128)(2,1)S(1)}, u32[]{:S(2)}, u32[]{:S(2)}) collective-permute-start(bf16[1,32,896]{2,1,0:T(8,128)(2,1)S(1)} %slice.147), channel_id=1, source_target_pairs={{0,16},{1,17},{2,18},{3,19},{4,20},{5,21},{6,22},{7,23},{8,24},{9,... | collective-permute-start | bytes 172040 | tf_op jit(solution)/shard_map/ppermute | solution.py:813
  259.2 11.7 %collective-permute-start.22 = (bf16[4,32,1024]{2,1,0:T(8,128)(2,1)}, bf16[4,32,1024]{2,1,0:T(8,128)(2,1)S(1)}, u32[]{:S(2)}, u32[]{:S(2)}) collective-permute-start(bf16[4,32,1024]{2,1,0:T(8,128)(2,1)} %slice.166), channel_id=1, source_target_pairs={{0,2},{1,5},{2,0},{3,7},{4,6},{5,1},{6,4},{7,3},{8,10},{9,13},{10,... | collective-permute-start | bytes 786440 | tf_op jit(solution)/shard_map/ppermute | solution.py:813
  265.9 9.3 %collective-permute-start.17 = (bf16[4,32,1280]{2,1,0:T(8,128)(2,1)S(1)}, bf16[4,32,1280]{2,1,0:T(8,128)(2,1)S(1)}, u32[]{:S(2)}, u32[]{:S(2)}) collective-permute-start(bf16[4,32,1280]{2,1,0:T(8,128)(2,1)S(1)} %slice.156), channel_id=1, source_target_pairs={{0,2},{1,5},{2,0},{3,7},{4,6},{5,1},{6,4},{7,3},{8,10},{9,13},{10,... | collective-permute-start | bytes 983048 | tf_op jit(solution)/shard_map/ppermute | solution.py:813
  271.0 5.0 %collective-permute-start.23 = (bf16[2,32,1024]{2,1,0:T(8,128)(2,1)S(1)}, bf16[2,32,1024]{2,1,0:T(8,128)(2,1)S(1)}, u32[]{:S(2)}, u32[]{:S(2)}) collective-permute-start(bf16[2,32,1024]{2,1,0:T(8,128)(2,1)S(1)} %slice.168), channel_id=1, source_target_pairs={{0,8},{1,9},{2,10},{3,11},{4,12},{5,13},{6,14},{7,15},{8,0},{9,1},... | collective-permute-start | bytes 393224 | tf_op jit(solution)/shard_map/ppermute | solution.py:813
  275.3 6.8 %collective-permute-start.18 = (bf16[2,32,1280]{2,1,0:T(8,128)(2,1)S(1)}, bf16[2,32,1280]{2,1,0:T(8,128)(2,1)S(1)}, u32[]{:S(2)}, u32[]{:S(2)}) collective-permute-start(bf16[2,32,1280]{2,1,0:T(8,128)(2,1)S(1)} %slice.158), channel_id=1, source_target_pairs={{0,8},{1,9},{2,10},{3,11},{4,12},{5,13},{6,14},{7,15},{8,0},{9,1},... | collective-permute-start | bytes 491528 | tf_op jit(solution)/shard_map/ppermute | solution.py:813
  276.1 8.4 %collective-permute-start.24 = (bf16[1,32,1024]{2,1,0:T(8,128)(2,1)S(1)}, bf16[1,32,1024]{2,1,0:T(8,128)(2,1)S(1)}, u32[]{:S(2)}, u32[]{:S(2)}) collective-permute-start(bf16[1,32,1024]{2,1,0:T(8,128)(2,1)S(1)} %slice.170), channel_id=1, source_target_pairs={{0,16},{1,17},{2,18},{3,19},{4,20},{5,21},{6,22},{7,23},{8,24},{9,... | collective-permute-start | bytes 196616 | tf_op jit(solution)/shard_map/ppermute | solution.py:813
  282.2 5.4 %collective-permute-start.19 = (bf16[1,32,1280]{2,1,0:T(8,128)(2,1)S(1)}, bf16[1,32,1280]{2,1,0:T(8,128)(2,1)S(1)}, u32[]{:S(2)}, u32[]{:S(2)}) collective-permute-start(bf16[1,32,1280]{2,1,0:T(8,128)(2,1)S(1)} %slice.160), channel_id=1, source_target_pairs={{0,16},{1,17},{2,18},{3,19},{4,20},{5,21},{6,22},{7,23},{8,24},{9,... | collective-permute-start | bytes 245768 | tf_op jit(solution)/shard_map/ppermute | solution.py:813
  (8 other events, 100.3 us)

commit v3 on v2

v3 whole, which is shorter than its diff:
```python
import functools
import math

import jax
import jax.numpy as jnp
from jax import lax
from jax.sharding import PartitionSpec as P
from jax.experimental import pallas as pl
from jax.experimental.pallas import tpu as pltpu

HEAD_DIM = 64
LEN = 1024
PIECES = 8
PAIRS = 4
D = 512
FF = 2048
HALF = 256
HEADS2 = 4
QB = 256
KB = 128
NQ = LEN // QB
NK = LEN // KB
BIG = 1e30
LOG2E = math.log2(math.e)
QSCALE = LOG2E / math.sqrt(HEAD_DIM)
KSCALE = math.log(2.0)
WIDTHS = (2, 3, 4, 5, 6, 7, 8)
EPS = 1e-5
C1 = math.sqrt(2.0 / math.pi)
C2 = C1 * 0.044715
F32 = jnp.float32
BF = jnp.bfloat16
VMEM_LIMIT = 60 * 1024 * 1024
TM = 256


def nn(a, b):
    return jnp.dot(a, b, preferred_element_type=F32)


def nt(a, b):
    return lax.dot_general(a, b, (((1,), (1,)), ((), ())), preferred_element_type=F32)


def tn(a, b):
    return lax.dot_general(a, b, (((0,), (0,)), ((), ())), preferred_element_type=F32)


def piece_ends(pieces_ref):
    ends, at = [], 0
    for j in range(PIECES):
        at = at + pieces_ref[j]
        ends.append(at)
    return ends


def window(block, ends):
    first = block * QB
    last = first + QB - 1
    low, high = jnp.int32(0), jnp.int32(LEN)
    for end in ends[:-1]:
        low = jnp.maximum(low, jnp.where(end <= first, end, 0))
        high = jnp.minimum(high, jnp.where(end > last, end, LEN))
    low = jnp.where(first >= ends[-2], first, low)
    high = jnp.where(last >= ends[-2], last + 1, high)
    return low // KB, (high + KB - 1) // KB


def over_widths(block, ends, run):
    low, high = window(block, ends)
    count = high - low
    previous = 0
    for wide in WIDTHS:
        begin = jnp.minimum(low, NK - wide)

        @pl.when((count > previous) & (count <= wide))
        def _(wide=wide, begin=begin):
            run(wide, pl.multiple_of(begin * KB, KB))

        previous = wide


def segment_codes(ends, segq_ref, segk_ref):
    rows = lax.broadcasted_iota(jnp.int32, (LEN, 128), 0)
    lanes = lax.broadcasted_iota(jnp.int32, (LEN, 128), 1)
    ids = jnp.zeros((LEN, 128), jnp.int32)
    for end in ends[:-1]:
        ids = ids + jnp.where(rows >= end, 1, 0)
    same = lanes == ids
    segk_ref[...] = jnp.where(same, 1.0, 0.0).astype(BF)
    free = (lanes >= PIECES) | (same & (lanes < PIECES - 1))
    segq_ref[...] = jnp.where(free, 0.0, -BIG).astype(BF)


def lane_half(shape):
    return lax.broadcasted_iota(jnp.int32, shape, 1) < HEAD_DIM


def two_heads(block):
    left = lane_half(block.shape)
    zero = jnp.zeros_like(block)
    return jnp.where(left, block, zero), jnp.where(left, zero, block)


def block_rows(index, size):
    return pl.ds(pl.multiple_of(index * size, size), size)


def head_norms(values, half):
    heads = lax.broadcasted_iota(jnp.int32, (HALF, 128), 0) // HEAD_DIM + half * (HALF // HEAD_DIM)
    pick = jnp.where(heads == lax.broadcasted_iota(jnp.int32, (HALF, 128), 1), 1.0, 0.0).astype(BF)
    return jnp.max(nn((values * values).astype(BF), pick), axis=0, keepdims=True)


def project_stage(x_ref, w_refs, q_ref, k_ref, v_ref, vt_ref):
    def chunk(i, carry):
        rows = block_rows(i, TM)
        low = x_ref[rows, :]
        q_top, k_top = carry
        for half in range(2):
            cols = slice(half * HALF, (half + 1) * HALF)
            queries = nn(low, w_refs[half][:, :HALF]) * QSCALE
            keys = nn(low, w_refs[half][:, HALF:2 * HALF])
            q_ref[rows, cols] = queries.astype(BF)
            k_ref[rows, cols] = keys.astype(BF)
            q_top = jnp.maximum(q_top, head_norms(queries, half))
            k_top = jnp.maximum(k_top, head_norms(keys, half))
            values = nn(low, w_refs[half][:, 2 * HALF:3 * HALF])
            v_ref[rows, cols] = values.astype(BF)
            for pair in range(2):
                vt_ref[half * 2 + pair, :128, rows] = values[:, pair * 128:(pair + 1) * 128].T.astype(BF)
        return q_top, k_top

    zero = jnp.zeros((1, 128), F32)
    q_top, k_top = lax.fori_loop(0, LEN // TM, chunk, (zero, zero))
    for pair in range(HEADS2):
        vt_ref[pair, 128:, :] = jnp.ones((16, LEN), BF)
    return jnp.max(q_top * k_top)


def probs_copy(p_slots, p_hbm, sem, i, wide, out):
    slot = i % 2
    here = p_slots.at[slot, :, pl.ds(0, wide * KB), :]
    there = p_hbm.at[i, :, pl.ds(0, wide * KB), :]
    return pltpu.make_async_copy(here, there, sem.at[slot]) if out else pltpu.make_async_copy(there, here, sem.at[slot])


def attend_stage(ends, shifted, resident, q_ref, k_ref, v_ref, mixed_ref, low_ref, inv_ref, vt_ref, segq_ref, segk_ref,
                 p_slots, p_out, p_sem, done):
    def block(i, carry):
        rows = block_rows(i, QB)
        p_ref = p_slots.at[i % 2]

        @pl.when(i >= 2)
        def _():
            over_widths(i - 2, ends, lambda wide, begin: probs_copy(p_slots, p_out, p_sem, i - 2, wide, True).wait())

        def run(wide, begin):
            keys = pl.ds(begin, wide * KB)
            segq = segq_ref[rows, :]
            segk = segk_ref[keys, :]
            pad = lax.broadcasted_iota(jnp.int32, (QB, 128), 0) + i * QB >= ends[-2]
            span = [slice(pair * 128, (pair + 1) * 128) for pair in range(HEADS2)]

            def score(pair):
                even, odd = two_heads(q_ref[rows, span[pair]])
                query = jnp.concatenate(
                    [jnp.concatenate([even, segq], axis=1), jnp.concatenate([odd, segq], axis=1)], axis=0)
                key = jnp.concatenate([k_ref[keys, span[pair]], segk], axis=1)
                return nt(key, query)

            def soften(pair, scores):
                if shifted:
                    scores = scores - jnp.max(scores, axis=0, keepdims=True)
                probs = jnp.exp2(scores).astype(BF)
                p_ref[pair, :wide * KB, :] = probs
                return probs

            def mix(pair, probs):
                return nn(vt_ref[pair, :, keys], probs)

            def finish(pair, out):
                cols = span[pair]
                inv = 1.0 / jnp.maximum(out[128:129, :], 1e-30)
                inv_ref[pl.ds(i * HEADS2 + pair, 1), :] = inv
                inv_both = jnp.concatenate(
                    [jnp.broadcast_to(inv[:, :QB], (64, QB)), jnp.broadcast_to(inv[:, QB:], (64, QB))], axis=0)
                exact = (jnp.concatenate([out[:64, :QB], out[64:128, QB:]], axis=0) * inv_both).T
                mixed = jnp.where(pad, v_ref[rows, cols].astype(F32), exact).astype(BF)
                mixed_ref[rows, cols] = mixed
                low_ref[rows, cols] = (exact - mixed.astype(F32)).astype(BF)

            s = {0: score(0), 1: score(1)}
            p, o = {}, {}
            for pair in range(HEADS2):
                p[pair] = soften(pair, s[pair])
                if pair + 2 < HEADS2:
                    s[pair + 2] = score(pair + 2)
                if pair:
                    o[pair - 1] = mix(pair - 1, p[pair - 1])
                if pair > 1:
                    finish(pair - 2, o[pair - 2])
            out = probs_copy(p_slots, p_out, p_sem, i, wide, True)
            if resident:
                pl.when(i < NQ - 2)(out.start)
            else:
                out.start()
            o[HEADS2 - 1] = mix(HEADS2 - 1, p[HEADS2 - 1])
            finish(HEADS2 - 2, o[HEADS2 - 2])
            finish(HEADS2 - 1, o[HEADS2 - 1])

        over_widths(i, ends, run)
        done(i, rows)
        return carry

    lax.fori_loop(0, NQ, block, 0)
    if not resident:
        for i in range(NQ - 2, NQ):
            over_widths(i, ends, lambda wide, begin, i=i: probs_copy(p_slots, p_out, p_sem, i, wide, True).wait())


def grad_columns(part, pair):
    at = pair // 2 * 3 * HALF + part * HALF + pair % 2 * 128
    return slice(at, at + 128)


def attend_back_stage(ends, resident, q_ref, k_ref, v_ref, mixed_ref, low_ref, grad_ref, kt_ref, p_in, p_slots, p_sem,
                      dk_ref, dv_ref, grads_ref, first=(), later=()):
    if not resident:
        for i in (NQ - 1, NQ - 2):
            over_widths(i, ends, lambda wide, begin, i=i: probs_copy(p_slots, p_in, p_sem, i, wide, False).start())
    dk_ref[...] = jnp.zeros_like(dk_ref)
    dv_ref[...] = jnp.zeros_like(dv_ref)
    wait(*first)
    for pair in range(HEADS2):
        kt_ref[pair, :128, :] = k_ref[:, pair * 128:(pair + 1) * 128].astype(F32).T.astype(BF)
    span = [slice(pair * 128, (pair + 1) * 128) for pair in range(HEADS2)]

    def block(j, carry):
        i = NQ - 1 - j
        rows = block_rows(i, QB)
        p_ref = p_slots.at[i % 2]

        def run(wide, begin):
            keys = pl.ds(begin, wide * KB)
            arrived = probs_copy(p_slots, p_in, p_sem, i, wide, False)
            if resident:
                pl.when(j >= 2)(arrived.wait)
            else:
                arrived.wait()

            def outer(pair):
                return jnp.concatenate(two_heads(grad_ref[rows, span[pair]]), axis=0)

            def slope(pair):
                grad = grad_ref[rows, span[pair]]
                exact = mixed_ref[rows, span[pair]].astype(F32) + low_ref[rows, span[pair]].astype(F32)
                inner = grad.astype(F32) * exact
                high = inner.astype(BF)
                rest = pltpu.roll(inner - high.astype(F32), HEAD_DIM, 1).astype(BF)
                left = lane_half(inner.shape)
                inner = jnp.concatenate([jnp.where(left, high, rest), jnp.where(left, rest, high)], axis=0)
                both = jnp.concatenate([outer(pair), inner], axis=1)
                value = jnp.concatenate([v_ref[keys, span[pair]], jnp.full((wide * KB, 128), -1.0, BF)], axis=1)
                return nt(value, both)

            def bend(pair, slope):
                return (p_ref[pair, :wide * KB, :].astype(F32) * slope).astype(BF)

            def values(pair):
                dv_ref[keys, span[pair]] += nn(p_ref[pair, :wide * KB, :], outer(pair))

            def rest(pair, scores):
                query = jnp.concatenate(two_heads(q_ref[rows, span[pair]]), axis=0)
                dk_ref[keys, span[pair]] += nn(scores, query)
                out = nn(kt_ref[pair, :128, keys], scores)
                out = jnp.concatenate([out[:64, :QB], out[64:, QB:]], axis=0)
                grads_ref[rows, grad_columns(0, pair)] = (out.T * (HEAD_DIM ** -0.5)).astype(BF)

            s = {0: slope(0), 1: slope(1)}
            d = {}
            for pair in range(HEADS2):
                d[pair] = bend(pair, s[pair])
                values(pair)
                if pair + 2 < HEADS2:
                    s[pair + 2] = slope(pair + 2)
                if pair:
                    rest(pair - 1, d[pair - 1])
            rest(HEADS2 - 1, d[HEADS2 - 1])

        over_widths(i, ends, run)

        if later:
            @pl.when(j == 0)
            def _():
                for copy in later:
                    copy.start()

        @pl.when(j < NQ - 2)
        def _():
            over_widths(i - 2, ends, lambda wide, begin: probs_copy(p_slots, p_in, p_sem, i - 2, wide, False).start())

        return carry

    lax.fori_loop(0, NQ, block, 0)
    for pair in range(HEADS2):
        grads_ref[:, grad_columns(1, pair)] = (dk_ref[:, span[pair]] * KSCALE).astype(BF)
        grads_ref[:, grad_columns(2, pair)] = dv_ref[:, span[pair]].astype(BF)


def unit_rows(values):
    center = values - jnp.mean(values, axis=-1, keepdims=True)
    spread = jnp.mean(center * center, axis=-1, keepdims=True)
    inv = lax.rsqrt(spread + EPS)
    return center * inv, inv


HID = HALF
DOWN = HALF + FF // 2
REST = HALF + FF
FIRST = 3 * HALF + 128
STEP = 512
PER_HALF = FF // 2 // STEP


def feed_stage(x_ref, mixed_ref, w_refs, par_ref, out_ref, unit1_ref, inv1_ref, norm_ref, act_ref, slope_ref,
               unit2_ref, inv2_ref, tm=512):
    def chunk(i, carry):
        rows = block_rows(i, tm)
        summed = x_ref[rows, :]
        for half in range(2):
            summed = summed + nt(mixed_ref[rows, half * HALF:(half + 1) * HALF], w_refs[half][:, :HALF])
        unit, inv = unit_rows(summed)
        unit1_ref[rows, :] = unit.astype(BF)
        inv1_ref[rows, :] = inv
        normed = unit * par_ref[0:1, :] + par_ref[1:2, :]
        low = normed.astype(BF)
        norm_ref[rows, :] = low
        for part in range(2 * PER_HALF):
            cols = slice(part * STEP, (part + 1) * STEP)
            at = HID + part % PER_HALF * STEP
            hidden = nn(low, w_refs[part // PER_HALF][:, at:at + STEP])
            square = hidden * hidden
            gate = 0.5 + 0.5 * jnp.tanh(hidden * (C1 + C2 * square))
            act_ref[rows, cols] = (hidden * gate).astype(BF)
            slope_ref[rows, cols] = (gate + gate * (1.0 - gate) * hidden * (2 * C1 + 6 * C2 * square)).astype(BF)
        total = normed
        for half in range(2):
            total = total + nt(act_ref[rows, half * (FF // 2):(half + 1) * (FF // 2)], w_refs[half][:, DOWN:])
        unit, inv = unit_rows(total)
        unit2_ref[rows, :] = unit.astype(BF)
        inv2_ref[rows, :] = inv
        out_ref[rows, :] = unit * par_ref[2:3, :] + par_ref[3:4, :]
        return carry

    lax.fori_loop(0, LEN // tm, chunk, 0)


def unit_back(grad, unit, inv, gain):
    scaled = grad * gain
    first = jnp.mean(scaled, axis=-1, keepdims=True)
    second = jnp.mean(scaled * unit, axis=-1, keepdims=True)
    return inv * (scaled - first - unit * second)


def fold_rows(values):
    return jnp.sum(values.reshape(-1, 8, values.shape[-1]), axis=0)


def total_stage(limit, grad_ref, unit2_ref, inv2_ref, par_ref, total_ref, low_ref, small_ref, tm=512):
    small_ref[...] = jnp.zeros_like(small_ref)

    def chunk(i, carry):
        rows = block_rows(i, tm)
        grad = grad_ref[rows, :]
        if limit is not None:
            grad = jnp.where(lax.broadcasted_iota(jnp.int32, grad.shape, 0) + i * tm < limit, grad, 0.0)
        unit2 = unit2_ref[rows, :].astype(F32)
        small_ref[16:24, :] += fold_rows(grad * unit2)
        small_ref[24:32, :] += fold_rows(grad)
        total = unit_back(grad, unit2, inv2_ref[rows, :], par_ref[2:3, :])
        total_ref[rows, :] = total
        low_ref[rows, :] = total.astype(BF)
        return carry

    lax.fori_loop(0, LEN // tm, chunk, 0)


def feed_back_stage(total_ref, low_ref, unit1_ref, inv1_ref, slope_ref, inv_ref, w_refs, par_ref,
                    base_ref, gm_ref, small_ref, hid_ref, att_ref, tm=512):
    def chunk(i, carry):
        rows = block_rows(i, tm)
        low = low_ref[rows, :]
        for part in range(2 * PER_HALF):
            cols = slice(part * STEP, (part + 1) * STEP)
            at = DOWN + part % PER_HALF * STEP
            slope = nn(low, w_refs[part // PER_HALF][:, at:at + STEP])
            hid_ref[rows, cols] = (slope * slope_ref[rows, cols].astype(F32)).astype(BF)
        normed = total_ref[rows, :]
        for half in range(2):
            normed = normed + nt(hid_ref[rows, half * (FF // 2):(half + 1) * (FF // 2)], w_refs[half][:, HID:DOWN])
        unit1 = unit1_ref[rows, :].astype(F32)
        small_ref[0:8, :] += fold_rows(normed * unit1)
        small_ref[8:16, :] += fold_rows(normed)
        summed = unit_back(normed, unit1, inv1_ref[rows, :], par_ref[0:1, :])
        base_ref[rows, :] = summed
        low = summed.astype(BF)
        att_ref[rows, :] = low
        for half in range(2):
            grad = nn(low, w_refs[half][:, :HALF])
            for pair in range(2):
                for part in range(tm // QB):
                    inv = inv_ref[pl.ds((i * (tm // QB) + part) * HEADS2 + half * 2 + pair, 1), :]
                    inv = jnp.concatenate([jnp.broadcast_to(inv[:, :QB], (64, QB)),
                                           jnp.broadcast_to(inv[:, QB:], (64, QB))], axis=0).T
                    value = grad[part * QB:(part + 1) * QB, pair * 128:(pair + 1) * 128] * inv
                    gm_ref[pl.ds(pl.multiple_of(i * tm + part * QB, QB), QB),
                           half * HALF + pair * 128:half * HALF + (pair + 1) * 128] = value.astype(BF)
        return carry

    lax.fori_loop(0, LEN // tm, chunk, 0)


def weight_stage(left_ref, right_ref, olds, outs, offset, width):
    cols = slice(offset, offset + width)
    for half in range(2):
        value = tn(left_ref[...], right_ref[:, half * width:(half + 1) * width])
        if olds is not None:
            value = value + olds[half][:, cols].astype(F32)
        outs[half][:, cols] = value.astype(BF)


def project_grad_stage(low_ref, grads_ref, olds, outs):
    for half in range(2):
        value = tn(low_ref[...], grads_ref[:, half * 3 * HALF:(half + 1) * 3 * HALF])
        if olds is not None:
            value = value + olds[half][...].astype(F32)
        outs[half][:, :3 * HALF] = value.astype(BF)


def input_stage(base_ref, grads_ref, w_refs, out_ref, size=LEN):
    def chunk(i, carry):
        rows = block_rows(i, TM)
        value = base_ref[rows, :]
        for half in range(2):
            value = value + nt(grads_ref[rows, half * 3 * HALF:(half + 1) * 3 * HALF], w_refs[half][:, :3 * HALF])
        out_ref[rows, :] = value
        return carry

    lax.fori_loop(0, size // TM, chunk, 0)


def add_row(x_ref, row, low_ref, keep):
    def chunk(i, carry):
        rows = block_rows(i, TM)
        value = x_ref[rows, :] + row
        if keep:
            x_ref[rows, :] = value
        if low_ref is not None:
            low_ref[rows, :] = value.astype(BF)
        return carry

    lax.fori_loop(0, LEN // TM, chunk, 0)


LIMIT = 64.0 ** 2
P_SHAPE = (NQ, HEADS2, LEN, 2 * QB)
VMEM = pltpu.VMEM


class Moves:
    def __init__(self, sem):
        self.sem, self.count, self.open = sem, 0, []

    def make(self, source, target):
        copy = pltpu.make_async_copy(source, target, self.sem.at[self.count])
        self.count += 1
        return copy

    def fetch(self, source, target):
        copy = self.make(source, target)
        copy.start()
        return copy

    def send(self, source, target):
        copy = self.fetch(source, target)
        self.open.append(copy)
        return copy

    def finish(self):
        wait(*self.open)
        self.open = []


def wait(*copies):
    for copy in copies:
        copy.wait()


class Either:
    def __init__(self, moves, index, count, make):
        self.low, self.copies = index < count, []
        at = moves.count
        for ref, place in ((0, index), (1, index - count)):
            moves.count = at
            self.copies.append(moves.make(*make(ref, jnp.clip(place, 0, count - 1))))

    def start(self):
        pl.when(self.low)(self.copies[0].start)
        pl.when(jnp.logical_not(self.low))(self.copies[1].start)

    def wait(self):
        self.copies[0].wait()


def parts_in(moves, at_ref, half, sources, target):
    if len(sources) == 1:
        return rows_in(moves, at_ref, half, sources[0], target)
    count, rows, _ = sources[0].shape
    copies = []
    for b in range(2 * count):
        copy = Either(moves, at_ref[half, b], count,
                      lambda ref, place, b=b: (sources[ref].at[place], target.at[pl.ds(b * rows, rows), :]))
        copy.start()
        copies.append(copy)
    return copies


def parts_out(moves, at_ref, half, source, targets):
    if len(targets) == 1:
        return rows_out(moves, at_ref, half, source, targets[0])
    count, rows, _ = targets[0].shape
    for b in range(2 * count):
        copy = Either(moves, at_ref[half, b], count,
                      lambda ref, place, b=b: (source.at[pl.ds(b * rows, rows), :], targets[ref].at[place]))
        copy.start()
        moves.open.append(copy)


def rows_in(moves, at_ref, half, source, target, start=True):
    move = moves.fetch if start else moves.make
    if len(source.shape) == 2:
        return [move(source, target)]
    dp, rows, _ = source.shape
    return [move(source.at[at_ref[half, b]], target.at[pl.ds(b * rows, rows), :]) for b in range(dp)]


def rows_out(moves, at_ref, half, source, target):
    if len(target.shape) == 2:
        moves.send(source, target)
        return
    dp, rows, _ = target.shape
    for b in range(dp):
        moves.send(source.at[pl.ds(b * rows, rows), :], target.at[at_ref[half, b]])


ANY = pl.BlockSpec(memory_space=pl.ANY)
SMEM = pl.BlockSpec(memory_space=pltpu.SMEM)


def like(shapes):
    return [VMEM(s, t) for s, t in shapes]


def full(width, kind=BF):
    return ((LEN, width), kind)


def call(kernel, outs, scratch, sems, flops, *args):
    smem = sum(a.dtype == jnp.int32 for a in args)
    return pl.pallas_call(
        kernel,
        in_specs=[SMEM] * smem + [ANY] * (len(args) - smem),
        out_specs=[ANY] * len(outs),
        out_shape=[jax.ShapeDtypeStruct(s, t) for s, t in outs],
        scratch_shapes=scratch + [pltpu.SemaphoreType.DMA((sems,))],
        compiler_params=pltpu.CompilerParams(vmem_limit_bytes=VMEM_LIMIT),
        cost_estimate=pl.CostEstimate(flops=flops, bytes_accessed=8 << 20, transcendentals=0),
    )(*args)


HEADS_OUT = (full(D), full(D), full(D), full(D), full(D), ((NQ * HEADS2, 2 * QB), F32))
ATTEND_WORK = [VMEM((HEADS2, 144, LEN), BF), VMEM((LEN, 128), BF), VMEM((LEN, 128), BF),
               VMEM((2,) + P_SHAPE[1:], BF), pltpu.SemaphoreType.DMA((2,))]


def either(ends, bound, resident, heads, work, p_out, done):
    for shifted in (False, True):
        @pl.when((bound > LIMIT) if shifted else (bound <= LIMIT))
        def _(shifted=shifted):
            attend_stage(ends, shifted, resident, *heads, *work[:4], p_out, work[4], done)


VT = ((HEADS2, 144, LEN), BF)


def open_kernel(pieces_ref, tag_ref, at_ref, emb_ref, own_ref, other_ref, *refs):
    outs, par_o, bound_o, refs = refs[:4], refs[4], refs[5], refs[6:]
    heads, par, x, low, wa, wb, sem = refs[:4], refs[4], refs[5], refs[6], refs[7], refs[8], refs[9]
    moves = Moves(sem)
    first = rows_in(moves, at_ref, 0, own_ref, wa)
    third = moves.fetch(emb_ref, x)
    second = rows_in(moves, at_ref, 1, other_ref, wb)
    wait(*first)
    par[...] = wa[:, 3 * HALF:].astype(F32).T[:8, :]
    moves.send(par, par_o)
    wait(third)
    add_row(x, par[pl.ds(4 + tag_ref[0], 1), :], low, False)
    wait(*second)
    bound_o[0] = project_stage(low, (wa, wb), *heads)
    for a, b in zip(heads, outs):
        moves.send(a, b)
    moves.finish()


def open_visit(pieces, tag, at, embedded, own, other):
    outs = (full(D), full(D), full(D), VT, ((8, D), F32))
    scratch = like(outs + (full(D, F32), full(D), ((D, FIRST), BF), ((D, FIRST), BF)))
    got = pl.pallas_call(
        open_kernel,
        in_specs=[SMEM] * 3 + [ANY] * 3,
        out_specs=[ANY] * 5 + [SMEM],
        out_shape=[jax.ShapeDtypeStruct(s, t) for s, t in outs + (((1,), F32),)],
        scratch_shapes=scratch + [pltpu.SemaphoreType.DMA((160,))],
        compiler_params=pltpu.CompilerParams(vmem_limit_bytes=VMEM_LIMIT),
        cost_estimate=pl.CostEstimate(flops=4_000_000_000, bytes_accessed=8 << 20, transcendentals=0),
    )(pieces, tag, at, embedded, own, other)
    return got[:4], got[4], got[5]


def attend_kernel(pieces_ref, bound_ref, q_ref, k_ref, v_ref, vt_ref, *refs):
    outs, p_o, refs = refs[:3], refs[3], refs[4:]
    heads, work, row_sem, sem = refs[:6], refs[6:11], refs[11], refs[12]
    moves = Moves(sem)
    ends = piece_ends(pieces_ref)
    first = [moves.fetch(a, b) for a, b in zip((q_ref, k_ref, vt_ref, v_ref), heads[:2] + work[:1] + heads[2:3])]
    segment_codes(ends, work[1], work[2])
    wait(*first)

    def sent(i, rows):
        return [pltpu.make_async_copy(heads[n].at[rows, :], outs[n - 3].at[rows, :], row_sem.at[n - 3, i])
                for n in (3, 4)]

    def done(i, rows):
        for copy in sent(i, rows):
            copy.start()

    either(ends, bound_ref[0], False, heads, work, p_o, done)
    moves.send(heads[5], outs[2])
    for i in range(NQ):
        wait(*sent(i, pl.ds(i * QB, QB)))
    moves.finish()


def attend_visit(pieces, bound, q, k, v, vt):
    outs = HEADS_OUT[3:] + ((P_SHAPE, BF),)
    scratch = like(HEADS_OUT) + ATTEND_WORK + [pltpu.SemaphoreType.DMA((2, NQ)), pltpu.SemaphoreType.DMA((16,))]
    got = pl.pallas_call(
        attend_kernel,
        in_specs=[SMEM] * 2 + [ANY] * 4,
        out_specs=[ANY] * 4,
        out_shape=[jax.ShapeDtypeStruct(s, t) for s, t in outs],
        scratch_shapes=scratch,
        compiler_params=pltpu.CompilerParams(vmem_limit_bytes=VMEM_LIMIT),
        cost_estimate=pl.CostEstimate(flops=8_000_000_000, bytes_accessed=8 << 20, transcendentals=0),
    )(pieces, bound, q, k, v, vt)
    return got[:3], got[3]


SAVED = (full(D), full(1, F32), full(D), full(FF), full(FF), full(D), full(1, F32))


def middle_kernel(parts, pieces_ref, tag_ref, at_ref, emb_ref, mixed_ref, inv_ref, par_ref, fa_ref, fb_ref, *refs):
    ra_ref, rb_ref, cot_ref, refs = refs[:parts], refs[parts:2 * parts], refs[2 * parts], refs[2 * parts + 1:]
    saved_o, refs = refs[:7], refs[7:]
    result_o, p_o, base_o, gm_o, small_o, pro_o = refs[:5] + (refs[5:7],)
    keep_o, send_o, refs = refs[7:7 + parts], refs[7 + parts:7 + 2 * parts], refs[7 + 2 * parts:]
    x, result, cot, par, wf, wr, low, att, gm, small, small_b = (
        refs[0], refs[1], refs[2], refs[3], refs[4:6], refs[6:8], refs[8], refs[9], refs[10], refs[11], refs[12])
    saved, heads, sums, pro = refs[13:20], refs[20:26], refs[26:28], refs[28:30]
    work, sem = refs[30:35], refs[35]
    unit1, inv1, norm, act, slope, unit2, inv2 = saved
    mixed, inv = heads[3], heads[5]
    moves = Moves(sem)
    ends = piece_ends(pieces_ref)
    first = [moves.fetch(emb_ref, x), moves.fetch(mixed_ref, mixed), moves.fetch(par_ref, par)]
    second = parts_in(moves, at_ref, 0, ra_ref, wr[0]) + parts_in(moves, at_ref, 1, rb_ref, wr[1])
    segment_codes(ends, work[1], work[2])
    wait(*first)
    add_row(x, par[pl.ds(4 + tag_ref[0], 1), :], None, True)
    wait(*second)
    third = rows_in(moves, at_ref, 0, fa_ref, wf[0]) + rows_in(moves, at_ref, 1, fb_ref, wf[1])
    feed_stage(x, mixed, wr, par, x, *saved)
    for a, b in zip(saved, saved_o):
        moves.send(a, b)
    add_row(x, 0.0, low, False)
    wait(*third)
    bound = project_stage(low, wf, heads[0], heads[1], heads[2], work[0])
    either(ends, bound, True, heads, work, p_o, lambda i, rows: None)
    seed = moves.fetch(cot_ref, cot)
    moves.finish()
    feed_stage(x, mixed, wr, par, result, *saved)
    out = moves.fetch(result, result_o)
    wait(seed)
    total_stage(ends[-2], cot, unit2, inv2, par, cot, att, small)
    weight_stage(att, act, None, sums, DOWN, FF // 2)
    again = [moves.fetch(saved_o[n], saved[n]) for n in (3, 5, 6)]
    feed_back_stage(cot, att, unit1, inv1, slope, inv, wr, par, x, gm, small, slope, att)
    weight_stage(att, mixed, None, sums, 0, HALF)
    weight_stage(norm, slope, None, sums, HID, FF // 2)
    later = [moves.fetch(saved_o[n], saved[n]) for n in (0, 1, 2)] + [moves.fetch(inv_ref, inv)]
    wait(out)
    grads = slope.at[:, :3 * D]
    attend_back_stage(ends, True, *heads[:5], gm, work[0], p_o, work[3], work[4], result, cot, grads)
    later.append(moves.fetch(mixed_ref, mixed))
    input_stage(x, grads, wf, x)
    project_grad_stage(low, grads, None, pro)
    moves.send(pro[0], pro_o[0])
    moves.send(pro[1], pro_o[1])
    later.append(moves.fetch(saved_o[4], slope))
    wait(*again)
    total_stage(None, x, unit2, inv2, par, x, att, small_b)
    weight_stage(att, act, sums, sums, DOWN, FF // 2)
    wait(*later)
    feed_back_stage(x, att, unit1, inv1, slope, inv, wr, par, x, gm, small_b, slope, att)
    moves.send(x, base_o)
    moves.send(gm, gm_o)
    small[...] += small_b[...]
    moves.send(small, small_o)
    weight_stage(att, mixed, sums, sums, 0, HALF)
    weight_stage(norm, slope, sums, sums, HID, FF // 2)
    parts_out(moves, at_ref, 0, sums[0], keep_o)
    parts_out(moves, at_ref, 1, sums[1], send_o)
    moves.finish()


def middle(pieces, tag, at, embedded, mixed, inv, par, first, rest, cot):
    two = lambda *shape: ((shape, BF),) * 2
    small = ((32, D), F32)
    outs = (SAVED + (full(D, F32), (P_SHAPE, BF), full(D, F32), full(D), small) + two(D, 3 * HALF)
            + tuple((r.shape, BF) for r in rest))
    parts = len(rest) // 2
    scratch = like((full(D, F32),) * 3 + (((8, D), F32),) + two(D, FIRST) + two(D, REST) + (full(D),) * 3
                   + (small, small) + SAVED + HEADS_OUT + two(D, REST) + two(D, 3 * HALF)) + ATTEND_WORK
    got = call(functools.partial(middle_kernel, parts), outs, scratch, 4 * 64 + 200, 60_000_000_000,
               pieces, tag, at, embedded, mixed, inv, par, *first, *rest, cot)
    return got[7], got[9], got[10], got[11], got[12:14], got[14:]


def heads_back_kernel(pieces_ref, q_ref, k_ref, v_ref, mixed_ref, low_ref, gm_ref, p_ref, grads_o, *refs):
    heads, refs = refs[:6], refs[6:]
    p_slots, kt, dk, dv, grads, p_sem, sem = refs
    moves = Moves(sem)
    ends = piece_ends(pieces_ref)
    first = [moves.fetch(a, b) for a, b in zip((q_ref, k_ref, v_ref, mixed_ref, low_ref, gm_ref), heads)]
    attend_back_stage(ends, False, *heads, kt, p_ref, p_slots, p_sem, dk, dv, grads, first)
    moves.send(grads, grads_o)
    moves.finish()


def heads_back(pieces, heads, gm, p):
    scratch = like((full(D),) * 6)
    scratch += [VMEM((2,) + P_SHAPE[1:], BF), VMEM((HEADS2, 128, LEN), BF), VMEM((LEN, D), F32), VMEM((LEN, D), F32),
                VMEM((LEN, 3 * D), BF), pltpu.SemaphoreType.DMA((2,))]
    return call(heads_back_kernel, (full(3 * D),), scratch, 16, 18_000_000_000, pieces, *heads, gm, p)[0]


def last_kernel(tag_ref, at_ref, grads_ref, emb_ref, par_ref, base_ref, fa_ref, fb_ref, old_a_ref, old_b_ref, small_ref,
                *refs):
    out_o, keep_o, send_o = refs[:3]
    grads, x, low, par, base, wf, old, small, pro, sem = (
        refs[3], refs[4], refs[5], refs[6], refs[7], refs[8:10], refs[10:12], refs[12], refs[13:15], refs[15])
    moves = Moves(sem)
    first = [moves.fetch(a, b) for a, b in ((par_ref, par), (emb_ref, x), (grads_ref, grads))]
    second = [moves.fetch(a, b) for a, b in ((old_a_ref, old[0]), (old_b_ref, old[1]))]
    third = [moves.fetch(a, b) for a, b in ((base_ref, base), (small_ref, small))]
    third += rows_in(moves, at_ref, 0, fa_ref, wf[0]) + rows_in(moves, at_ref, 1, fb_ref, wf[1])
    wait(*first[:2])
    add_row(x, par[pl.ds(4 + tag_ref[0], 1), :], low, False)
    wait(*first[2:], *second)
    project_grad_stage(low, grads, old, pro)
    wait(*third)
    input_stage(base, grads, wf, base)
    moves.send(base, out_o)
    column = jnp.sum(base[...], axis=0, keepdims=True)
    norms = jnp.sum(small[...].reshape(4, 8, D), axis=1)
    tags = lax.broadcasted_iota(jnp.int32, (PAIRS, D), 0) == tag_ref[0]
    table = jnp.where(tags, jnp.broadcast_to(column, (PAIRS, D)), 0.0)
    stats = jnp.concatenate([norms, table, jnp.zeros((120, D), F32)], axis=0).T.astype(BF)
    for half, target in enumerate((keep_o, send_o)):
        pro[half][:, 3 * HALF:] = stats
        rows_out(moves, at_ref, half, pro[half], target)
    moves.finish()


def last_back(tag, at, part, grads, embedded, par, base, first, old, small):
    two = lambda *shape: ((shape, BF),) * 2
    scratch = like((full(3 * D), full(D, F32), full(D), ((8, D), F32), full(D, F32)) + two(D, FIRST)
                   + two(D, 3 * HALF) + (((32, D), F32),) + two(D, FIRST))
    return call(last_kernel, (full(D, F32),) + two(*part(FIRST)), scratch, 4 * 64 + 40, 8_000_000_000,
                tag, at, grads, embedded, par, base, *first, *old, small)


GROUP = ("dp", "tensor")


def plan(dp):
    if dp == 16:
        return (8, 4, 1, 2), (8, 4, 2, 1)
    bits = [1 << i for i in range(dp.bit_length() - 1)]
    side = len(bits) // 3
    x, y, z = bits[:side], bits[side:2 * side], bits[2 * side:]
    return tuple(z[::-1] + x[::-1] + y[::-1]), tuple(z[::-1] + y[::-1] + x[::-1])


def flip(value, dp, masks):
    pairs = [(d * 2 + t, (d ^ masks[t]) * 2 + t) for d in range(dp) for t in range(2)]
    return lax.ppermute(value, GROUP, pairs)


def swap(value):
    return lax.ppermute(value, "tensor", [(0, 1), (1, 0)])


def doubled(held, dp, masks):
    return jnp.concatenate([held, flip(held, dp, masks)], axis=0)


def after(value, *others):
    return lax.optimization_barrier((value, *others))[0]


def places(dp, mine, tensor):
    rel = jnp.arange(dp, dtype=jnp.int32) ^ mine
    found = []
    for order in plan(dp):
        found.append(sum(((rel & mask) // mask) << i for i, mask in enumerate(order)))
    return jnp.stack([jnp.where(tensor == t, found[0], found[1]) for t in (0, 1)])


def reduced(held, dp, masks, kind=BF):
    half = held.shape[0] // 2
    return add(held[:half], flip(held[half:], dp, masks), kind)


def add(a, b, kind=BF):
    return (a.astype(F32) + b.astype(F32)).astype(kind)


def body(embedded, piece_lengths, pair_tags, pair_embedding, w_query, w_key, w_value, w_output, w_hidden,
         w_down, first_gain, first_shift, second_gain, second_shift, cotangent):
    dp = lax.axis_size("dp")
    mine, tensor = lax.axis_index("dp"), lax.axis_index("tensor")
    rows = D // dp
    blocked = rows % 16 == 0
    pieces = lax.dynamic_index_in_dim(piece_lengths, tensor, 0, keepdims=False)
    tag = lax.dynamic_index_in_dim(pair_tags, tensor, 0, keepdims=True)
    small = jnp.concatenate([jnp.stack([first_gain, first_shift, second_gain, second_shift]), pair_embedding], axis=0)
    small = tn(small, jnp.eye(8, 128, dtype=BF)).astype(BF)
    at = places(dp, mine, tensor)

    def arranged(held):
        both = held, swap(held)
        if blocked:
            return both
        return tuple(h[at[i]].reshape(D, -1) for i, h in enumerate(both))

    def part(width):
        return (dp, rows, width) if blocked else (D, width)

    def swapped(keep, send):
        if not blocked:
            keep, send = (v.reshape(dp, rows, -1)[jnp.zeros((dp,), jnp.int32).at[at[i]].set(jnp.arange(dp))]
                          for i, v in enumerate((keep, send)))
        return add(keep, swap(send))

    def summed(held, phases):
        for i, masks in enumerate(phases):
            held = reduced(held, dp, masks, F32 if i == len(phases) - 1 else BF)
        return held[0]

    phases = list(zip(*plan(dp)))
    split = len(phases) - 1
    first = jnp.concatenate([w_query, w_key, w_value, small], axis=1)[None]
    rest = jnp.concatenate([w_output.T, w_hidden, w_down.T], axis=1)[None]
    for i, masks in enumerate(phases):
        first = doubled(first, dp, masks)
        if i < split - 1:
            rest = doubled(after(rest, first, *((tag, pieces, at) if i == 0 else ())), dp, masks)
        elif i == split - 1:
            rest = after(rest, first)
            arrived = flip(rest, dp, masks)
    first = arranged(after(first, rest))
    heads, par, bound = open_visit(pieces, tag, at, embedded, *first)
    rest = jnp.concatenate([after(rest, *heads), arrived], axis=0)
    rest, heads = lax.optimization_barrier((rest, heads))
    arrived, swapped_rest = flip(rest, dp, phases[-1]), swap(rest)
    q, k, v, vt = heads
    (mixed, low, inv), probs = attend_visit(pieces, bound, q, k, v, vt)
    arrived = after(arrived, mixed)
    if blocked:
        rest = (rest, arrived, swapped_rest, swap(arrived))
    else:
        rest = arranged(jnp.concatenate([rest, arrived], axis=0))
    result, base, gm, stats, old, sums = middle(pieces, tag, at, embedded, mixed, inv, par, first, rest, cotangent)
    if blocked:
        keep, keep_out, send, send_out = sums
        out = add(keep_out, swap(send_out))
        gm = after(gm, out)
        out = flip(out, dp, phases[-1])
        sums = add(add(keep, swap(send), F32), out)
    else:
        sums = reduced(swapped(*sums), dp, phases[-1])
    grads = heads_back(pieces, (q, k, v, mixed, low), gm, probs)
    sums, grads = lax.optimization_barrier((sums, grads))
    half = sums.shape[0] // 2
    out = flip(sums[half:], dp, phases[-2])
    grad, *da = last_back(tag, at, part, grads, embedded, par, base, first, old, stats)
    *da, out = lax.optimization_barrier((*da, out))
    sums = add(sums[:half], out)
    da = swapped(*da)
    sums = summed(sums, phases[-3::-1])
    da = summed(da, phases[::-1])
    small = da[:, 3 * HALF:3 * HALF + 8].T
    return (result, grad, small[4:], da[:, :HALF], da[:, HALF:2 * HALF], da[:, 2 * HALF:3 * HALF],
            sums[:, :HALF].T, sums[:, HID:DOWN], sums[:, DOWN:].T, small[0], small[1], small[2], small[3])


def solution(mesh):
    both = P(GROUP, None)
    params = (P("dp", "tensor"),) * 3 + (P("tensor", "dp"), P("dp", "tensor"), P("tensor", "dp"))
    in_specs = (both, P("dp", None), P("dp"), P(None, "dp")) + params + (P("dp"),) * 4 + (both,)
    out_specs = (both, both, P(None, "dp")) + params + (P("dp"),) * 4
    return jax.shard_map(body, mesh=mesh, in_specs=in_specs, out_specs=out_specs, check_vma=False)
```

time: 293 us -> 230 us (0.78)
  starting transfers between devices: 55.5 us -> 32.4 us
  Pallas kernels: 155 us -> 133 us
  waiting for transfers between devices: 57.4 us -> 43.3 us
  local copies, waits for them, and re-layouts: 12.6 us -> 8.19 us
    pallas_call x7 -> x3, Pallas kernels: 148 us -> 111 us  [call(): pl.pallas_call(kernel, in_specs=[SMEM] * smem + [ANY] * (len(args) - smem...]
    ppermute x20 -> x16, starting transfers between devices: 54.7 us -> 27.2 us  [flip(): return lax.ppermute(value, GROUP, pairs)]
    ppermute x20 -> x16, waiting for transfers between devices: 54.1 us -> 35.6 us  [flip(): return lax.ppermute(value, GROUP, pairs)]
    pallas_call x1 -> x2, Pallas kernels: 6.66 us -> 21.5 us  [the longest x1 10.8 us: attend_visit(): pl.pallas_call(attend_kernel, in_specs=[SMEM] * 2 + [ANY] * 4, out_specs=...]
    ppermute x5 -> x6, starting transfers between devices: 0.72 us -> 5.21 us  [swap(): return lax.ppermute(value, 'tensor', [(0, 1), (1, 0)])]
    ppermute x5 -> x6, waiting for transfers between devices: 3.26 us -> 7.73 us  [swap(): return lax.ppermute(value, 'tensor', [(0, 1), (1, 0)])]
  transfers between devices with their start and end apart: 25 -> 22, of which waited for: 16 -> 15; matrix products, arithmetic and copies ran while one was open for 6% -> 3% of each run, Pallas kernels for 9% -> 23%
where the time goes in v3:
time: 230 us; the launch traced here: 225 us
  Pallas kernels  133 us (58%)
  waiting for transfers between devices  43.3 us (19%)
  starting transfers between devices  32.4 us (14%)
  local copies, waits for them, and re-layouts  8.19 us (4%)
  other arithmetic  7.24 us (3%)
    pallas_call x3, Pallas kernels, call(): pl.pallas_call(kernel, in_specs=[SMEM] * smem + [ANY] * (len(args) - smem...  111 us
    ppermute x16, waiting for transfers between devices, flip(): return lax.ppermute(value, GROUP, pairs)  35.6 us
    ppermute x16, starting transfers between devices, flip(): return lax.ppermute(value, GROUP, pairs)  27.2 us
    pallas_call x1, Pallas kernels, attend_visit(): pl.pallas_call(attend_kernel, in_specs=[SMEM] * 2 + [ANY] * 4, out_specs=...  10.8 us
    pallas_call x1, Pallas kernels, open_visit(): pl.pallas_call(open_kernel, in_specs=[SMEM] * 3 + [ANY] * 3, out_specs=[A...  10.7 us
    ppermute x6, waiting for transfers between devices, swap(): return lax.ppermute(value, 'tensor', [(0, 1), (1, 0)])  7.73 us
    ppermute x6, starting transfers between devices, swap(): return lax.ppermute(value, 'tensor', [(0, 1), (1, 0)])  5.21 us
  transfers between devices with their start and end apart: 22, of which 15 were waited for; matrix products, arithmetic and copies ran while one was open for 3% of the time, Pallas kernels for 23%

profile of v3, /device:TPU:0, one launch (start us, length us, event | category | flops | bytes accessed | tf_op | source)
XLA Modules:
  0.0 225.1 jit_solution(13759417474704818380)
XLA Ops:
  2.4 4.0 %collective-permute-start = (bf16[1,32,896]{2,1,0:T(8,128)(2,1)S(1)}, bf16[1,32,896]{2,1,0:T(8,128)(2,1)S(1)}, u32[]{:S(2)}, u32[]{:S(2)}) collective-permute-start(bf16[1,32,896]{2,1,0:T(8,128)(2,1)S(1)} %maximum_bitcast_fusion.1), channel_id=1, source_target_pairs={{0,16},{1,17},{2,18},{3,19},{4,20},{5,21},{6,22},{7,23},{8,24},{9,... | collective-permute-start | bytes 172040 | tf_op jit(solution)/shard_map/ppermute | solution.py:818
  9.2 1.4 collective-permute-start.1
  11.1 1.2 dynamic_slice.9.tag_ref
  12.3 3.2 %collective-permute-start.4 = (bf16[1,32,2304]{2,1,0:T(8,128)(2,1)S(1)}, bf16[1,32,2304]{2,1,0:T(8,128)(2,1)S(1)}, u32[]{:S(2)}, u32[]{:S(2)}) collective-permute-start(bf16[1,32,2304]{2,1,0:T(8,128)(2,1)S(1)} %maximum_bitcast_fusion), channel_id=1, source_target_pairs={{0,16},{1,17},{2,18},{3,19},{4,20},{5,21},{6,22},{7,23},{8,24},{9,... | collective-permute-start | bytes 442376 | tf_op jit(solution)/shard_map/ppermute | solution.py:818
  15.6 1.6 collective-permute-start.2
  17.1 4.0 %collective-permute-done.4 = bf16[1,32,2304]{2,1,0:T(8,128)(2,1)S(1)} collective-permute-done((bf16[1,32,2304]{2,1,0:T(8,128)(2,1)S(1)}, bf16[1,32,2304]{2,1,0:T(8,128)(2,1)S(1)}, u32[]{:S(2)}, u32[]{:S(2)}) %collective-permute-start.4) | collective-permute-done | bytes 147488 | tf_op jit(solution)/shard_map/ppermute | solution.py:818
  21.7 1.6 collective-permute-start.3
  23.3 5.7 %collective-permute-done.5 = bf16[2,32,2304]{2,1,0:T(8,128)(2,1)S(1)} collective-permute-done((bf16[2,32,2304]{2,1,0:T(8,128)(2,1)S(1)}, bf16[2,32,2304]{2,1,0:T(8,128)(2,1)S(1)}, u32[]{:S(2)}, u32[]{:S(2)}) %collective-permute-start.5) | collective-permute-done | bytes 294944 | tf_op jit(solution)/shard_map/ppermute | solution.py:818
  30.4 1.6 collective-permute-start.7
  33.8 10.7 %shard_map.246 = (bf16[1024,512]{1,0:T(8,128)(2,1)}, bf16[1024,512]{1,0:T(8,128)(2,1)}, bf16[1024,512]{1,0:T(8,128)(2,1)}, bf16[4,144,1024]{2,1,0:T(8,128)(2,1)}, f32[8,512]{1,0:T(8,128)}, /*index=5*/f32[1]{0:T(128)}) custom-call(s32[8]{0:T(128)} %dynamic-slice_bitcast_fusion.pieces_ref, s32[1]{0:T(128)} %dynamic_slice.9.tag_ref, ...), custom_call_target="tpu_custom_call" | custom-call | flops 4000000000 | bytes 8388608 | tf_op jit(solution)/shard_map/pallas_call | solution.py:619
  44.6 1.6 collective-permute-start.8
  46.2 10.8 %shard_map.247 = (bf16[1024,512]{1,0:T(8,128)(2,1)}, bf16[1024,512]{1,0:T(8,128)(2,1)}, f32[16,512]{1,0:T(8,128)}, bf16[4,4,1024,512]{3,2,1,0:T(8,128)(2,1)}) custom-call(s32[8]{0:T(128)} %dynamic-slice_bitcast_fusion.pieces_ref, f32[1]{0:T(128)} %get-tuple-element.57.bound_ref, bf16[1024,512]{1,0:T(8,128)(2,1)} %get-tuple-element.63.q_ref, ...), custom_call_target="tpu_custom_call" | custom-call | flops 8000000000 | bytes 8388608 | tf_op jit(solution)/shard_map/pallas_call | solution.py:658
  57.0 3.9 %collective-permute-done.8.refs_1_ = bf16[8,32,2304]{2,1,0:T(8,128)(2,1)S(1)} collective-permute-done((bf16[8,32,2304]{2,1,0:T(8,128)(2,1)S(1)}, bf16[8,32,2304]{2,1,0:T(8,128)(2,1)S(1)}, u32[]{:S(2)}, u32[]{:S(2)}) %collective-permute-start.8) | collective-permute-done | bytes 1179680 | tf_op jit(solution)/shard_map/ppermute | solution.py:818
  60.9 1.6 collective-permute-start.10
  62.5 2.5 %collective-permute-done.10.refs_3_ = bf16[8,32,2304]{2,1,0:T(8,128)(2,1)S(1)} collective-permute-done((bf16[8,32,2304]{2,1,0:T(8,128)(2,1)S(1)}, bf16[8,32,2304]{2,1,0:T(8,128)(2,1)S(1)}, u32[]{:S(2)}, u32[]{:S(2)}) %collective-permute-start.10) | collective-permute-done | bytes 1179680 | tf_op jit(solution)/shard_map/ppermute | solution.py:822
  66.0 81.6 %shard_map.248 = (bf16[1024,512]{1,0:T(8,128)(2,1)}, f32[1024,1]{1,0:T(8,128)}, bf16[1024,512]{1,0:T(8,128)(2,1)}, bf16[1024,2048]{1,0:T(8,128)(2,1)}, bf16[1024...) custom-call(s32[8]{0:T(128)} %dynamic-slice_bitcast_fusion.pieces_re, ...), custom_call_target="tpu_custom_call" | custom-call | flops 60000002048 | bytes 8388608 | tf_op jit(solution)/shard_map/pallas_call | solution.py:571
  147.6 3.4 %collective-permute-start.12 = (bf16[8,32,2304]{2,1,0:T(8,128)(2,1)}, bf16[8,32,2304]{2,1,0:T(8,128)(2,1)S(1)}, u32[]{:S(2)}, u32[]{:S(2)}) collective-permute-start(bf16[8,32,2304]{2,1,0:T(8,128)(2,1)} %get-tuple-element.76), channel_id=1, source_target_pairs={{0,1},{1,0},{2,3},{3,2},{4,5},{5,4},{6,7},{7,6},{8,9},{9,8},{10,11... | collective-permute-start | bytes 3538952 | tf_op jit(solution)/shard_map/ppermute | solution.py:822
  151.1 2.6 %collective-permute-done.12 = bf16[8,32,2304]{2,1,0:T(8,128)(2,1)S(1)} collective-permute-done((bf16[8,32,2304]{2,1,0:T(8,128)(2,1)}, bf16[8,32,2304]{2,1,0:T(8,128)(2,1)S(1)}, u32[]{:S(2)}, u32[]{:S(2)}) %collective-permute-start.12) | collective-permute-done | bytes 1179680 | tf_op jit(solution)/shard_map/ppermute | solution.py:822
  153.7 1.6 add_convert_fusion.1
  155.3 1.7 collective-permute-start.13
  157.0 16.4 %shard_map.249.grads_ref = bf16[1024,1536]{1,0:T(8,128)(2,1)} custom-call(s32[8]{0:T(128)} %dynamic-slice_bitcast_fusion.pieces_ref, bf16[1024,512]{1,0:T(8,128)(2,1)} %get-tuple-element.63.q_ref, bf16[1024,512]{1,0:T(8,128)(2,1)} %get-tuple-element.64.k_ref, bf16[1024,512]{1,0:T(8,128)(2,1)} %get-tuple-element.65.v_ref, ...), custom_call_target="tpu_custom_call" | custom-call | flops 17999998976 | bytes 8388608 | tf_op jit(solution)/shard_map/pallas_call | solution.py:571
  173.4 1.7 add_convert_fusion
  175.2 4.9 %collective-permute-start.14 = (bf16[4,32,2304]{2,1,0:T(8,128)(2,1)S(1)}, bf16[4,32,2304]{2,1,0:T(8,128)(2,1)S(1)}, u32[]{:S(2)}, u32[]{:S(2)}) collective-permute-start(bf16[4,32,2304]{2,1,0:T(8,128)(2,1)S(1)} %slice.78), channel_id=1, source_target_pairs={{0,2},{1,5},{2,0},{3,7},{4,6},{5,1},{6,4},{7,3},{8,10},{9,13},{10,... | collective-permute-start | bytes 1769480 | tf_op jit(solution)/shard_map/ppermute | solution.py:818
  180.1 13.1 %shard_map.250 = (f32[1024,512]{1,0:T(8,128)}, bf16[16,32,896]{2,1,0:T(8,128)(2,1)}, bf16[16,32,896]{2,1,0:T(8,128)(2,1)}) custom-call(s32[1]{0:T(128)} %dynamic_slice.9.tag_ref, s32[2,16]{1,0:T(2,128)} %pad_add_fusion.at_ref, bf16[1024,1536]{1,0:T(8,128)(2,1)} %shard_map.249.grads_ref, f32[1024,512]{1,0:T(8,128)} %emb_ref.5, ...), custom_call_target="tpu_custom_call" | custom-call | flops 8000000000 | bytes 8388608 | tf_op jit(solution)/shard_map/pallas_call | solution.py:571
  194.3 1.7 collective-permute-done.15
  196.4 6.6 %collective-permute-done.20 = bf16[2,32,2304]{2,1,0:T(8,128)(2,1)S(1)} collective-permute-done((bf16[2,32,2304]{2,1,0:T(8,128)(2,1)S(1)}, bf16[2,32,2304]{2,1,0:T(8,128)(2,1)S(1)}, u32[]{:S(2)}, u32[]{:S(2)}) %collective-permute-start.20) | collective-permute-done | bytes 294944 | tf_op jit(solution)/shard_map/ppermute | solution.py:818
  203.1 1.4 collective-permute-start.21
  205.0 1.4 collective-permute-start.17
  206.3 5.6 %collective-permute-done.21 = bf16[1,32,2304]{2,1,0:T(8,128)(2,1)S(1)} collective-permute-done((bf16[1,32,2304]{2,1,0:T(8,128)(2,1)S(1)}, bf16[1,32,2304]{2,1,0:T(8,128)(2,1)S(1)}, u32[]{:S(2)}, u32[]{:S(2)}) %collective-permute-start.21) | collective-permute-done | bytes 147488 | tf_op jit(solution)/shard_map/ppermute | solution.py:818
  213.3 3.9 %collective-permute-done.18 = bf16[2,32,896]{2,1,0:T(8,128)(2,1)S(1)} collective-permute-done((bf16[2,32,896]{2,1,0:T(8,128)(2,1)S(1)}, bf16[2,32,896]{2,1,0:T(8,128)(2,1)S(1)}, u32[]{:S(2)}, u32[]{:S(2)}) %collective-permute-start.18) | collective-permute-done | bytes 114720 | tf_op jit(solution)/shard_map/ppermute | solution.py:818
  217.3 1.5 collective-permute-start.19
  219.4 3.4 %collective-permute-done.19 = bf16[1,32,896]{2,1,0:T(8,128)(2,1)S(1)} collective-permute-done((bf16[1,32,896]{2,1,0:T(8,128)(2,1)S(1)}, bf16[1,32,896]{2,1,0:T(8,128)(2,1)S(1)}, u32[]{:S(2)}, u32[]{:S(2)}) %collective-permute-start.19) | collective-permute-done | bytes 57376 | tf_op jit(solution)/shard_map/ppermute | solution.py:818
  (80 shorter events, 16.1 us)
Async XLA Ops:
  0.6 9.9 %copy-start = (s32[2,8]{1,0:T(2,128)S(1)}, s32[2,8]{1,0:T(2,128)}, u32[]{:S(2)}) copy-start(s32[2,8]{1,0:T(2,128)} %param.16) | copy-start | bytes 196
  2.4 6.8 %collective-permute-start = (bf16[1,32,896]{2,1,0:T(8,128)(2,1)S(1)}, bf16[1,32,896]{2,1,0:T(8,128)(2,1)S(1)}, u32[]{:S(2)}, u32[]{:S(2)}) collective-permute-start(bf16[1,32,896]{2,1,0:T(8,128)(2,1)S(1)} %maximum_bitcast_fusion.1), channel_id=1, source_target_pairs={{0,16},{1,17},{2,18},{3,19},{4,20},{5,21},{6,22},{7,23},{8,24},{9,... | collective-permute-start | bytes 172040 | tf_op jit(solution)/shard_map/ppermute | solution.py:818
  9.2 6.3 %collective-permute-start.1 = (bf16[2,32,896]{2,1,0:T(8,128)(2,1)S(1)}, bf16[2,32,896]{2,1,0:T(8,128)(2,1)S(1)}, u32[]{:S(2)}, u32[]{:S(2)}) collective-permute-start(bf16[2,32,896]{2,1,0:T(8,128)(2,1)S(1)} %pad_maximum_fusion.5), channel_id=1, source_target_pairs={{0,8},{1,9},{2,10},{3,11},{4,12},{5,13},{6,14},{7,15},{8,0},{9,1},... | collective-permute-start | bytes 344072 | tf_op jit(solution)/shard_map/ppermute | solution.py:818
  12.3 8.8 %collective-permute-start.4 = (bf16[1,32,2304]{2,1,0:T(8,128)(2,1)S(1)}, bf16[1,32,2304]{2,1,0:T(8,128)(2,1)S(1)}, u32[]{:S(2)}, u32[]{:S(2)}) collective-permute-start(bf16[1,32,2304]{2,1,0:T(8,128)(2,1)S(1)} %maximum_bitcast_fusion), channel_id=1, source_target_pairs={{0,16},{1,17},{2,18},{3,19},{4,20},{5,21},{6,22},{7,23},{8,24},{9,... | collective-permute-start | bytes 442376 | tf_op jit(solution)/shard_map/ppermute | solution.py:818
  15.6 6.1 %collective-permute-start.2 = (bf16[4,32,896]{2,1,0:T(8,128)(2,1)S(1)}, bf16[4,32,896]{2,1,0:T(8,128)(2,1)S(1)}, u32[]{:S(2)}, u32[]{:S(2)}) collective-permute-start(bf16[4,32,896]{2,1,0:T(8,128)(2,1)S(1)} %pad_maximum_fusion.4), channel_id=1, source_target_pairs={{0,2},{1,5},{2,0},{3,7},{4,6},{5,1},{6,4},{7,3},{8,10},{9,13},{10,... | collective-permute-start | bytes 688136 | tf_op jit(solution)/shard_map/ppermute | solution.py:818
  21.1 7.9 %collective-permute-start.5 = (bf16[2,32,2304]{2,1,0:T(8,128)(2,1)S(1)}, bf16[2,32,2304]{2,1,0:T(8,128)(2,1)S(1)}, u32[]{:S(2)}, u32[]{:S(2)}) collective-permute-start(bf16[2,32,2304]{2,1,0:T(8,128)(2,1)S(1)} %pad_maximum_fusion.3), channel_id=1, source_target_pairs={{0,8},{1,9},{2,10},{3,11},{4,12},{5,13},{6,14},{7,15},{8,0},{9,1},... | collective-permute-start | bytes 884744 | tf_op jit(solution)/shard_map/ppermute | solution.py:818
  21.7 8.5 %collective-permute-start.3 = (bf16[8,32,896]{2,1,0:T(8,128)(2,1)S(1)}, bf16[8,32,896]{2,1,0:T(8,128)(2,1)S(1)}, u32[]{:S(2)}, u32[]{:S(2)}) collective-permute-start(bf16[8,32,896]{2,1,0:T(8,128)(2,1)S(1)} %pad_maximum_fusion.2), channel_id=1, source_target_pairs={{0,4},{1,3},{2,6},{3,1},{4,0},{5,7},{6,2},{7,5},{8,12},{9,11},{10,... | collective-permute-start | bytes 1376264 | tf_op jit(solution)/shard_map/ppermute | solution.py:818
  30.3 2.6 %copy-start.5 = (bf16[16,32,896]{2,1,0:T(8,128)(2,1)}, bf16[16,32,896]{2,1,0:T(8,128)(2,1)S(1)}, u32[]{:S(2)}) copy-start(bf16[16,32,896]{2,1,0:T(8,128)(2,1)S(1)} %constant_dynamic-update-slice_fusion.own_ref.fa_ref) | copy-start | bytes 2752516
  30.3 2.5 %collective-permute-start.6 = (bf16[16,32,896]{2,1,0:T(8,128)(2,1)S(1)}, bf16[16,32,896]{2,1,0:T(8,128)(2,1)S(1)}, u32[]{:S(2)}, u32[]{:S(2)}) collective-permute-start(bf16[16,32,896]{2,1,0:T(8,128)(2,1)S(1)} %constant_dynamic-update-slice_fusion.own_ref.fa_ref), channel_id=1, source_target_pairs={{0,1},{1,0},{2,3},{3,2},{4,5},{5,4},{6,7},{7,6},{8,9},{9,8},{10,11... | collective-permute-start | bytes 2752520 | tf_op jit(solution)/shard_map/ppermute | solution.py:822
  30.4 14.1 %collective-permute-start.7 = (bf16[4,32,2304]{2,1,0:T(8,128)(2,1)S(1)}, bf16[4,32,2304]{2,1,0:T(8,128)(2,1)S(1)}, u32[]{:S(2)}, u32[]{:S(2)}) collective-permute-start(bf16[4,32,2304]{2,1,0:T(8,128)(2,1)S(1)} %pad_maximum_fusion.1), channel_id=1, source_target_pairs={{0,2},{1,5},{2,0},{3,7},{4,6},{5,1},{6,4},{7,3},{8,10},{9,13},{10,... | collective-permute-start | bytes 1769480 | tf_op jit(solution)/shard_map/ppermute | solution.py:818
  32.9 0.9 copy-start.9
  44.6 12.4 %copy-start.2 = (bf16[8,32,2304]{2,1,0:T(8,128)(2,1)}, bf16[8,32,2304]{2,1,0:T(8,128)(2,1)S(1)}, u32[]{:S(2)}) copy-start(bf16[8,32,2304]{2,1,0:T(8,128)(2,1)S(1)} %pad_maximum_fusion.refs_0_) | copy-start | bytes 3538948
  44.6 16.3 %collective-permute-start.8 = (bf16[8,32,2304]{2,1,0:T(8,128)(2,1)S(1)}, bf16[8,32,2304]{2,1,0:T(8,128)(2,1)S(1)}, u32[]{:S(2)}, u32[]{:S(2)}) collective-permute-start(bf16[8,32,2304]{2,1,0:T(8,128)(2,1)S(1)} %pad_maximum_fusion.refs_0_), channel_id=1, source_target_pairs={{0,4},{1,3},{2,6},{3,1},{4,0},{5,7},{6,2},{7,5},{8,12},{9,11},{10,... | collective-permute-start | bytes 3538952 | tf_op jit(solution)/shard_map/ppermute | solution.py:818
  46.2 16.3 %collective-permute-start.9 = (bf16[8,32,2304]{2,1,0:T(8,128)(2,1)S(1)}, bf16[8,32,2304]{2,1,0:T(8,128)(2,1)S(1)}, u32[]{:S(2)}, u32[]{:S(2)}) collective-permute-start(bf16[8,32,2304]{2,1,0:T(8,128)(2,1)S(1)} %pad_maximum_fusion.refs_0_), channel_id=1, source_target_pairs={{0,1},{1,0},{2,3},{3,2},{4,5},{5,4},{6,7},{7,6},{8,9},{9,8},{10,11... | collective-permute-start | bytes 3538952 | tf_op jit(solution)/shard_map/ppermute | solution.py:822
  60.9 5.1 %copy-start.6 = (bf16[8,32,2304]{2,1,0:T(8,128)(2,1)}, bf16[8,32,2304]{2,1,0:T(8,128)(2,1)S(1)}, u32[]{:S(2)}) copy-start(bf16[8,32,2304]{2,1,0:T(8,128)(2,1)S(1)} %collective-permute-done.8.refs_1_) | copy-start | bytes 3538948
  60.9 4.0 %collective-permute-start.10 = (bf16[8,32,2304]{2,1,0:T(8,128)(2,1)S(1)}, bf16[8,32,2304]{2,1,0:T(8,128)(2,1)S(1)}, u32[]{:S(2)}, u32[]{:S(2)}) collective-permute-start(bf16[8,32,2304]{2,1,0:T(8,128)(2,1)S(1)} %collective-permute-done.8.refs_1_), channel_id=1, source_target_pairs={{0,1},{1,0},{2,3},{3,2},{4,5},{5,4},{6,7},{7,6},{8,9},{9,8},{10,11... | collective-permute-start | bytes 3538952 | tf_op jit(solution)/shard_map/ppermute | solution.py:822
  62.5 3.5 %copy-start.7 = (bf16[8,32,2304]{2,1,0:T(8,128)(2,1)}, bf16[8,32,2304]{2,1,0:T(8,128)(2,1)S(1)}, u32[]{:S(2)}) copy-start(bf16[8,32,2304]{2,1,0:T(8,128)(2,1)S(1)} %collective-permute-done.9.refs_2_) | copy-start | bytes 3538948
  64.9 1.0 copy-start.8
  147.6 6.1 %collective-permute-start.12 = (bf16[8,32,2304]{2,1,0:T(8,128)(2,1)}, bf16[8,32,2304]{2,1,0:T(8,128)(2,1)S(1)}, u32[]{:S(2)}, u32[]{:S(2)}) collective-permute-start(bf16[8,32,2304]{2,1,0:T(8,128)(2,1)} %get-tuple-element.76), channel_id=1, source_target_pairs={{0,1},{1,0},{2,3},{3,2},{4,5},{5,4},{6,7},{7,6},{8,9},{9,8},{10,11... | collective-permute-start | bytes 3538952 | tf_op jit(solution)/shard_map/ppermute | solution.py:822
  151.0 22.4 %collective-permute-start.11 = (bf16[8,32,2304]{2,1,0:T(8,128)(2,1)}, bf16[8,32,2304]{2,1,0:T(8,128)(2,1)S(1)}, u32[]{:S(2)}, u32[]{:S(2)}) collective-permute-start(bf16[8,32,2304]{2,1,0:T(8,128)(2,1)} %get-tuple-element.74), channel_id=1, source_target_pairs={{0,1},{1,0},{2,3},{3,2},{4,5},{5,4},{6,7},{7,6},{8,9},{9,8},{10,11... | collective-permute-start | bytes 3538952 | tf_op jit(solution)/shard_map/ppermute | solution.py:822
  155.3 18.1 %collective-permute-start.13 = (bf16[8,32,2304]{2,1,0:T(8,128)(2,1)S(1)}, bf16[8,32,2304]{2,1,0:T(8,128)(2,1)}, u32[]{:S(2)}, u32[]{:S(2)}) collective-permute-start(bf16[8,32,2304]{2,1,0:T(8,128)(2,1)S(1)} %add_convert_fusion.1), channel_id=1, source_target_pairs={{0,4},{1,3},{2,6},{3,1},{4,0},{5,7},{6,2},{7,5},{8,12},{9,11},{10,... | collective-permute-start | bytes 3538952 | tf_op jit(solution)/shard_map/ppermute | solution.py:818
  157.0 16.4 %copy-start.3 = (bf16[8,32,2304]{2,1,0:T(8,128)(2,1)S(1)}, bf16[8,32,2304]{2,1,0:T(8,128)(2,1)}, u32[]{:S(2)}) copy-start(bf16[8,32,2304]{2,1,0:T(8,128)(2,1)} %get-tuple-element.73) | copy-start | bytes 3538948
  175.2 18.1 %collective-permute-start.14 = (bf16[4,32,2304]{2,1,0:T(8,128)(2,1)S(1)}, bf16[4,32,2304]{2,1,0:T(8,128)(2,1)S(1)}, u32[]{:S(2)}, u32[]{:S(2)}) collective-permute-start(bf16[4,32,2304]{2,1,0:T(8,128)(2,1)S(1)} %slice.78), channel_id=1, source_target_pairs={{0,2},{1,5},{2,0},{3,7},{4,6},{5,1},{6,4},{7,3},{8,10},{9,13},{10,... | collective-permute-start | bytes 1769480 | tf_op jit(solution)/shard_map/ppermute | solution.py:818
  193.2 2.8 %copy-start.4 = (bf16[16,32,896]{2,1,0:T(8,128)(2,1)S(1)}, bf16[16,32,896]{2,1,0:T(8,128)(2,1)}, u32[]{:S(2)}) copy-start(bf16[16,32,896]{2,1,0:T(8,128)(2,1)} %get-tuple-element.90) | copy-start | bytes 2752516
  193.3 2.7 %collective-permute-start.15 = (bf16[16,32,896]{2,1,0:T(8,128)(2,1)}, bf16[16,32,896]{2,1,0:T(8,128)(2,1)S(1)}, u32[]{:S(2)}, u32[]{:S(2)}) collective-permute-start(bf16[16,32,896]{2,1,0:T(8,128)(2,1)} %get-tuple-element.91), channel_id=1, source_target_pairs={{0,1},{1,0},{2,3},{3,2},{4,5},{5,4},{6,7},{7,6},{8,9},{9,8},{10,11... | collective-permute-start | bytes 2752520 | tf_op jit(solution)/shard_map/ppermute | solution.py:822
  193.5 9.5 %collective-permute-start.20 = (bf16[2,32,2304]{2,1,0:T(8,128)(2,1)S(1)}, bf16[2,32,2304]{2,1,0:T(8,128)(2,1)S(1)}, u32[]{:S(2)}, u32[]{:S(2)}) collective-permute-start(bf16[2,32,2304]{2,1,0:T(8,128)(2,1)S(1)} %slice.118), channel_id=1, source_target_pairs={{0,8},{1,9},{2,10},{3,11},{4,12},{5,13},{6,14},{7,15},{8,0},{9,1},... | collective-permute-start | bytes 884744 | tf_op jit(solution)/shard_map/ppermute | solution.py:818
  196.3 8.5 %collective-permute-start.16 = (bf16[8,32,896]{2,1,0:T(8,128)(2,1)S(1)}, bf16[8,32,896]{2,1,0:T(8,128)(2,1)S(1)}, u32[]{:S(2)}, u32[]{:S(2)}) collective-permute-start(bf16[8,32,896]{2,1,0:T(8,128)(2,1)S(1)} %slice.105), channel_id=1, source_target_pairs={{0,4},{1,3},{2,6},{3,1},{4,0},{5,7},{6,2},{7,5},{8,12},{9,11},{10,... | collective-permute-start | bytes 1376264 | tf_op jit(solution)/shard_map/ppermute | solution.py:818
  203.1 8.9 %collective-permute-start.21 = (bf16[1,32,2304]{2,1,0:T(8,128)(2,1)S(1)}, bf16[1,32,2304]{2,1,0:T(8,128)(2,1)S(1)}, u32[]{:S(2)}, u32[]{:S(2)}) collective-permute-start(bf16[1,32,2304]{2,1,0:T(8,128)(2,1)S(1)} %slice.120), channel_id=1, source_target_pairs={{0,16},{1,17},{2,18},{3,19},{4,20},{5,21},{6,22},{7,23},{8,24},{9,... | collective-permute-start | bytes 442376 | tf_op jit(solution)/shard_map/ppermute | solution.py:818
  205.0 7.0 %collective-permute-start.17 = (bf16[4,32,896]{2,1,0:T(8,128)(2,1)S(1)}, bf16[4,32,896]{2,1,0:T(8,128)(2,1)S(1)}, u32[]{:S(2)}, u32[]{:S(2)}) collective-permute-start(bf16[4,32,896]{2,1,0:T(8,128)(2,1)S(1)} %slice.107), channel_id=1, source_target_pairs={{0,2},{1,5},{2,0},{3,7},{4,6},{5,1},{6,4},{7,3},{8,10},{9,13},{10,... | collective-permute-start | bytes 688136 | tf_op jit(solution)/shard_map/ppermute | solution.py:818
  212.0 12.9 %copy-start.1 = (s32[2,8]{1,0:T(2,128)S(1)}, s32[2,8]{1,0:T(2,128)}, u32[]{:S(2)}) copy-start(s32[2,8]{1,0:T(2,128)} %param.16) | copy-start | bytes 196
  212.1 5.1 %collective-permute-start.18 = (bf16[2,32,896]{2,1,0:T(8,128)(2,1)S(1)}, bf16[2,32,896]{2,1,0:T(8,128)(2,1)S(1)}, u32[]{:S(2)}, u32[]{:S(2)}) collective-permute-start(bf16[2,32,896]{2,1,0:T(8,128)(2,1)S(1)} %slice.109), channel_id=1, source_target_pairs={{0,8},{1,9},{2,10},{3,11},{4,12},{5,13},{6,14},{7,15},{8,0},{9,1},... | collective-permute-start | bytes 344072 | tf_op jit(solution)/shard_map/ppermute | solution.py:818
  217.3 5.5 %collective-permute-start.19 = (bf16[1,32,896]{2,1,0:T(8,128)(2,1)S(1)}, bf16[1,32,896]{2,1,0:T(8,128)(2,1)S(1)}, u32[]{:S(2)}, u32[]{:S(2)}) collective-permute-start(bf16[1,32,896]{2,1,0:T(8,128)(2,1)S(1)} %slice.111), channel_id=1, source_target_pairs={{0,16},{1,17},{2,18},{3,19},{4,20},{5,21},{6,22},{7,23},{8,24},{9,... | collective-permute-start | bytes 172040 | tf_op jit(solution)/shard_map/ppermute | solution.py:818
